TPU v7x, 512 devices: a whole 4x8x8 slice. The times are simulated.
512 devices in a mesh: tower: 2 (over x_lo), blk: 128 (over z, x_hi, y), mp: 2 (over core).
Axes of the slice: x: 4 (x_hi: 2, x_lo: 2; x = x_hi * 2 + x_lo), y: 8, z: 8, core: 2. Of those that a mesh axis runs over, the one named last changes fastest.
Arguments:
- tower_inputs: bfloat16 [2, 2048, 2, 18432], P('tower', 'blk', 'mp'), may hold values from -10 to 10
- image_proj: bfloat16 [1536, 1536], P('mp'), may hold values from -4 to 4
- text_proj: bfloat16 [1152, 1536], P('mp'), may hold values from -4 to 4
- text_lengths: int32 [2048], P('blk'), may hold values from 1 to 32
- partner: int32 [2048], P('blk'), may hold values from 0 to 2047, as said below
- log_scale: float32 [1], replicated, may hold values from 2 to 2.6
- bias: float32 [1], replicated, may hold values from -2.5 to -1
Outputs:
- emb_grads: float32 [2, 2048, 1536], P('tower', ('blk', 'mp'))
- loss_sums: float32 [2, 2048], P('tower', ('blk', 'mp'))
Inputs may be any that keep to these rules, and one draw needn't show every extreme that they name: `text_lengths`: the number of real tokens of each text; slots past it are padding. Image p is paired with text partner[p]; every text is paired with exactly one image.
All inputs are finite; a program needn't handle non-finite values.
Results may differ from a plain program's by a relative error of at most 0.0015.
Values may be sent and summed in bfloat16 or wider, within the bound.
No kernel may reach another device: no remote copies, remote signals or barrier semaphores. Data moves between devices by JAX's collectives and lax.ppermute only.
A program may use at most 64 MiB of HBM per device.

v0:
```python
import jax
import jax.numpy as jnp
from jax import lax
from jax.sharding import PartitionSpec as P

EPS = 1e-06


def from_partner(value, axis, stride):
    mask = 2**stride
    pairs = [(source, source ^ mask) for source in range(lax.axis_size(axis))]
    return lax.ppermute(value, axis, pairs)


def image_partial(slices, image_proj):
    row_count = slices.shape[0]
    feature_width = image_proj.shape[0]
    patch_count = slices.shape[1] // feature_width
    summed = jnp.sum(
        slices.reshape(row_count, patch_count, feature_width), axis=1, dtype=jnp.float32
    )
    pooled = (summed / patch_count).astype(jnp.bfloat16)
    return jnp.dot(pooled, image_proj, preferred_element_type=jnp.float32)


def text_partial(slices, text_lengths, text_proj):
    row_count = slices.shape[0]
    feature_width = text_proj.shape[0]
    slot_count = slices.shape[1] // feature_width
    keep_mask = (
        lax.broadcasted_iota(jnp.int32, (row_count, slot_count), 1) < text_lengths[:, None]
    ).astype(jnp.bfloat16)
    summed = jnp.einsum(
        "rlf,rl->rf",
        slices.reshape(row_count, slot_count, feature_width),
        keep_mask,
        preferred_element_type=jnp.float32,
    )
    pooled = (summed / text_lengths.astype(jnp.float32)[:, None]).astype(jnp.bfloat16)
    return jnp.dot(pooled, text_proj, preferred_element_type=jnp.float32)


def make_score(rows_low, rows_key, temper, offset):

    def score(carry, piece, start):
        piece_low, piece_key = piece
        logits = (
            temper
            * lax.dot_general(
                rows_low, piece_low, (((1,), (1,)), ((), ())), preferred_element_type=jnp.float32
            )
            + offset
        )
        paired = rows_key[:, None] == piece_key[None, :]
        losses = jax.nn.softplus(jnp.where(paired, -logits, logits))
        weights = (jax.nn.sigmoid(logits) - paired.astype(jnp.float32)).astype(jnp.bfloat16)
        grad_sum = temper * jnp.dot(weights, piece_low, preferred_element_type=jnp.float32)
        return (grad_sum, jnp.sum(losses, axis=1))

    return score


def fresh_carry(rows_low):
    return (jnp.zeros(rows_low.shape, jnp.float32), jnp.zeros((rows_low.shape[0],), jnp.float32))


def shards(tower_inputs, image_proj, text_proj, text_lengths, partner, log_scale, bias):
    slices = tower_inputs[0, :, 0, :]
    row_count = slices.shape[0]
    tower_index = lax.axis_index("tower")

    def image_branch():
        return image_partial(slices, image_proj)

    def text_branch():
        return text_partial(slices, text_lengths, text_proj)

    partial_emb = lax.cond(tower_index == 0, image_branch, text_branch)
    embedding = lax.psum(partial_emb, "mp")
    inverse = lax.rsqrt(jnp.sum(embedding * embedding, axis=1, keepdims=True) + EPS)
    unit = embedding * inverse
    unit_low = unit.astype(jnp.bfloat16)
    own_index = lax.axis_index("blk") * row_count + lax.iota(jnp.int32, row_count)
    match_key = jnp.where(tower_index == 0, partner, own_index)
    share = row_count // lax.axis_size("mp")
    first = lax.axis_index("mp") * share
    temper = jnp.exp(log_scale[0])
    offset = bias[0]
    own_low = lax.dynamic_slice_in_dim(unit_low, first, share, 0)
    own_key = lax.dynamic_slice_in_dim(match_key, first, share, 0)
    send_low, send_key = (unit_low, match_key)
    other_low, other_key = from_partner((send_low, send_key), "tower", 0)
    score = make_score(own_low, own_key, temper, offset)
    grad_sum, loss_sum = score(
        fresh_carry(own_low),
        (
            lax.all_gather(other_low, "blk", axis=0, tiled=True),
            lax.all_gather(other_key, "blk", axis=0, tiled=True),
        ),
        jnp.int32(0),
    )
    unit_share = lax.dynamic_slice_in_dim(unit, first, share, 0)
    inverse_share = lax.dynamic_slice_in_dim(inverse, first, share, 0)
    along = jnp.sum(unit_share * grad_sum, axis=1, keepdims=True)
    gradient = inverse_share * (grad_sum - unit_share * along)
    return (gradient[None], loss_sum[None])


def solution(mesh):
    placed = (
        P("tower", "blk", "mp", None),
        P("mp", None),
        P("mp", None),
        P("blk"),
        P("blk"),
        P(),
        P(),
    )
    return jax.shard_map(
        shards,
        mesh=mesh,
        in_specs=placed,
        out_specs=(P("tower", ("blk", "mp"), None), P("tower", ("blk", "mp"))),
        check_vma=False,
    )
```

profile of v0, /device:TPU:1, one launch (start us, length us, event | category | flops | bytes accessed | tf_op | source)
XLA Modules:
  0.0 221.5 jit_solution(8096204702785022471)
XLA Ops:
  7.2 0.0 all-reduce.3.cloned.1.call-start
  7.2 0.0 copy-start.4
  7.2 2.3 %conditional.1 = (f32[16,1536]{1,0:T(8,128)S(1)}) conditional(s32[]{:T(128)} %convert_element_type.32, (s32[16]{0:T(128)}, bf16[1,16,1,18432]{3,1,2,0:T(8,128)(2,1)}, bf16[576,1536]{1,0:T(8,128)(2,1)}) %tuple.14, (bf16[1,16,1,18432]{3,1,2,0:T(8,128)(2,1)}, bf16[768,1536]{1,0:T(8,128)(2,1)}) %tuple.15), branch_computations={%region_0.0_spmd, %region_1.0_spmd} | conditional | flops 38055936 | bytes 14942244 | solution.py:78
  7.2 0.0 copy-start.1
  7.3 1.3 copy.17
  8.6 0.1 bitcast_reduce_fusion
  8.7 0.4 copy-done.1
  9.1 0.4 fusion.7
  9.5 0.0 copy-start.2
  9.5 0.6 copy-done.2
  10.1 0.0 all-reduce.3.cloned.1.call-update
  10.2 0.0 all-gather.2.cloned.1.call-start
  10.2 44.1 %all-reduce.3.cloned.1.call-done = f32[16,1536]{1,0:T(8,128)} async-done(((f32[16,1536]{1,0:T(8,128)}), f32[16,1536]{1,0:T(8,128)}) %all-reduce.3.cloned.1.call-update) | async-done | bytes 98320 | tf_op jit(solution)/shard_map/psum | solution.py:79
  54.3 1.0 multiply_reduce_fusion
  55.3 1.0 fusion.23
  56.3 2.1 collective-permute-start
  58.4 2.7 %collective-permute-done = bf16[16,1536]{1,0:T(8,128)(2,1)S(1)} collective-permute-done((bf16[16,1536]{1,0:T(8,128)(2,1)S(1)}, bf16[16,1536]{1,0:T(8,128)(2,1)S(1)}, u32[]{:S(2)}, u32[]{:S(2)}) %collective-permute-start) | collective-permute-done | bytes 49184 | tf_op jit(solution)/shard_map/ppermute | solution.py:12
  61.1 0.6 copy-done.3
  61.7 0.0 all-gather.2.cloned.1.call-update
  61.8 0.0 copy-done.4
  61.8 2.1 collective-permute-start.1
  65.2 0.1 dynamic_slice.11
  65.3 1.3 dynamic-slice.4
  67.2 0.0 collective-permute-done.1
  67.3 0.3 dynamic-update-slice
  67.5 25.6 %all-reduce = s32[2048]{0:T(1024)S(1)} all-reduce(s32[2048]{0:T(1024)S(1)} %dynamic-update-slice), channel_id=1, replica_groups=mesh['tower'=2,'blk'=128,'mp'=2] {'blk'}, use_global_device_ids=true, to_apply=%add | all-reduce | flops 2048 | bytes 16384
  93.2 0.1 dynamic-slice.3
  93.2 114.4 %all-gather.2.cloned.1.call-done = bf16[2048,1536]{1,0:T(8,128)(2,1)} async-done(((bf16[16,1536]{1,0:T(8,128)(2,1)}), bf16[2048,1536]{1,0:T(8,128)(2,1)}) %all-gather.2.cloned.1.call-update) | async-done | bytes 6291472 | tf_op jit(solution)/shard_map/all_gather | solution.py:97
  207.6 5.3 %fusion.15 = (f32[8]{0:T(128)}, f32[8,2048]{1,0:T(8,128)S(1)}) fusion(s32[2048]{0:T(1024)S(1)} %all-reduce, s32[8]{0:T(128)S(1)} %dynamic_slice.11, f32[]{:T(128)} %bitcast.29, bf16[2048,1536]{1,0:T(8,128)(2,1)} %all-gather.2.cloned.1.call-done, bf16[16,1536]{1,0:T(8,128)(2,1)S(1)} %get-tuple-element.33, s32[]{:T(128)S(6)} %select_n.22, f32[]{:T(128)} %bitcast.2), kind=kOutput, calls=%fused_computation.25 | convolution fusion | flops 50528248 | bytes 6390316 | tf_op jit(solution)/shard_map/dot_general | solution.py:49
  212.9 0.0 copy-done
  212.9 1.1 multiply_reduce_fusion.1
  214.0 0.7 multiply_bitcast_fusion
  (5 shorter events, 0.0 us)
Async XLA Ops:
  7.2 47.1 %all-reduce.3.cloned.1.call-start = ((), (), s32[]{:S(2)}) async-start(), calls=%async_computation | async-start | bytes 196608 | tf_op jit(solution)/shard_map/psum | solution.py:79
  7.2 54.6 %copy-start.4 = (s32[16]{0:T(128)S(1)}, s32[16]{0:T(128)}, u32[]{:S(2)}) copy-start(s32[16]{0:T(128)} %param.13) | copy-start | bytes 196
  7.2 1.8 copy-start.1
  9.5 0.6 copy-start.2
  10.2 197.4 %all-gather.2.cloned.1.call-start = ((), (), s32[]{:S(2)}) async-start(), calls=%async_computation.1 | async-start | bytes 6340608 | tf_op jit(solution)/shard_map/all_gather | solution.py:97
  56.3 4.8 %collective-permute-start = (bf16[16,1536]{1,0:T(8,128)(2,1)S(1)}, bf16[16,1536]{1,0:T(8,128)(2,1)S(1)}, u32[]{:S(2)}, u32[]{:S(2)}) collective-permute-start(bf16[16,1536]{1,0:T(8,128)(2,1)S(1)} %get-tuple-element.33), channel_id=1, source_target_pairs={{0,256},{256,0},{1,257},{257,1},{2,258},{258,2},{3,259},{259,3},{4... | collective-permute-start | bytes 147464 | tf_op jit(solution)/shard_map/ppermute | solution.py:12
  61.1 0.6 copy-start.3
  61.8 5.4 %collective-permute-start.1 = (s32[16]{0:T(128)S(1)}, s32[16]{0:T(128)S(1)}, u32[]{:S(2)}, u32[]{:S(2)}) collective-permute-start(s32[16]{0:T(128)S(1)} %broadcast_select_fusion), channel_id=1, source_target_pairs={{0,256},{256,0},{1,257},{257,1},{2,258},{258,2},{3,259},{259,3},{4... | collective-permute-start | bytes 200 | tf_op jit(solution)/shard_map/ppermute | solution.py:12
  207.6 5.3 %copy-start = (bf16[2048,1536]{1,0:T(8,128)(2,1)S(1)}, bf16[2048,1536]{1,0:T(8,128)(2,1)}, u32[]{:S(2)}) copy-start(bf16[2048,1536]{1,0:T(8,128)(2,1)} %all-gather.2.cloned.1.call-done) | copy-start | bytes 18874372
Sparse Core Ops, SparseCore 0:
  10.8 43.3 all-reduce.2
  61.9 145.6 all-gather.1
where the time goes:
time: 224 us; the launch traced here: 222 us
  waiting for transfers between devices  161 us (72%)
  blocking collectives  25.6 us (11%)
  between operations  16.1 us (7%)
  matrix products  6.79 us (3%)
  local copies, waits for them, and re-layouts  4.67 us (2%)
  starting transfers between devices  4.28 us (2%)
  other arithmetic  2.85 us (1%)
    all_gather x1, waiting for transfers between devices, shards(): lax.all_gather(other_low, 'blk', axis=0, tiled=True)  114 us
    psum x1, waiting for transfers between devices, shards(): embedding = lax.psum(partial_emb, 'mp')  44.1 us
    unnamed x1, blocking collectives  25.6 us
    dot_general x1, matrix products, score(): lax.dot_general(rows_low, piece_low, (((1,), (1,)), ((), ())), preferred_...  5.31 us
  transfers between devices with their start and end apart: 4, of which 3 were waited for; matrix products, arithmetic and copies ran while one was open for 1% of the time, Pallas kernels for 0%

commit v1 on v0

v1 whole, which is shorter than its diff:
```python
import jax
import jax.numpy as jnp
from jax import lax
from jax.experimental import pallas as pl
from jax.experimental.pallas import tpu as pltpu
from jax.sharding import Mesh
from jax.sharding import PartitionSpec as P

EPS = 1e-06
PIECE = 256
LANES = 128
BASE = 16


def project(pooled, weights, copies, core_ref, keep_ref, send_ref):
    total = None
    for copy, first, last in copies:
        copy.wait()
        piece = jnp.dot(
            pooled[:, first:last], weights[first:last, :], preferred_element_type=jnp.float32
        )
        total = piece if total is None else total + piece
    share = keep_ref.shape[0]
    upper, lower = total[:share], total[share:]
    first_core = core_ref[0] == 0
    keep_ref[...] = jnp.where(first_core, upper, lower)
    send_ref[...] = jnp.where(first_core, lower, upper)


def fetch(slices_hbm, weights_hbm, slices, weights, sems):
    depth = weights_hbm.shape[0]
    first_copy = pltpu.make_async_copy(slices_hbm, slices, sems.at[0])
    first_copy.start()
    copies = []
    for place, first in enumerate(range(0, depth, PIECE)):
        last = min(first + PIECE, depth)
        copy = pltpu.make_async_copy(
            weights_hbm.at[first:last], weights.at[first:last], sems.at[1 + place]
        )
        copy.start()
        copies.append((copy, first, min(first + PIECE, weights.shape[0])))
    return first_copy, copies


def image_kernel(core_ref, slices_hbm, weights_hbm, keep_ref, send_ref, slices, weights, sems):
    first_copy, copies = fetch(slices_hbm, weights_hbm, slices, weights, sems)
    width = weights_hbm.shape[0]
    patch_count = slices.shape[1] // width
    first_copy.wait()
    summed = slices[:, :width].astype(jnp.float32)
    for patch in range(1, patch_count):
        summed += slices[:, patch * width : (patch + 1) * width].astype(jnp.float32)
    pooled = (summed / patch_count).astype(jnp.bfloat16)
    project(pooled, weights, copies, core_ref, keep_ref, send_ref)


def text_kernel(
    core_ref, lengths_ref, slices_hbm, weights_hbm, keep_ref, send_ref, slices, weights, sems
):
    first_copy, copies = fetch(slices_hbm, weights_hbm, slices, weights, sems)
    width = weights_hbm.shape[0]
    row_count = slices.shape[0]
    slot_count = slices.shape[1] // width
    padded = weights.shape[0]
    if padded > width:
        weights[width:, :] = jnp.zeros((padded - width, weights.shape[1]), jnp.bfloat16)
    shape = (row_count, 2 * width)
    row = lax.broadcasted_iota(jnp.int32, shape, 0)
    lengths = jnp.zeros(shape, jnp.int32)
    for index in range(row_count):
        lengths = jnp.where(row == index, lengths_ref[index], lengths)
    second = (lax.broadcasted_iota(jnp.int32, shape, 1) >= width).astype(jnp.int32)
    left = lengths - second
    first_copy.wait()
    summed = jnp.zeros(shape, jnp.float32)
    for slot in range(0, slot_count, 2):
        piece = slices[:, slot * width : (slot + 2) * width].astype(jnp.float32)
        summed += jnp.where(slot < left, piece, 0.0)
    summed = summed + pltpu.roll(summed, width, 1)
    pooled = (summed / lengths.astype(jnp.float32)).astype(jnp.bfloat16)
    project(pooled, weights, copies, core_ref, keep_ref, send_ref)


def pooled_partial(kernel, scalars, slices, weights):
    row_count = slices.shape[0]
    depth, width = weights.shape
    padded = -(-depth // LANES) * LANES
    pieces = -(-depth // PIECE)
    any_space = pl.BlockSpec(memory_space=pl.ANY)
    half = jax.ShapeDtypeStruct((row_count // 2, width), jnp.float32)
    return pl.pallas_call(
        kernel,
        out_shape=(half, half),
        in_specs=[pl.BlockSpec(memory_space=pltpu.SMEM)] * len(scalars) + [any_space] * 2,
        out_specs=(pl.BlockSpec(memory_space=pltpu.VMEM),) * 2,
        scratch_shapes=[
            pltpu.VMEM(slices.shape, jnp.bfloat16),
            pltpu.VMEM((padded, width), jnp.bfloat16),
            pltpu.SemaphoreType.DMA((1 + pieces,)),
        ],
        compiler_params=pltpu.CompilerParams(vmem_limit_bytes=32 * 2**20),
    )(*scalars, slices, weights)


def swap_gather(block, axis, after):
    members = lax.axis_size(axis)
    half = members // 2
    size = block.shape[0]

    def brought(value, across):
        return lax.ppermute(value, axis, [(index, index ^ across) for index in range(members)])

    pair = jnp.concatenate([block, brought(block, half)], axis=0)
    pair, _ = lax.optimization_barrier((pair, after))
    held = jnp.concatenate([pair] + [brought(pair, across) for across in range(1, half)], axis=0)
    place = lax.broadcasted_iota(jnp.int32, (members * size, members * size), 0)
    slot = lax.broadcasted_iota(jnp.int32, (members * size, members * size), 1)
    number = slot // size
    came_from = lax.axis_index(axis) ^ (number // 2 + (number % 2) * half)
    moves = (place // size == came_from) & (place % size == slot % size)
    ordered = jnp.dot(moves.astype(held.dtype), held, preferred_element_type=jnp.float32)
    return ordered.astype(held.dtype)


def shards(tower_inputs, image_proj, text_proj, text_lengths, partner, log_scale, bias):
    slices = tower_inputs[0, :, 0, :]
    row_count = slices.shape[0]
    tower = lax.axis_index("tower")
    core = lax.axis_index("mp")
    n_mp = lax.axis_size("mp")
    n_y = lax.axis_size("y")
    n_x = lax.axis_size("x")
    n_z = lax.axis_size("z")
    share = row_count // n_mp
    width = image_proj.shape[1]

    core_index = core.astype(jnp.int32).reshape(1)
    kept, sent = lax.cond(
        tower == 0,
        lambda: pooled_partial(image_kernel, (core_index,), slices, image_proj),
        lambda: pooled_partial(text_kernel, (core_index, text_lengths), slices, text_proj),
    )
    embedding = kept + lax.ppermute(sent, "mp", [(0, 1), (1, 0)])
    inverse = lax.rsqrt(jnp.sum(embedding * embedding, axis=1, keepdims=True) + EPS)
    unit = embedding * inverse
    unit_low = unit.astype(jnp.bfloat16)

    key = lax.dynamic_slice_in_dim(partner, core * share, share, 0)
    key_high = (key // BASE).astype(jnp.bfloat16)[:, None]
    key_low = (key % BASE).astype(jnp.bfloat16)[:, None]
    column = lax.broadcasted_iota(jnp.int32, (share, LANES), 1)
    key_block = jnp.where(column == 0, key_high, jnp.where(column == 1, key_low, 0))
    own = jnp.concatenate([unit_low, key_block], axis=1)

    near = lax.ppermute(own, "tower", [(0, 1), (1, 0)])
    across = lax.ppermute(own, ("tower", "x"), [(0, 3), (3, 0), (1, 2), (2, 1)])
    other = jnp.concatenate([near, across], axis=0)
    copies = jnp.broadcast_to(other[None], (n_y,) + other.shape)
    own_all = swap_gather(own, "z", other[:1, :LANES])
    other_mine = lax.all_to_all(copies, "y", 0, 0, tiled=True)
    other_mine = other_mine.reshape(n_y * n_x * share, width + LANES)
    other_theirs = lax.ppermute(other_mine, "mp", [(0, 1), (1, 0)])

    def sent_key(gathered):
        pair = gathered[:, width : width + 2].astype(jnp.int32)
        return pair[:, 0] * BASE + pair[:, 1]

    z = lax.axis_index("z")
    y = lax.axis_index("y")
    x = lax.axis_index("x")

    def pair_at(z_at, x_at, y_at):
        return ((z_at * n_x + x_at) * n_y + y_at) * row_count

    own_slot = lax.iota(jnp.int32, n_z * share)
    own_place = pair_at(own_slot // share, x, y) + core * share + own_slot % share
    other_slot = lax.iota(jnp.int32, n_y * n_x * share)
    other_x = x ^ (other_slot // share % n_x)
    other_base = pair_at(z, other_x, other_slot // (n_x * share)) + other_slot % share
    own_key = jnp.where(tower == 0, sent_key(own_all), own_place)
    temper = jnp.exp(log_scale[0])
    own_low = own_all[:, :width]

    def score(others, other_core):
        other_place = other_base + other_core * share
        other_key = jnp.where(tower == 0, other_place, sent_key(others))
        other_low = others[:, :width]
        logits = (
            temper
            * lax.dot_general(
                own_low, other_low, (((1,), (1,)), ((), ())), preferred_element_type=jnp.float32
            )
            + bias[0]
        )
        paired = own_key[:, None] == other_key[None, :]
        losses = jax.nn.softplus(jnp.where(paired, -logits, logits))
        weights = (jax.nn.sigmoid(logits) - paired.astype(jnp.float32)).astype(jnp.bfloat16)
        grad = jnp.dot(weights, other_low, preferred_element_type=jnp.float32)
        return grad, jnp.sum(losses, axis=1, keepdims=True)

    grad_mine, loss_mine = score(other_mine, core)
    grad_theirs, loss_theirs = score(other_theirs, 1 - core)
    grad_part = grad_mine + grad_theirs
    loss_part = loss_mine + loss_theirs

    loss_high = lax.reduce_precision(loss_part, 5, 10)
    loss_rest = loss_part - loss_high
    lane = lax.broadcasted_iota(jnp.int32, (n_z * share, LANES), 1)
    loss_block = jnp.where(lane == 0, loss_high, loss_rest).astype(jnp.float16)
    sums = jnp.concatenate([grad_part.astype(jnp.float16), loss_block], axis=1)
    sums = lax.all_to_all(sums.reshape(n_z, share, width + LANES), "z", 0, 0, tiled=True)
    total = jnp.sum(sums.astype(jnp.float32), axis=0)
    grad_sum = temper * total[:, :width]
    loss_sum = total[:, width] + total[:, width + 1]

    along = jnp.sum(unit * grad_sum, axis=1, keepdims=True)
    gradient = inverse * (grad_sum - unit * along)
    return (gradient[None], loss_sum[None])


def solution(mesh):
    n_tower, n_blk, n_mp = (mesh.shape[name] for name in ("tower", "blk", "mp"))
    n_z, n_x = 8, 2
    grid = Mesh(
        mesh.devices.reshape(n_tower, n_z, n_x, n_blk // (n_z * n_x), n_mp),
        ("tower", "z", "x", "y", "mp"),
    )
    blk = ("z", "x", "y")
    placed = (
        P("tower", blk, "mp", None),
        P("mp", None),
        P("mp", None),
        P(blk),
        P(blk),
        P(),
        P(),
    )
    return jax.shard_map(
        shards,
        mesh=grid,
        in_specs=placed,
        out_specs=(P("tower", blk + ("mp",), None), P("tower", blk + ("mp",))),
        check_vma=False,
    )
```

time: 224 us -> 69.8 us (0.31)
  waiting for transfers between devices: 161 us -> 4.37 us
  starting transfers between devices: 4.28 us -> 41 us
  between operations: 16.1 us -> 2.23 us
  blocking collectives: 25.6 us -> 13.8 us
  matrix products: 6.79 us -> 1.43 us
  local copies, waits for them, and re-layouts: 4.67 us -> 0.79 us
    all_gather x1 -> x0, waiting for transfers between devices: 114 us -> none  [shards(): lax.all_gather(other_low, 'blk', axis=0, tiled=True)]
    psum x1 -> x0, waiting for transfers between devices: 44.1 us -> none  [shards(): embedding = lax.psum(partial_emb, 'mp')]
    ppermute x2 -> x8, starting transfers between devices: 4.2 us -> 34.2 us  [the longest x4 17.6 us: brought(): lax.ppermute(value, axis, [(index, index ^ across) for index in range(mem...]
    unnamed x1 -> x0, blocking collectives: 25.6 us -> none
    all_to_all x0 -> x1, blocking collectives: none -> 13.8 us  [shards(): lax.all_to_all(sums.reshape(n_z, share, width + LANES), 'z', 0, 0, tiled=...]
    all_to_all x0 -> x1, starting transfers between devices: none -> 6.82 us  [shards(): other_mine = lax.all_to_all(copies, 'y', 0, 0, tiled=True)]
    dot_general x3 -> x5, matrix products: 6.79 us -> 1.43 us  [the longest x2 0.65 us: score(): lax.dot_general(own_low, other_low, (((1,), (1,)), ((), ())), preferred_e...]
    unnamed x11 -> x2, local copies, waits for them, and re-layouts: 2.82 us -> 0.01 us
  transfers between devices with their start and end apart: 4 -> 9, of which waited for: 3 -> 5; matrix products, arithmetic and copies ran while one was open for 1% -> 3% of each run, Pallas kernels for 0% -> 0%
where the time goes in v1:
time: 69.8 us; the launch traced here: 68.5 us
  starting transfers between devices  41 us (59%)
  blocking collectives  13.8 us (20%)
  waiting for transfers between devices  4.37 us (6%)
  other arithmetic  2.78 us (4%)
  between operations  2.23 us (3%)
  Pallas kernels  2.04 us (3%)
  matrix products  1.43 us (2%)
  local copies, waits for them, and re-layouts  0.79 us (1%)
    ppermute x4, starting transfers between devices, brought(): lax.ppermute(value, axis, [(index, index ^ across) for index in range(mem...  17.6 us
    all_to_all x1, blocking collectives, shards(): lax.all_to_all(sums.reshape(n_z, share, width + LANES), 'z', 0, 0, tiled=...  13.8 us
    ppermute x1, starting transfers between devices, shards(): embedding = kept + lax.ppermute(sent, 'mp', [(0, 1), (1, 0)])  8.79 us
    all_to_all x1, starting transfers between devices, shards(): other_mine = lax.all_to_all(copies, 'y', 0, 0, tiled=True)  6.82 us
    ppermute x1, starting transfers between devices, shards(): other_theirs = lax.ppermute(other_mine, 'mp', [(0, 1), (1, 0)])  4.01 us
    pallas_call x1, Pallas kernels, pooled_partial(): pl.pallas_call(kernel, out_shape=(half, half), in_specs=[pl.BlockSpec(mem...  2.04 us
    ppermute x1, starting transfers between devices, shards(): near = lax.ppermute(own, 'tower', [(0, 1), (1, 0)])  1.92 us
    all_to_all x1, waiting for transfers between devices, shards(): other_mine = lax.all_to_all(copies, 'y', 0, 0, tiled=True)  1.92 us
  transfers between devices with their start and end apart: 9, of which 5 were waited for; matrix products, arithmetic and copies ran while one was open for 3% of the time, Pallas kernels for 0%

profile of v1, /device:TPU:1, one launch (start us, length us, event | category | flops | bytes accessed | tf_op | source)
XLA Modules:
  0.0 68.5 jit_solution(9126764097811049959)
XLA Ops:
  0.6 2.1 %conditional.1 = ((f32[8,1536]{1,0:T(8,128)S(1)}, f32[8,1536]{1,0:T(8,128)S(1)})) conditional(s32[]{:T(128)} %convert_element_type.48, (s32[1]{0:T(128)}, s32[16]{0:T(128)}, bf16[16,18432]{1,0:T(8,128)(2,1)}, bf16[576,1536]{1,0:T(8,128)(2,1)}) %tuple.31, (s32[1]{0:T(128)}, bf16[16,18432]{1,0:T(8,128)(2,1)}, bf16[768,1536]{1,0:T(8,128)(2,1)}) %tuple.32), branch_computations={%region_0.0_spmd, %region_1.0_spmd} | conditional | bytes 8 | solution.py:138
  0.7 2.0 %branch_1_fun.1 = (f32[8,1536]{1,0:T(8,128)S(1)}, f32[8,1536]{1,0:T(8,128)S(1)}) custom-call(s32[1]{0:T(128)} %get-tuple-element.18.core_ref, bf16[16,18432]{1,0:T(8,128)(2,1)} %get-tuple-element.19.slices_hbm, bf16[768,1536]{1,0:T(8,128)(2,1)} %get-tuple-element.32.weights_hbm), custom_call_target="tpu_custom_call" | custom-call | tf_op jit(solution)/shard_map/cond/branch_1_fun/pallas_call | solution.py:91
  2.7 8.8 %collective-permute-start = (f32[8,1536]{1,0:T(8,128)S(1)}, f32[8,1536]{1,0:T(8,128)S(1)}, u32[]{:S(2)}, u32[]{:S(2)}) collective-permute-start(f32[8,1536]{1,0:T(8,128)S(1)} %get-tuple-element.26), channel_id=1, source_target_pairs={{0,1},{1,0},{2,3},{3,2},{4,5},{5,4},{6,7},{7,6},{8,9},{9,8},{10,11... | collective-permute-start | bytes 147464 | tf_op jit(solution)/shard_map/ppermute | solution.py:143
  11.5 0.1 fusion.92
  11.7 0.7 collective-permute-done
  12.4 0.1 multiply_reduce_fusion.1
  12.6 1.9 %collective-permute-start.6 = (bf16[8,1664]{1,0:T(8,128)(2,1)S(1)}, bf16[8,1664]{1,0:T(8,128)(2,1)S(1)}, u32[]{:S(2)}, u32[]{:S(2)}) collective-permute-start(bf16[8,1664]{1,0:T(8,128)(2,1)S(1)} %pad_maximum_fusion.2), channel_id=1, source_target_pairs={{0,272},{272,0},{16,256},{256,16},{1,273},{273,1},{17,257},{257,17... | collective-permute-start | bytes 79880 | tf_op jit(solution)/shard_map/ppermute | solution.py:156
  14.5 1.9 %collective-permute-start.5 = (bf16[8,1664]{1,0:T(8,128)(2,1)S(1)}, bf16[8,1664]{1,0:T(8,128)(2,1)S(1)}, u32[]{:S(2)}, u32[]{:S(2)}) collective-permute-start(bf16[8,1664]{1,0:T(8,128)(2,1)S(1)} %pad_maximum_fusion.2), channel_id=1, source_target_pairs={{0,256},{256,0},{1,257},{257,1},{2,258},{258,2},{3,259},{259,3},{4... | collective-permute-start | bytes 79880 | tf_op jit(solution)/shard_map/ppermute | solution.py:155
  16.5 8.3 %collective-permute-start.1 = (bf16[8,1664]{1,0:T(8,128)(2,1)S(1)}, bf16[8,1664]{1,0:T(8,128)(2,1)S(1)}, u32[]{:S(2)}, u32[]{:S(2)}) collective-permute-start(bf16[8,1664]{1,0:T(8,128)(2,1)S(1)} %pad_maximum_fusion.2), channel_id=1, source_target_pairs={{0,128},{32,160},{64,192},{96,224},{128,0},{160,32},{192,64},{224,... | collective-permute-start | bytes 79880 | tf_op jit(solution)/shard_map/ppermute | solution.py:111
  24.8 0.8 %broadcast_in_dim.59 = bf16[8,16,1664]{2,1,0:T(8,128)(2,1)} broadcast(bf16[16,1664]{1,0:T(8,128)(2,1)S(1)} %pad_maximum_fusion.1), dimensions={1,2} | broadcast | bytes 479232 | tf_op jit(solution)/shard_map/broadcast_in_dim | solution.py:158
  25.6 6.8 %all-to-all-start = ((bf16[8,16,1664]{2,1,0:T(8,128)(2,1)}), bf16[8,16,1664]{2,1,0:T(8,128)(2,1)S(1)}, u32[]{:S(2)}, u32[]{:S(2)}) async-start(bf16[8,16,1664]{2,1,0:T(8,128)(2,1)} %broadcast_in_dim.59), calls=%async_computation | async-start | bytes 851968 | tf_op jit(solution)/shard_map/all_to_all | solution.py:160
  32.4 4.9 %collective-permute-start.4 = (bf16[16,1664]{1,0:T(8,128)(2,1)S(1)}, bf16[16,1664]{1,0:T(8,128)(2,1)S(1)}, u32[]{:S(2)}, u32[]{:S(2)}) collective-permute-start(bf16[16,1664]{1,0:T(8,128)(2,1)S(1)} %pad_maximum_fusion), channel_id=1, source_target_pairs={{0,96},{32,64},{64,32},{96,0},{128,224},{160,192},{192,160},{224,1... | collective-permute-start | bytes 159752 | tf_op jit(solution)/shard_map/ppermute | solution.py:111
  37.4 1.9 %collective-permute-start.3 = (bf16[16,1664]{1,0:T(8,128)(2,1)S(1)}, bf16[16,1664]{1,0:T(8,128)(2,1)S(1)}, u32[]{:S(2)}, u32[]{:S(2)}) collective-permute-start(bf16[16,1664]{1,0:T(8,128)(2,1)S(1)} %pad_maximum_fusion), channel_id=1, source_target_pairs={{0,64},{32,96},{64,0},{96,32},{128,192},{160,224},{192,128},{224,1... | collective-permute-start | bytes 159752 | tf_op jit(solution)/shard_map/ppermute | solution.py:111
  39.3 2.4 %collective-permute-start.2 = (bf16[16,1664]{1,0:T(8,128)(2,1)S(1)}, bf16[16,1664]{1,0:T(8,128)(2,1)S(1)}, u32[]{:S(2)}, u32[]{:S(2)}) collective-permute-start(bf16[16,1664]{1,0:T(8,128)(2,1)S(1)} %pad_maximum_fusion), channel_id=1, source_target_pairs={{0,32},{32,0},{64,96},{96,64},{128,160},{160,128},{192,224},{224,1... | collective-permute-start | bytes 159752 | tf_op jit(solution)/shard_map/ppermute | solution.py:111
  43.1 0.3 collective-permute-done.3
  43.4 0.8 %collective-permute-done.2 = bf16[16,1664]{1,0:T(8,128)(2,1)S(1)} collective-permute-done((bf16[16,1664]{1,0:T(8,128)(2,1)S(1)}, bf16[16,1664]{1,0:T(8,128)(2,1)S(1)}, u32[]{:S(2)}, u32[]{:S(2)}) %collective-permute-start.2) | collective-permute-done | bytes 53280 | tf_op jit(solution)/shard_map/ppermute | solution.py:111
  44.2 0.3 convolution_convert_fusion
  44.5 0.2 fusion.51
  44.7 1.9 %all-to-all-done = bf16[8,16,1664]{2,1,0:T(8,128)(2,1)S(1)} async-done(((bf16[8,16,1664]{2,1,0:T(8,128)(2,1)}), bf16[8,16,1664]{2,1,0:T(8,128)(2,1)S(1)}, u32[]{:S(2)}, u32[]{:S(2)}) %all-to-all-start) | async-done | bytes 426016 | tf_op jit(solution)/shard_map/all_to_all | solution.py:160
  46.6 4.0 %collective-permute-start.7 = (bf16[128,1664]{1,0:T(8,128)(2,1)S(1)}, bf16[128,1664]{1,0:T(8,128)(2,1)S(1)}, u32[]{:S(2)}, u32[]{:S(2)}) collective-permute-start(bf16[128,1664]{1,0:T(8,128)(2,1)S(1)} %bitcast.14), channel_id=1, source_target_pairs={{0,1},{1,0},{2,3},{3,2},{4,5},{5,4},{6,7},{7,6},{8,9},{9,8},{10,11... | collective-permute-start | bytes 1277960 | tf_op jit(solution)/shard_map/ppermute | solution.py:162
  50.7 0.2 fusion.18
  50.9 0.3 fusion.1
  51.1 0.2 fusion.5
  51.4 0.6 collective-permute-done.7
  52.0 0.2 fusion.17
  52.2 0.4 fusion.50
  52.6 0.1 select_convert_fusion
  52.7 0.3 fusion
  53.1 13.8 %all_to_all.10 = f16[8,8,1664]{2,1,0:T(8,128)(2,1)S(1)} all-to-all(f16[8,8,1664]{2,1,0:T(8,128)(2,1)S(1)} %maximum_bitcast_fusion), channel_id=1, replica_groups=mesh['tower'=2,'z'=8,'x'=2,'y'=8,'mp'=2] {'z'}, dimensions={0} | all-to-all | bytes 425984 | tf_op jit(solution)/shard_map/all_to_all | solution.py:211
  66.9 0.2 multiply_reduce_fusion
  67.1 0.7 %fusion.83 = f32[8]{0:T(128)} fusion(f32[8,1664]{1,0:T(8,128)S(1)} %convert_reduce_fusion), kind=kLoop, calls=%fused_computation.125 | loop fusion | flops 8 | bytes 96 | tf_op jit(solution)/shard_map/add | solution.py:214
  67.8 0.7 %multiply_bitcast_fusion = f32[1,8,1536]{2,1,0:T(8,128)} fusion(f32[8,1664]{1,0:T(8,128)S(1)} %convert_reduce_fusion, f32[8,1536]{1,0:T(8,128)S(1)} %get-tuple-element.36, f32[8]{0:T(128)S(1)} %multiply_reduce_fusion, f32[]{:T(128)} %bitcast.2, f32[8]{0:T(128)S(1)} %add_rsqrt_fusion), kind=kLoop, calls=%fused_computation.45 | loop fusion | flops 61440 | bytes 147524 | tf_op jit(solution)/shard_map/broadcast_in_dim | solution.py:218
  (25 shorter events, 0.4 us)
Async XLA Ops:
  0.6 10.9 %copy-start = (s32[16]{0:T(128)S(1)}, s32[16]{0:T(128)}, u32[]{:S(2)}) copy-start(s32[16]{0:T(128)} %param.13) | copy-start | bytes 196
  2.7 9.7 %collective-permute-start = (f32[8,1536]{1,0:T(8,128)S(1)}, f32[8,1536]{1,0:T(8,128)S(1)}, u32[]{:S(2)}, u32[]{:S(2)}) collective-permute-start(f32[8,1536]{1,0:T(8,128)S(1)} %get-tuple-element.26), channel_id=1, source_target_pairs={{0,1},{1,0},{2,3},{3,2},{4,5},{5,4},{6,7},{7,6},{8,9},{9,8},{10,11... | collective-permute-start | bytes 147464 | tf_op jit(solution)/shard_map/ppermute | solution.py:143
  12.6 12.2 %collective-permute-start.6 = (bf16[8,1664]{1,0:T(8,128)(2,1)S(1)}, bf16[8,1664]{1,0:T(8,128)(2,1)S(1)}, u32[]{:S(2)}, u32[]{:S(2)}) collective-permute-start(bf16[8,1664]{1,0:T(8,128)(2,1)S(1)} %pad_maximum_fusion.2), channel_id=1, source_target_pairs={{0,272},{272,0},{16,256},{256,16},{1,273},{273,1},{17,257},{257,17... | collective-permute-start | bytes 79880 | tf_op jit(solution)/shard_map/ppermute | solution.py:156
  14.5 10.3 %collective-permute-start.5 = (bf16[8,1664]{1,0:T(8,128)(2,1)S(1)}, bf16[8,1664]{1,0:T(8,128)(2,1)S(1)}, u32[]{:S(2)}, u32[]{:S(2)}) collective-permute-start(bf16[8,1664]{1,0:T(8,128)(2,1)S(1)} %pad_maximum_fusion.2), channel_id=1, source_target_pairs={{0,256},{256,0},{1,257},{257,1},{2,258},{258,2},{3,259},{259,3},{4... | collective-permute-start | bytes 79880 | tf_op jit(solution)/shard_map/ppermute | solution.py:155
  16.5 16.0 %collective-permute-start.1 = (bf16[8,1664]{1,0:T(8,128)(2,1)S(1)}, bf16[8,1664]{1,0:T(8,128)(2,1)S(1)}, u32[]{:S(2)}, u32[]{:S(2)}) collective-permute-start(bf16[8,1664]{1,0:T(8,128)(2,1)S(1)} %pad_maximum_fusion.2), channel_id=1, source_target_pairs={{0,128},{32,160},{64,192},{96,224},{128,0},{160,32},{192,64},{224,... | collective-permute-start | bytes 79880 | tf_op jit(solution)/shard_map/ppermute | solution.py:111
  25.6 21.1 %all-to-all-start = ((bf16[8,16,1664]{2,1,0:T(8,128)(2,1)}), bf16[8,16,1664]{2,1,0:T(8,128)(2,1)S(1)}, u32[]{:S(2)}, u32[]{:S(2)}) async-start(bf16[8,16,1664]{2,1,0:T(8,128)(2,1)} %broadcast_in_dim.59), calls=%async_computation | async-start | bytes 851968 | tf_op jit(solution)/shard_map/all_to_all | solution.py:160
  32.4 10.7 %collective-permute-start.4 = (bf16[16,1664]{1,0:T(8,128)(2,1)S(1)}, bf16[16,1664]{1,0:T(8,128)(2,1)S(1)}, u32[]{:S(2)}, u32[]{:S(2)}) collective-permute-start(bf16[16,1664]{1,0:T(8,128)(2,1)S(1)} %pad_maximum_fusion), channel_id=1, source_target_pairs={{0,96},{32,64},{64,32},{96,0},{128,224},{160,192},{192,160},{224,1... | collective-permute-start | bytes 159752 | tf_op jit(solution)/shard_map/ppermute | solution.py:111
  37.4 6.1 %collective-permute-start.3 = (bf16[16,1664]{1,0:T(8,128)(2,1)S(1)}, bf16[16,1664]{1,0:T(8,128)(2,1)S(1)}, u32[]{:S(2)}, u32[]{:S(2)}) collective-permute-start(bf16[16,1664]{1,0:T(8,128)(2,1)S(1)} %pad_maximum_fusion), channel_id=1, source_target_pairs={{0,64},{32,96},{64,0},{96,32},{128,192},{160,224},{192,128},{224,1... | collective-permute-start | bytes 159752 | tf_op jit(solution)/shard_map/ppermute | solution.py:111
  39.3 5.0 %collective-permute-start.2 = (bf16[16,1664]{1,0:T(8,128)(2,1)S(1)}, bf16[16,1664]{1,0:T(8,128)(2,1)S(1)}, u32[]{:S(2)}, u32[]{:S(2)}) collective-permute-start(bf16[16,1664]{1,0:T(8,128)(2,1)S(1)} %pad_maximum_fusion), channel_id=1, source_target_pairs={{0,32},{32,0},{64,96},{96,64},{128,160},{160,128},{192,224},{224,1... | collective-permute-start | bytes 159752 | tf_op jit(solution)/shard_map/ppermute | solution.py:111
  46.6 5.4 %collective-permute-start.7 = (bf16[128,1664]{1,0:T(8,128)(2,1)S(1)}, bf16[128,1664]{1,0:T(8,128)(2,1)S(1)}, u32[]{:S(2)}, u32[]{:S(2)}) collective-permute-start(bf16[128,1664]{1,0:T(8,128)(2,1)S(1)} %bitcast.14), channel_id=1, source_target_pairs={{0,1},{1,0},{2,3},{3,2},{4,5},{5,4},{6,7},{7,6},{8,9},{9,8},{10,11... | collective-permute-start | bytes 1277960 | tf_op jit(solution)/shard_map/ppermute | solution.py:162

commit v2 on v1

--- a/solution.py
+++ b/solution.py
@@ -55,8 +55,10 @@
 
 
 def text_kernel(
-    core_ref, lengths_ref, slices_hbm, weights_hbm, keep_ref, send_ref, slices, weights, sems
+    core_ref, lengths_hbm, slices_hbm, weights_hbm, keep_ref, send_ref, slices, weights, sems, lengths_ref
 ):
+    lengths_copy = pltpu.make_async_copy(lengths_hbm, lengths_ref, sems.at[sems.shape[0] - 1])
+    lengths_copy.start()
     first_copy, copies = fetch(slices_hbm, weights_hbm, slices, weights, sems)
     width = weights_hbm.shape[0]
     row_count = slices.shape[0]
@@ -67,6 +69,7 @@
     shape = (row_count, 2 * width)
     row = lax.broadcasted_iota(jnp.int32, shape, 0)
     lengths = jnp.zeros(shape, jnp.int32)
+    lengths_copy.wait()
     for index in range(row_count):
         lengths = jnp.where(row == index, lengths_ref[index], lengths)
     second = (lax.broadcasted_iota(jnp.int32, shape, 1) >= width).astype(jnp.int32)
@@ -81,25 +84,39 @@
     project(pooled, weights, copies, core_ref, keep_ref, send_ref)
 
 
-def pooled_partial(kernel, scalars, slices, weights):
+def pooled_partial(kernel, core_index, slices, weights, lengths=None):
     row_count = slices.shape[0]
     depth, width = weights.shape
     padded = -(-depth // LANES) * LANES
     pieces = -(-depth // PIECE)
     any_space = pl.BlockSpec(memory_space=pl.ANY)
     half = jax.ShapeDtypeStruct((row_count // 2, width), jnp.float32)
+    given = (slices, weights) if lengths is None else (lengths, slices, weights)
+    scratch = [
+        pltpu.VMEM(slices.shape, jnp.bfloat16),
+        pltpu.VMEM((padded, width), jnp.bfloat16),
+        pltpu.SemaphoreType.DMA((2 + pieces,)),
+    ]
+    if lengths is not None:
+        scratch.append(pltpu.SMEM(lengths.shape, jnp.int32))
     return pl.pallas_call(
         kernel,
         out_shape=(half, half),
-        in_specs=[pl.BlockSpec(memory_space=pltpu.SMEM)] * len(scalars) + [any_space] * 2,
+        in_specs=[pl.BlockSpec(memory_space=pltpu.SMEM)] + [any_space] * len(given),
         out_specs=(pl.BlockSpec(memory_space=pltpu.VMEM),) * 2,
-        scratch_shapes=[
-            pltpu.VMEM(slices.shape, jnp.bfloat16),
-            pltpu.VMEM((padded, width), jnp.bfloat16),
-            pltpu.SemaphoreType.DMA((1 + pieces,)),
-        ],
+        scratch_shapes=scratch,
         compiler_params=pltpu.CompilerParams(vmem_limit_bytes=32 * 2**20),
-    )(*scalars, slices, weights)
+    )(core_index, *given)
+
+
+def mirrored(blocks, axis):
+    members = lax.axis_size(axis)
+    cores = lax.axis_size("mp")
+    groups = [
+        [at * cores + core for at in (range(members) if core == 0 else reversed(range(members)))]
+        for core in range(cores)
+    ]
+    return lax.all_to_all(blocks, (axis, "mp"), 0, 0, axis_index_groups=groups, tiled=True)
 
 
 def swap_gather(block, axis, after):
@@ -117,7 +134,8 @@
     slot = lax.broadcasted_iota(jnp.int32, (members * size, members * size), 1)
     number = slot // size
     came_from = lax.axis_index(axis) ^ (number // 2 + (number % 2) * half)
-    moves = (place // size == came_from) & (place % size == slot % size)
+    member = jnp.where(lax.axis_index("mp") == 0, place // size, members - 1 - place // size)
+    moves = (member == came_from) & (place % size == slot % size)
     ordered = jnp.dot(moves.astype(held.dtype), held, preferred_element_type=jnp.float32)
     return ordered.astype(held.dtype)
 
@@ -137,8 +155,8 @@
     core_index = core.astype(jnp.int32).reshape(1)
     kept, sent = lax.cond(
         tower == 0,
-        lambda: pooled_partial(image_kernel, (core_index,), slices, image_proj),
-        lambda: pooled_partial(text_kernel, (core_index, text_lengths), slices, text_proj),
+        lambda: pooled_partial(image_kernel, core_index, slices, image_proj),
+        lambda: pooled_partial(text_kernel, core_index, slices, text_proj, text_lengths),
     )
     embedding = kept + lax.ppermute(sent, "mp", [(0, 1), (1, 0)])
     inverse = lax.rsqrt(jnp.sum(embedding * embedding, axis=1, keepdims=True) + EPS)
@@ -157,7 +175,7 @@
     other = jnp.concatenate([near, across], axis=0)
     copies = jnp.broadcast_to(other[None], (n_y,) + other.shape)
     own_all = swap_gather(own, "z", other[:1, :LANES])
-    other_mine = lax.all_to_all(copies, "y", 0, 0, tiled=True)
+    other_mine = mirrored(copies, "y")
     other_mine = other_mine.reshape(n_y * n_x * share, width + LANES)
     other_theirs = lax.ppermute(other_mine, "mp", [(0, 1), (1, 0)])
 
@@ -173,16 +191,19 @@
         return ((z_at * n_x + x_at) * n_y + y_at) * row_count
 
     own_slot = lax.iota(jnp.int32, n_z * share)
-    own_place = pair_at(own_slot // share, x, y) + core * share + own_slot % share
+    own_z = jnp.where(core == 0, own_slot // share, n_z - 1 - own_slot // share)
+    own_place = pair_at(own_z, x, y) + core * share + own_slot % share
     other_slot = lax.iota(jnp.int32, n_y * n_x * share)
     other_x = x ^ (other_slot // share % n_x)
-    other_base = pair_at(z, other_x, other_slot // (n_x * share)) + other_slot % share
+    other_y = other_slot // (n_x * share)
+    other_reversed = n_y - 1 - other_y
     own_key = jnp.where(tower == 0, sent_key(own_all), own_place)
     temper = jnp.exp(log_scale[0])
     own_low = own_all[:, :width]
 
     def score(others, other_core):
-        other_place = other_base + other_core * share
+        other_at = jnp.where(other_core == 0, other_y, other_reversed)
+        other_place = pair_at(z, other_x, other_at) + other_core * share + other_slot % share
         other_key = jnp.where(tower == 0, other_place, sent_key(others))
         other_low = others[:, :width]
         logits = (
@@ -208,7 +229,7 @@
     lane = lax.broadcasted_iota(jnp.int32, (n_z * share, LANES), 1)
     loss_block = jnp.where(lane == 0, loss_high, loss_rest).astype(jnp.float16)
     sums = jnp.concatenate([grad_part.astype(jnp.float16), loss_block], axis=1)
-    sums = lax.all_to_all(sums.reshape(n_z, share, width + LANES), "z", 0, 0, tiled=True)
+    sums = mirrored(sums.reshape(n_z, share, width + LANES), "z")
     total = jnp.sum(sums.astype(jnp.float32), axis=0)
     grad_sum = temper * total[:, :width]
     loss_sum = total[:, width] + total[:, width + 1]

time: 69.8 us -> 66.5 us (0.953)
  the two profiles are of different devices: /device:TPU:1 before, /device:TPU:10 now
where the time goes in v2:
time: 66.5 us; the launch traced here: 66 us
  starting transfers between devices  39.5 us (59%)
  blocking collectives  13.6 us (20%)
  waiting for transfers between devices  3.65 us (5%)
  other arithmetic  2.78 us (4%)
  between operations  2.24 us (3%)
  Pallas kernels  1.97 us (3%)
  matrix products  1.42 us (2%)
  local copies, waits for them, and re-layouts  0.79 us (1%)
    ppermute x4, starting transfers between devices, brought(): lax.ppermute(value, axis, [(index, index ^ across) for index in range(mem...  21 us
    all_to_all x1, blocking collectives, mirrored(): lax.all_to_all(blocks, (axis, 'mp'), 0, 0, axis_index_groups=groups, tile...  13.6 us
    all_to_all x1, starting transfers between devices, mirrored(): lax.all_to_all(blocks, (axis, 'mp'), 0, 0, axis_index_groups=groups, tile...  7.55 us
    ppermute x1, starting transfers between devices, shards(): near = lax.ppermute(own, 'tower', [(0, 1), (1, 0)])  3.63 us
    ppermute x1, starting transfers between devices, shards(): across = lax.ppermute(own, ('tower', 'x'), [(0, 3), (3, 0), (1, 2), (2, 1)])  3.48 us
    pallas_call x1, Pallas kernels, pooled_partial(): pl.pallas_call(kernel, out_shape=(half, half), in_specs=[pl.BlockSpec(mem...  1.97 us
    ppermute x1, starting transfers between devices, shards(): embedding = kept + lax.ppermute(sent, 'mp', [(0, 1), (1, 0)])  1.92 us
    ppermute x1, starting transfers between devices, shards(): other_theirs = lax.ppermute(other_mine, 'mp', [(0, 1), (1, 0)])  1.92 us
  transfers between devices with their start and end apart: 9, of which 4 were waited for; matrix products, arithmetic and copies ran while one was open for 3% of the time, Pallas kernels for 0%

profile of v2, /device:TPU:10, one launch (start us, length us, event | category | flops | bytes accessed | tf_op | source)
XLA Modules:
  0.0 66.0 jit_solution(7176634727225494474)
XLA Ops:
  0.6 2.0 %conditional.1 = ((f32[8,1536]{1,0:T(8,128)S(1)}, f32[8,1536]{1,0:T(8,128)S(1)})) conditional(s32[]{:T(128)} %convert_element_type.48, (s32[1]{0:T(128)}, s32[16]{0:T(128)}, bf16[16,18432]{1,0:T(8,128)(2,1)}, bf16[576,1536]{1,0:T(8,128)(2,1)}) %tuple.31, (s32[1]{0:T(128)}, bf16[16,18432]{1,0:T(8,128)(2,1)}, bf16[768,1536]{1,0:T(8,128)(2,1)}) %tuple.32), branch_computations={%region_0.0_spmd, %region_1.0_spmd} | conditional | bytes 8 | solution.py:156
  0.7 2.0 %branch_0_fun.1 = (f32[8,1536]{1,0:T(8,128)S(1)}, f32[8,1536]{1,0:T(8,128)S(1)}) custom-call(s32[1]{0:T(128)} %get-tuple-element.14.core_ref, s32[16]{0:T(128)} %get-tuple-element.29.lengths_hbm, bf16[16,18432]{1,0:T(8,128)(2,1)} %get-tuple-element.16.slices_hbm, bf16[576,1536]{1,0:T(8,128)(2,1)} %get-tuple-element.30.weights_hbm), custom_call_target="tpu_custom_call" | custom-call | tf_op jit(solution)/shard_map/cond/branch_0_fun/pallas_call | solution.py:102
  2.6 1.9 %collective-permute-start = (f32[8,1536]{1,0:T(8,128)S(1)}, f32[8,1536]{1,0:T(8,128)S(1)}, u32[]{:S(2)}, u32[]{:S(2)}) collective-permute-start(f32[8,1536]{1,0:T(8,128)S(1)} %get-tuple-element.26), channel_id=1, source_target_pairs={{0,1},{1,0},{2,3},{3,2},{4,5},{5,4},{6,7},{7,6},{8,9},{9,8},{10,11... | collective-permute-start | bytes 147464 | tf_op jit(solution)/shard_map/ppermute | solution.py:161
  4.6 0.1 fusion.93
  4.7 0.1 select_select_fusion.1
  4.8 1.0 %collective-permute-done = f32[8,1536]{1,0:T(8,128)S(1)} collective-permute-done((f32[8,1536]{1,0:T(8,128)S(1)}, f32[8,1536]{1,0:T(8,128)S(1)}, u32[]{:S(2)}, u32[]{:S(2)}) %collective-permute-start) | collective-permute-done | bytes 49184 | tf_op jit(solution)/shard_map/ppermute | solution.py:161
  5.8 0.1 multiply_reduce_fusion.1
  6.0 3.5 %collective-permute-start.6 = (bf16[8,1664]{1,0:T(8,128)(2,1)S(1)}, bf16[8,1664]{1,0:T(8,128)(2,1)S(1)}, u32[]{:S(2)}, u32[]{:S(2)}) collective-permute-start(bf16[8,1664]{1,0:T(8,128)(2,1)S(1)} %pad_maximum_fusion.2), channel_id=1, source_target_pairs={{0,272},{272,0},{16,256},{256,16},{1,273},{273,1},{17,257},{257,17... | collective-permute-start | bytes 79880 | tf_op jit(solution)/shard_map/ppermute | solution.py:174
  9.5 3.6 %collective-permute-start.5 = (bf16[8,1664]{1,0:T(8,128)(2,1)S(1)}, bf16[8,1664]{1,0:T(8,128)(2,1)S(1)}, u32[]{:S(2)}, u32[]{:S(2)}) collective-permute-start(bf16[8,1664]{1,0:T(8,128)(2,1)S(1)} %pad_maximum_fusion.2), channel_id=1, source_target_pairs={{0,256},{256,0},{1,257},{257,1},{2,258},{258,2},{3,259},{259,3},{4... | collective-permute-start | bytes 79880 | tf_op jit(solution)/shard_map/ppermute | solution.py:173
  13.1 10.9 %collective-permute-start.1 = (bf16[8,1664]{1,0:T(8,128)(2,1)S(1)}, bf16[8,1664]{1,0:T(8,128)(2,1)S(1)}, u32[]{:S(2)}, u32[]{:S(2)}) collective-permute-start(bf16[8,1664]{1,0:T(8,128)(2,1)S(1)} %pad_maximum_fusion.2), channel_id=1, source_target_pairs={{0,128},{32,160},{64,192},{96,224},{128,0},{160,32},{192,64},{224,... | collective-permute-start | bytes 79880 | tf_op jit(solution)/shard_map/ppermute | solution.py:128
  24.1 0.8 %broadcast_in_dim.59 = bf16[8,16,1664]{2,1,0:T(8,128)(2,1)} broadcast(bf16[16,1664]{1,0:T(8,128)(2,1)S(1)} %pad_maximum_fusion.1), dimensions={1,2} | broadcast | bytes 479232 | tf_op jit(solution)/shard_map/broadcast_in_dim | solution.py:176
  24.9 7.5 %all-to-all-start = ((bf16[8,16,1664]{2,1,0:T(8,128)(2,1)}), bf16[8,16,1664]{2,1,0:T(8,128)(2,1)S(1)}, u32[]{:S(2)}, u32[]{:S(2)}) async-start(bf16[8,16,1664]{2,1,0:T(8,128)(2,1)} %broadcast_in_dim.59), calls=%async_computation | async-start | bytes 851968 | tf_op jit(solution)/shard_map/all_to_all | solution.py:119
  32.4 5.2 %collective-permute-start.4 = (bf16[16,1664]{1,0:T(8,128)(2,1)S(1)}, bf16[16,1664]{1,0:T(8,128)(2,1)S(1)}, u32[]{:S(2)}, u32[]{:S(2)}) collective-permute-start(bf16[16,1664]{1,0:T(8,128)(2,1)S(1)} %pad_maximum_fusion), channel_id=1, source_target_pairs={{0,96},{32,64},{64,32},{96,0},{128,224},{160,192},{192,160},{224,1... | collective-permute-start | bytes 159752 | tf_op jit(solution)/shard_map/ppermute | solution.py:128
  37.6 1.9 %collective-permute-start.3 = (bf16[16,1664]{1,0:T(8,128)(2,1)S(1)}, bf16[16,1664]{1,0:T(8,128)(2,1)S(1)}, u32[]{:S(2)}, u32[]{:S(2)}) collective-permute-start(bf16[16,1664]{1,0:T(8,128)(2,1)S(1)} %pad_maximum_fusion), channel_id=1, source_target_pairs={{0,64},{32,96},{64,0},{96,32},{128,192},{160,224},{192,128},{224,1... | collective-permute-start | bytes 159752 | tf_op jit(solution)/shard_map/ppermute | solution.py:128
  39.6 3.0 %collective-permute-start.2 = (bf16[16,1664]{1,0:T(8,128)(2,1)S(1)}, bf16[16,1664]{1,0:T(8,128)(2,1)S(1)}, u32[]{:S(2)}, u32[]{:S(2)}) collective-permute-start(bf16[16,1664]{1,0:T(8,128)(2,1)S(1)} %pad_maximum_fusion), channel_id=1, source_target_pairs={{0,32},{32,0},{64,96},{96,64},{128,160},{160,128},{192,224},{224,1... | collective-permute-start | bytes 159752 | tf_op jit(solution)/shard_map/ppermute | solution.py:128
  43.9 0.6 collective-permute-done.3
  44.6 1.0 %collective-permute-done.2 = bf16[16,1664]{1,0:T(8,128)(2,1)S(1)} collective-permute-done((bf16[16,1664]{1,0:T(8,128)(2,1)S(1)}, bf16[16,1664]{1,0:T(8,128)(2,1)S(1)}, u32[]{:S(2)}, u32[]{:S(2)}) %collective-permute-start.2) | collective-permute-done | bytes 53280 | tf_op jit(solution)/shard_map/ppermute | solution.py:128
  45.6 0.3 convolution_convert_fusion
  45.9 0.2 fusion.53
  46.1 1.9 %collective-permute-start.7 = (bf16[128,1664]{1,0:T(8,128)(2,1)S(1)}, bf16[128,1664]{1,0:T(8,128)(2,1)S(1)}, u32[]{:S(2)}, u32[]{:S(2)}) collective-permute-start(bf16[128,1664]{1,0:T(8,128)(2,1)S(1)} %bitcast.14), channel_id=1, source_target_pairs={{0,1},{1,0},{2,3},{3,2},{4,5},{5,4},{6,7},{7,6},{8,9},{9,8},{10,11... | collective-permute-start | bytes 1277960 | tf_op jit(solution)/shard_map/ppermute | solution.py:180
  48.0 0.2 fusion.18
  48.2 0.3 fusion.1
  48.5 0.2 fusion.5
  48.7 1.0 %collective-permute-done.7 = bf16[128,1664]{1,0:T(8,128)(2,1)S(1)} collective-permute-done((bf16[128,1664]{1,0:T(8,128)(2,1)S(1)}, bf16[128,1664]{1,0:T(8,128)(2,1)S(1)}, u32[]{:S(2)}, u32[]{:S(2)}) %collective-permute-start.7) | collective-permute-done | bytes 426016 | tf_op jit(solution)/shard_map/ppermute | solution.py:180
  49.8 0.2 fusion.17
  50.0 0.4 fusion.50
  50.4 0.1 select_convert_fusion
  50.4 0.3 fusion
  50.8 13.6 %all_to_all.10 = f16[8,8,1664]{2,1,0:T(8,128)(2,1)S(1)} all-to-all(f16[8,8,1664]{2,1,0:T(8,128)(2,1)S(1)} %maximum_bitcast_fusion), channel_id=1, replica_groups={{0,32,64,96,128,160,192,224},{225,193,161,129,97,65,33,1},{2,34,66,98,1..., dimensions={0} | all-to-all | bytes 425984 | tf_op jit(solution)/shard_map/all_to_all | solution.py:119
  64.4 0.2 multiply_reduce_fusion
  64.6 0.7 %fusion.85 = f32[8]{0:T(128)} fusion(f32[8,1664]{1,0:T(8,128)S(1)} %convert_reduce_fusion), kind=kLoop, calls=%fused_computation.129 | loop fusion | flops 8 | bytes 96 | tf_op jit(solution)/shard_map/add | solution.py:235
  65.3 0.7 %multiply_bitcast_fusion = f32[1,8,1536]{2,1,0:T(8,128)} fusion(f32[8,1664]{1,0:T(8,128)S(1)} %convert_reduce_fusion, f32[8,1536]{1,0:T(8,128)S(1)} %get-tuple-element.36, f32[8]{0:T(128)S(1)} %multiply_reduce_fusion, f32[]{:T(128)} %bitcast.2, f32[8]{0:T(128)S(1)} %add_rsqrt_fusion), kind=kLoop, calls=%fused_computation.45 | loop fusion | flops 61440 | bytes 147524 | tf_op jit(solution)/shard_map/broadcast_in_dim | solution.py:239
  (25 shorter events, 0.3 us)
Async XLA Ops:
  0.6 4.0 %copy-start = (s32[16]{0:T(128)S(1)}, s32[16]{0:T(128)}, u32[]{:S(2)}) copy-start(s32[16]{0:T(128)} %param.13) | copy-start | bytes 196
  2.6 3.1 %collective-permute-start = (f32[8,1536]{1,0:T(8,128)S(1)}, f32[8,1536]{1,0:T(8,128)S(1)}, u32[]{:S(2)}, u32[]{:S(2)}) collective-permute-start(f32[8,1536]{1,0:T(8,128)S(1)} %get-tuple-element.26), channel_id=1, source_target_pairs={{0,1},{1,0},{2,3},{3,2},{4,5},{5,4},{6,7},{7,6},{8,9},{9,8},{10,11... | collective-permute-start | bytes 147464 | tf_op jit(solution)/shard_map/ppermute | solution.py:161
  6.0 18.1 %collective-permute-start.6 = (bf16[8,1664]{1,0:T(8,128)(2,1)S(1)}, bf16[8,1664]{1,0:T(8,128)(2,1)S(1)}, u32[]{:S(2)}, u32[]{:S(2)}) collective-permute-start(bf16[8,1664]{1,0:T(8,128)(2,1)S(1)} %pad_maximum_fusion.2), channel_id=1, source_target_pairs={{0,272},{272,0},{16,256},{256,16},{1,273},{273,1},{17,257},{257,17... | collective-permute-start | bytes 79880 | tf_op jit(solution)/shard_map/ppermute | solution.py:174
  9.5 14.6 %collective-permute-start.5 = (bf16[8,1664]{1,0:T(8,128)(2,1)S(1)}, bf16[8,1664]{1,0:T(8,128)(2,1)S(1)}, u32[]{:S(2)}, u32[]{:S(2)}) collective-permute-start(bf16[8,1664]{1,0:T(8,128)(2,1)S(1)} %pad_maximum_fusion.2), channel_id=1, source_target_pairs={{0,256},{256,0},{1,257},{257,1},{2,258},{258,2},{3,259},{259,3},{4... | collective-permute-start | bytes 79880 | tf_op jit(solution)/shard_map/ppermute | solution.py:173
  13.1 19.3 %collective-permute-start.1 = (bf16[8,1664]{1,0:T(8,128)(2,1)S(1)}, bf16[8,1664]{1,0:T(8,128)(2,1)S(1)}, u32[]{:S(2)}, u32[]{:S(2)}) collective-permute-start(bf16[8,1664]{1,0:T(8,128)(2,1)S(1)} %pad_maximum_fusion.2), channel_id=1, source_target_pairs={{0,128},{32,160},{64,192},{96,224},{128,0},{160,32},{192,64},{224,... | collective-permute-start | bytes 79880 | tf_op jit(solution)/shard_map/ppermute | solution.py:128
  24.9 21.2 %all-to-all-start = ((bf16[8,16,1664]{2,1,0:T(8,128)(2,1)}), bf16[8,16,1664]{2,1,0:T(8,128)(2,1)S(1)}, u32[]{:S(2)}, u32[]{:S(2)}) async-start(bf16[8,16,1664]{2,1,0:T(8,128)(2,1)} %broadcast_in_dim.59), calls=%async_computation | async-start | bytes 851968 | tf_op jit(solution)/shard_map/all_to_all | solution.py:119
  32.4 11.5 %collective-permute-start.4 = (bf16[16,1664]{1,0:T(8,128)(2,1)S(1)}, bf16[16,1664]{1,0:T(8,128)(2,1)S(1)}, u32[]{:S(2)}, u32[]{:S(2)}) collective-permute-start(bf16[16,1664]{1,0:T(8,128)(2,1)S(1)} %pad_maximum_fusion), channel_id=1, source_target_pairs={{0,96},{32,64},{64,32},{96,0},{128,224},{160,192},{192,160},{224,1... | collective-permute-start | bytes 159752 | tf_op jit(solution)/shard_map/ppermute | solution.py:128
  37.6 6.9 %collective-permute-start.3 = (bf16[16,1664]{1,0:T(8,128)(2,1)S(1)}, bf16[16,1664]{1,0:T(8,128)(2,1)S(1)}, u32[]{:S(2)}, u32[]{:S(2)}) collective-permute-start(bf16[16,1664]{1,0:T(8,128)(2,1)S(1)} %pad_maximum_fusion), channel_id=1, source_target_pairs={{0,64},{32,96},{64,0},{96,32},{128,192},{160,224},{192,128},{224,1... | collective-permute-start | bytes 159752 | tf_op jit(solution)/shard_map/ppermute | solution.py:128
  39.6 6.0 %collective-permute-start.2 = (bf16[16,1664]{1,0:T(8,128)(2,1)S(1)}, bf16[16,1664]{1,0:T(8,128)(2,1)S(1)}, u32[]{:S(2)}, u32[]{:S(2)}) collective-permute-start(bf16[16,1664]{1,0:T(8,128)(2,1)S(1)} %pad_maximum_fusion), channel_id=1, source_target_pairs={{0,32},{32,0},{64,96},{96,64},{128,160},{160,128},{192,224},{224,1... | collective-permute-start | bytes 159752 | tf_op jit(solution)/shard_map/ppermute | solution.py:128
  46.1 3.7 %collective-permute-start.7 = (bf16[128,1664]{1,0:T(8,128)(2,1)S(1)}, bf16[128,1664]{1,0:T(8,128)(2,1)S(1)}, u32[]{:S(2)}, u32[]{:S(2)}) collective-permute-start(bf16[128,1664]{1,0:T(8,128)(2,1)S(1)} %bitcast.14), channel_id=1, source_target_pairs={{0,1},{1,0},{2,3},{3,2},{4,5},{5,4},{6,7},{7,6},{8,9},{9,8},{10,11... | collective-permute-start | bytes 1277960 | tf_op jit(solution)/shard_map/ppermute | solution.py:180

commit v3 on v2

--- a/solution.py
+++ b/solution.py
@@ -140,6 +140,27 @@
     return ordered.astype(held.dtype)
 
 
+def final_kernel(scale_ref, total_ref, embedding_ref, grads_hbm, losses_hbm, grads, losses, sems):
+    share, width = embedding_ref.shape
+    loss = total_ref[:, width : width + 1] + total_ref[:, width + 1 : width + 2]
+    row = lax.broadcasted_iota(jnp.int32, (share, LANES), 0)
+    column = lax.broadcasted_iota(jnp.int32, (share, LANES), 1)
+    diagonal = jnp.where(row == column, jnp.broadcast_to(loss, (share, LANES)), 0.0)
+    losses[...] = jnp.sum(diagonal, axis=0, keepdims=True)[:, :share]
+    losses_copy = pltpu.make_async_copy(losses, losses_hbm, sems.at[0])
+    losses_copy.start()
+    embedding = embedding_ref[...]
+    inverse = lax.rsqrt(jnp.sum(embedding * embedding, axis=1, keepdims=True) + EPS)
+    unit = embedding * inverse
+    grad_sum = jnp.exp(jnp.full((1, LANES), scale_ref[0], jnp.float32))[:, :1] * total_ref[:, :width]
+    along = jnp.sum(unit * grad_sum, axis=1, keepdims=True)
+    grads[0] = inverse * (grad_sum - unit * along)
+    grads_copy = pltpu.make_async_copy(grads, grads_hbm, sems.at[1])
+    grads_copy.start()
+    losses_copy.wait()
+    grads_copy.wait()
+
+
 def shards(tower_inputs, image_proj, text_proj, text_lengths, partner, log_scale, bias):
     slices = tower_inputs[0, :, 0, :]
     row_count = slices.shape[0]
@@ -231,12 +252,23 @@
     sums = jnp.concatenate([grad_part.astype(jnp.float16), loss_block], axis=1)
     sums = mirrored(sums.reshape(n_z, share, width + LANES), "z")
     total = jnp.sum(sums.astype(jnp.float32), axis=0)
-    grad_sum = temper * total[:, :width]
-    loss_sum = total[:, width] + total[:, width + 1]
-
-    along = jnp.sum(unit * grad_sum, axis=1, keepdims=True)
-    gradient = inverse * (grad_sum - unit * along)
-    return (gradient[None], loss_sum[None])
+    vmem = pl.BlockSpec(memory_space=pltpu.VMEM)
+    any_space = pl.BlockSpec(memory_space=pl.ANY)
+    return pl.pallas_call(
+        final_kernel,
+        out_shape=(
+            jax.ShapeDtypeStruct((1, share, width), jnp.float32),
+            jax.ShapeDtypeStruct((1, share), jnp.float32),
+        ),
+        in_specs=[pl.BlockSpec(memory_space=pltpu.SMEM), vmem, vmem],
+        out_specs=(any_space, any_space),
+        scratch_shapes=[
+            pltpu.VMEM((1, share, width), jnp.float32),
+            pltpu.VMEM((1, share), jnp.float32),
+            pltpu.SemaphoreType.DMA((2,)),
+        ],
+        compiler_params=pltpu.CompilerParams(vmem_limit_bytes=8 * 2**20),
+    )(log_scale, total, embedding)
 
 
 def solution(mesh):

time: 66.5 us -> 65.8 us (0.989)
  other arithmetic: 2.78 us -> 1.2 us
  Pallas kernels: 1.97 us -> 2.81 us
    pallas_call x0 -> x1, Pallas kernels: none -> 0.84 us  [shards(): pl.pallas_call(final_kernel, out_shape=(jax.ShapeDtypeStruct((1, share, w...]
    broadcast_in_dim x1 -> x0, other arithmetic: 0.7 us -> none  [shards(): return (gradient[None], loss_sum[None])]
    add x1 -> x0, other arithmetic: 0.7 us -> none  [shards(): loss_sum = total[:, width] + total[:, width + 1]]
where the time goes in v3:
time: 65.8 us; the launch traced here: 65.3 us
  starting transfers between devices  39.5 us (60%)
  blocking collectives  13.6 us (21%)
  waiting for transfers between devices  3.67 us (6%)
  Pallas kernels  2.81 us (4%)
  between operations  2.24 us (3%)
  matrix products  1.42 us (2%)
  other arithmetic  1.2 us (2%)
  local copies, waits for them, and re-layouts  0.79 us (1%)
    ppermute x4, starting transfers between devices, brought(): lax.ppermute(value, axis, [(index, index ^ across) for index in range(mem...  21 us
    all_to_all x1, blocking collectives, mirrored(): lax.all_to_all(blocks, (axis, 'mp'), 0, 0, axis_index_groups=groups, tile...  13.6 us
    all_to_all x1, starting transfers between devices, mirrored(): lax.all_to_all(blocks, (axis, 'mp'), 0, 0, axis_index_groups=groups, tile...  7.55 us
    ppermute x1, starting transfers between devices, shards(): near = lax.ppermute(own, 'tower', [(0, 1), (1, 0)])  3.63 us
    ppermute x1, starting transfers between devices, shards(): across = lax.ppermute(own, ('tower', 'x'), [(0, 3), (3, 0), (1, 2), (2, 1)])  3.48 us
    pallas_call x1, Pallas kernels, pooled_partial(): pl.pallas_call(kernel, out_shape=(half, half), in_specs=[pl.BlockSpec(mem...  1.97 us
    ppermute x1, starting transfers between devices, shards(): embedding = kept + lax.ppermute(sent, 'mp', [(0, 1), (1, 0)])  1.92 us
    ppermute x1, starting transfers between devices, shards(): other_theirs = lax.ppermute(other_mine, 'mp', [(0, 1), (1, 0)])  1.92 us
  transfers between devices with their start and end apart: 9, of which 4 were waited for; matrix products, arithmetic and copies ran while one was open for 3% of the time, Pallas kernels for 0%

profile of v3, /device:TPU:10, one launch (start us, length us, event | category | flops | bytes accessed | tf_op | source)
XLA Modules:
  0.0 65.3 jit_solution(9350920021470399200)
XLA Ops:
  0.6 2.0 %conditional.1 = ((f32[8,1536]{1,0:T(8,128)S(1)}, f32[8,1536]{1,0:T(8,128)S(1)})) conditional(s32[]{:T(128)} %convert_element_type.48, (s32[1]{0:T(128)}, s32[16]{0:T(128)}, bf16[16,18432]{1,0:T(8,128)(2,1)}, bf16[576,1536]{1,0:T(8,128)(2,1)}) %tuple.29, (s32[1]{0:T(128)}, bf16[16,18432]{1,0:T(8,128)(2,1)}, bf16[768,1536]{1,0:T(8,128)(2,1)}) %tuple.30), branch_computations={%region_0.0_spmd, %region_1.0_spmd} | conditional | bytes 8 | solution.py:177
  0.7 2.0 %branch_0_fun.1 = (f32[8,1536]{1,0:T(8,128)S(1)}, f32[8,1536]{1,0:T(8,128)S(1)}) custom-call(s32[1]{0:T(128)} %get-tuple-element.14.core_ref, s32[16]{0:T(128)} %get-tuple-element.29.lengths_hbm, bf16[16,18432]{1,0:T(8,128)(2,1)} %get-tuple-element.16.slices_hbm, bf16[576,1536]{1,0:T(8,128)(2,1)} %get-tuple-element.30.weights_hbm), custom_call_target="tpu_custom_call" | custom-call | tf_op jit(solution)/shard_map/cond/branch_0_fun/pallas_call | solution.py:102
  2.6 1.9 %collective-permute-start = (f32[8,1536]{1,0:T(8,128)S(1)}, f32[8,1536]{1,0:T(8,128)S(1)}, u32[]{:S(2)}, u32[]{:S(2)}) collective-permute-start(f32[8,1536]{1,0:T(8,128)S(1)} %get-tuple-element.26), channel_id=1, source_target_pairs={{0,1},{1,0},{2,3},{3,2},{4,5},{5,4},{6,7},{7,6},{8,9},{9,8},{10,11... | collective-permute-start | bytes 147464 | tf_op jit(solution)/shard_map/ppermute | solution.py:182
  4.6 0.1 fusion.92
  4.7 0.1 select_select_fusion.1
  4.8 1.0 %collective-permute-done = f32[8,1536]{1,0:T(8,128)S(1)} collective-permute-done((f32[8,1536]{1,0:T(8,128)S(1)}, f32[8,1536]{1,0:T(8,128)S(1)}, u32[]{:S(2)}, u32[]{:S(2)}) %collective-permute-start) | collective-permute-done | bytes 49184 | tf_op jit(solution)/shard_map/ppermute | solution.py:182
  5.8 0.1 multiply_reduce_fusion
  5.9 0.1 multiply_convert_fusion
  6.0 3.5 %collective-permute-start.6 = (bf16[8,1664]{1,0:T(8,128)(2,1)S(1)}, bf16[8,1664]{1,0:T(8,128)(2,1)S(1)}, u32[]{:S(2)}, u32[]{:S(2)}) collective-permute-start(bf16[8,1664]{1,0:T(8,128)(2,1)S(1)} %pad_maximum_fusion.2), channel_id=1, source_target_pairs={{0,272},{272,0},{16,256},{256,16},{1,273},{273,1},{17,257},{257,17... | collective-permute-start | bytes 79880 | tf_op jit(solution)/shard_map/ppermute | solution.py:195
  9.5 3.6 %collective-permute-start.5 = (bf16[8,1664]{1,0:T(8,128)(2,1)S(1)}, bf16[8,1664]{1,0:T(8,128)(2,1)S(1)}, u32[]{:S(2)}, u32[]{:S(2)}) collective-permute-start(bf16[8,1664]{1,0:T(8,128)(2,1)S(1)} %pad_maximum_fusion.2), channel_id=1, source_target_pairs={{0,256},{256,0},{1,257},{257,1},{2,258},{258,2},{3,259},{259,3},{4... | collective-permute-start | bytes 79880 | tf_op jit(solution)/shard_map/ppermute | solution.py:194
  13.1 10.9 %collective-permute-start.1 = (bf16[8,1664]{1,0:T(8,128)(2,1)S(1)}, bf16[8,1664]{1,0:T(8,128)(2,1)S(1)}, u32[]{:S(2)}, u32[]{:S(2)}) collective-permute-start(bf16[8,1664]{1,0:T(8,128)(2,1)S(1)} %pad_maximum_fusion.2), channel_id=1, source_target_pairs={{0,128},{32,160},{64,192},{96,224},{128,0},{160,32},{192,64},{224,... | collective-permute-start | bytes 79880 | tf_op jit(solution)/shard_map/ppermute | solution.py:128
  24.1 0.8 %broadcast_in_dim.54 = bf16[8,16,1664]{2,1,0:T(8,128)(2,1)} broadcast(bf16[16,1664]{1,0:T(8,128)(2,1)S(1)} %pad_maximum_fusion.1), dimensions={1,2} | broadcast | bytes 479232 | tf_op jit(solution)/shard_map/broadcast_in_dim | solution.py:197
  24.9 7.5 %all-to-all-start = ((bf16[8,16,1664]{2,1,0:T(8,128)(2,1)}), bf16[8,16,1664]{2,1,0:T(8,128)(2,1)S(1)}, u32[]{:S(2)}, u32[]{:S(2)}) async-start(bf16[8,16,1664]{2,1,0:T(8,128)(2,1)} %broadcast_in_dim.54), calls=%async_computation | async-start | bytes 851968 | tf_op jit(solution)/shard_map/all_to_all | solution.py:119
  32.4 5.2 %collective-permute-start.4 = (bf16[16,1664]{1,0:T(8,128)(2,1)S(1)}, bf16[16,1664]{1,0:T(8,128)(2,1)S(1)}, u32[]{:S(2)}, u32[]{:S(2)}) collective-permute-start(bf16[16,1664]{1,0:T(8,128)(2,1)S(1)} %pad_maximum_fusion), channel_id=1, source_target_pairs={{0,96},{32,64},{64,32},{96,0},{128,224},{160,192},{192,160},{224,1... | collective-permute-start | bytes 159752 | tf_op jit(solution)/shard_map/ppermute | solution.py:128
  37.6 1.9 %collective-permute-start.3 = (bf16[16,1664]{1,0:T(8,128)(2,1)S(1)}, bf16[16,1664]{1,0:T(8,128)(2,1)S(1)}, u32[]{:S(2)}, u32[]{:S(2)}) collective-permute-start(bf16[16,1664]{1,0:T(8,128)(2,1)S(1)} %pad_maximum_fusion), channel_id=1, source_target_pairs={{0,64},{32,96},{64,0},{96,32},{128,192},{160,224},{192,128},{224,1... | collective-permute-start | bytes 159752 | tf_op jit(solution)/shard_map/ppermute | solution.py:128
  39.6 3.0 %collective-permute-start.2 = (bf16[16,1664]{1,0:T(8,128)(2,1)S(1)}, bf16[16,1664]{1,0:T(8,128)(2,1)S(1)}, u32[]{:S(2)}, u32[]{:S(2)}) collective-permute-start(bf16[16,1664]{1,0:T(8,128)(2,1)S(1)} %pad_maximum_fusion), channel_id=1, source_target_pairs={{0,32},{32,0},{64,96},{96,64},{128,160},{160,128},{192,224},{224,1... | collective-permute-start | bytes 159752 | tf_op jit(solution)/shard_map/ppermute | solution.py:128
  43.9 0.6 collective-permute-done.3
  44.6 1.0 %collective-permute-done.2 = bf16[16,1664]{1,0:T(8,128)(2,1)S(1)} collective-permute-done((bf16[16,1664]{1,0:T(8,128)(2,1)S(1)}, bf16[16,1664]{1,0:T(8,128)(2,1)S(1)}, u32[]{:S(2)}, u32[]{:S(2)}) %collective-permute-start.2) | collective-permute-done | bytes 53280 | tf_op jit(solution)/shard_map/ppermute | solution.py:128
  45.6 0.3 convolution_convert_fusion
  45.9 0.2 fusion.53
  46.1 1.9 %collective-permute-start.7 = (bf16[128,1664]{1,0:T(8,128)(2,1)S(1)}, bf16[128,1664]{1,0:T(8,128)(2,1)S(1)}, u32[]{:S(2)}, u32[]{:S(2)}) collective-permute-start(bf16[128,1664]{1,0:T(8,128)(2,1)S(1)} %bitcast.11), channel_id=1, source_target_pairs={{0,1},{1,0},{2,3},{3,2},{4,5},{5,4},{6,7},{7,6},{8,9},{9,8},{10,11... | collective-permute-start | bytes 1277960 | tf_op jit(solution)/shard_map/ppermute | solution.py:201
  48.0 0.2 fusion.18
  48.2 0.3 fusion.1
  48.5 0.2 fusion.5
  48.7 1.0 %collective-permute-done.7 = bf16[128,1664]{1,0:T(8,128)(2,1)S(1)} collective-permute-done((bf16[128,1664]{1,0:T(8,128)(2,1)S(1)}, bf16[128,1664]{1,0:T(8,128)(2,1)S(1)}, u32[]{:S(2)}, u32[]{:S(2)}) %collective-permute-start.7) | collective-permute-done | bytes 426016 | tf_op jit(solution)/shard_map/ppermute | solution.py:201
  49.8 0.2 fusion.17
  50.0 0.4 fusion.50
  50.4 0.1 select_convert_fusion
  50.5 0.3 fusion
  50.7 0.1 maximum_bitcast_fusion
  50.8 13.6 %all_to_all.10 = f16[8,8,1664]{2,1,0:T(8,128)(2,1)S(1)} all-to-all(f16[8,8,1664]{2,1,0:T(8,128)(2,1)S(1)} %maximum_bitcast_fusion), channel_id=1, replica_groups={{0,32,64,96,128,160,192,224},{225,193,161,129,97,65,33,1},{2,34,66,98,1..., dimensions={0} | all-to-all | bytes 425984 | tf_op jit(solution)/shard_map/all_to_all | solution.py:119
  64.4 0.8 %shard_map.89 = (f32[1,8,1536]{2,1,0:T(8,128)}, f32[1,8]{1,0:T(1,128)}) custom-call(f32[1]{0:T(128)S(6)} %copy.17.scale_ref, f32[8,1664]{1,0:T(8,128)S(1)} %convert_reduce_fusion.total_ref, f32[8,1536]{1,0:T(8,128)S(1)} %get-tuple-element.36.embedding_ref), custom_call_target="tpu_custom_call" | custom-call | tf_op jit(solution)/shard_map/pallas_call | solution.py:257
  (23 shorter events, 0.2 us)
Async XLA Ops:
  0.6 4.0 %copy-start = (s32[16]{0:T(128)S(1)}, s32[16]{0:T(128)}, u32[]{:S(2)}) copy-start(s32[16]{0:T(128)} %param.13) | copy-start | bytes 196
  2.6 3.1 %collective-permute-start = (f32[8,1536]{1,0:T(8,128)S(1)}, f32[8,1536]{1,0:T(8,128)S(1)}, u32[]{:S(2)}, u32[]{:S(2)}) collective-permute-start(f32[8,1536]{1,0:T(8,128)S(1)} %get-tuple-element.26), channel_id=1, source_target_pairs={{0,1},{1,0},{2,3},{3,2},{4,5},{5,4},{6,7},{7,6},{8,9},{9,8},{10,11... | collective-permute-start | bytes 147464 | tf_op jit(solution)/shard_map/ppermute | solution.py:182
  6.0 18.1 %collective-permute-start.6 = (bf16[8,1664]{1,0:T(8,128)(2,1)S(1)}, bf16[8,1664]{1,0:T(8,128)(2,1)S(1)}, u32[]{:S(2)}, u32[]{:S(2)}) collective-permute-start(bf16[8,1664]{1,0:T(8,128)(2,1)S(1)} %pad_maximum_fusion.2), channel_id=1, source_target_pairs={{0,272},{272,0},{16,256},{256,16},{1,273},{273,1},{17,257},{257,17... | collective-permute-start | bytes 79880 | tf_op jit(solution)/shard_map/ppermute | solution.py:195
  9.5 14.6 %collective-permute-start.5 = (bf16[8,1664]{1,0:T(8,128)(2,1)S(1)}, bf16[8,1664]{1,0:T(8,128)(2,1)S(1)}, u32[]{:S(2)}, u32[]{:S(2)}) collective-permute-start(bf16[8,1664]{1,0:T(8,128)(2,1)S(1)} %pad_maximum_fusion.2), channel_id=1, source_target_pairs={{0,256},{256,0},{1,257},{257,1},{2,258},{258,2},{3,259},{259,3},{4... | collective-permute-start | bytes 79880 | tf_op jit(solution)/shard_map/ppermute | solution.py:194
  13.1 19.3 %collective-permute-start.1 = (bf16[8,1664]{1,0:T(8,128)(2,1)S(1)}, bf16[8,1664]{1,0:T(8,128)(2,1)S(1)}, u32[]{:S(2)}, u32[]{:S(2)}) collective-permute-start(bf16[8,1664]{1,0:T(8,128)(2,1)S(1)} %pad_maximum_fusion.2), channel_id=1, source_target_pairs={{0,128},{32,160},{64,192},{96,224},{128,0},{160,32},{192,64},{224,... | collective-permute-start | bytes 79880 | tf_op jit(solution)/shard_map/ppermute | solution.py:128
  24.9 21.2 %all-to-all-start = ((bf16[8,16,1664]{2,1,0:T(8,128)(2,1)}), bf16[8,16,1664]{2,1,0:T(8,128)(2,1)S(1)}, u32[]{:S(2)}, u32[]{:S(2)}) async-start(bf16[8,16,1664]{2,1,0:T(8,128)(2,1)} %broadcast_in_dim.54), calls=%async_computation | async-start | bytes 851968 | tf_op jit(solution)/shard_map/all_to_all | solution.py:119
  32.4 11.5 %collective-permute-start.4 = (bf16[16,1664]{1,0:T(8,128)(2,1)S(1)}, bf16[16,1664]{1,0:T(8,128)(2,1)S(1)}, u32[]{:S(2)}, u32[]{:S(2)}) collective-permute-start(bf16[16,1664]{1,0:T(8,128)(2,1)S(1)} %pad_maximum_fusion), channel_id=1, source_target_pairs={{0,96},{32,64},{64,32},{96,0},{128,224},{160,192},{192,160},{224,1... | collective-permute-start | bytes 159752 | tf_op jit(solution)/shard_map/ppermute | solution.py:128
  37.6 6.9 %collective-permute-start.3 = (bf16[16,1664]{1,0:T(8,128)(2,1)S(1)}, bf16[16,1664]{1,0:T(8,128)(2,1)S(1)}, u32[]{:S(2)}, u32[]{:S(2)}) collective-permute-start(bf16[16,1664]{1,0:T(8,128)(2,1)S(1)} %pad_maximum_fusion), channel_id=1, source_target_pairs={{0,64},{32,96},{64,0},{96,32},{128,192},{160,224},{192,128},{224,1... | collective-permute-start | bytes 159752 | tf_op jit(solution)/shard_map/ppermute | solution.py:128
  39.6 6.0 %collective-permute-start.2 = (bf16[16,1664]{1,0:T(8,128)(2,1)S(1)}, bf16[16,1664]{1,0:T(8,128)(2,1)S(1)}, u32[]{:S(2)}, u32[]{:S(2)}) collective-permute-start(bf16[16,1664]{1,0:T(8,128)(2,1)S(1)} %pad_maximum_fusion), channel_id=1, source_target_pairs={{0,32},{32,0},{64,96},{96,64},{128,160},{160,128},{192,224},{224,1... | collective-permute-start | bytes 159752 | tf_op jit(solution)/shard_map/ppermute | solution.py:128
  46.1 3.7 %collective-permute-start.7 = (bf16[128,1664]{1,0:T(8,128)(2,1)S(1)}, bf16[128,1664]{1,0:T(8,128)(2,1)S(1)}, u32[]{:S(2)}, u32[]{:S(2)}) collective-permute-start(bf16[128,1664]{1,0:T(8,128)(2,1)S(1)} %bitcast.11), channel_id=1, source_target_pairs={{0,1},{1,0},{2,3},{3,2},{4,5},{5,4},{6,7},{7,6},{8,9},{9,8},{10,11... | collective-permute-start | bytes 1277960 | tf_op jit(solution)/shard_map/ppermute | solution.py:201

commit v4 on v3

--- a/solution.py
+++ b/solution.py
@@ -9,7 +9,8 @@
 EPS = 1e-06
 PIECE = 256
 LANES = 128
-BASE = 16
+HIGH, LOW = 64, 32
+SUMS = 3
 
 
 def project(pooled, weights, copies, core_ref, keep_ref, send_ref):
@@ -109,34 +110,42 @@
     )(core_index, *given)
 
 
-def mirrored(blocks, axis):
+def staggered(blocks, axis):
     members = lax.axis_size(axis)
     cores = lax.axis_size("mp")
     groups = [
-        [at * cores + core for at in (range(members) if core == 0 else reversed(range(members)))]
+        [(at ^ (core * (members // 2))) * cores + core for at in range(members)]
         for core in range(cores)
     ]
     return lax.all_to_all(blocks, (axis, "mp"), 0, 0, axis_index_groups=groups, tiled=True)
 
 
-def swap_gather(block, axis, after):
+def swap_gather(block, axis):
     members = lax.axis_size(axis)
     half = members // 2
-    size = block.shape[0]
 
     def brought(value, across):
         return lax.ppermute(value, axis, [(index, index ^ across) for index in range(members)])
 
     pair = jnp.concatenate([block, brought(block, half)], axis=0)
-    pair, _ = lax.optimization_barrier((pair, after))
-    held = jnp.concatenate([pair] + [brought(pair, across) for across in range(1, half)], axis=0)
+    wide = pair.astype(jnp.float32)
+    passed = jnp.sum(wide, axis=0, keepdims=True)
+    for _ in range(SUMS - 1):
+        passed = jnp.sum(wide * passed, axis=0, keepdims=True)
+    pair = pair + (passed * 0).astype(pair.dtype)
+    return jnp.concatenate([pair] + [brought(pair, across) for across in range(1, half)], axis=0)
+
+
+def in_order(held, axis, size, last):
+    members = lax.axis_size(axis)
     place = lax.broadcasted_iota(jnp.int32, (members * size, members * size), 0)
     slot = lax.broadcasted_iota(jnp.int32, (members * size, members * size), 1)
     number = slot // size
-    came_from = lax.axis_index(axis) ^ (number // 2 + (number % 2) * half)
-    member = jnp.where(lax.axis_index("mp") == 0, place // size, members - 1 - place // size)
+    came_from = lax.axis_index(axis) ^ (number // 2 + (number % 2) * (members // 2))
+    member = (place // size) ^ (lax.axis_index("mp") * (members // 2))
     moves = (member == came_from) & (place % size == slot % size)
-    ordered = jnp.dot(moves.astype(held.dtype), held, preferred_element_type=jnp.float32)
+    moves = moves.astype(held.dtype) + last[: members * size, : members * size] * 0
+    ordered = jnp.dot(moves, held, preferred_element_type=jnp.float32)
     return ordered.astype(held.dtype)
 
 
@@ -173,6 +182,9 @@
     share = row_count // n_mp
     width = image_proj.shape[1]
 
+    def pair_at(z_at, x_at, y_at):
+        return ((z_at * n_x + x_at) * n_y + y_at) * row_count
+
     core_index = core.astype(jnp.int32).reshape(1)
     kept, sent = lax.cond(
         tower == 0,
@@ -184,64 +196,43 @@
     unit = embedding * inverse
     unit_low = unit.astype(jnp.bfloat16)
 
-    key = lax.dynamic_slice_in_dim(partner, core * share, share, 0)
-    key_high = (key // BASE).astype(jnp.bfloat16)[:, None]
-    key_low = (key % BASE).astype(jnp.bfloat16)[:, None]
+    first = pair_at(lax.axis_index("z"), lax.axis_index("x"), lax.axis_index("y")) + core * share
+    partners = lax.dynamic_slice_in_dim(partner, core * share, share, 0)
+    key = jnp.where(tower == 0, partners, first + lax.iota(jnp.int32, share))[:, None]
     column = lax.broadcasted_iota(jnp.int32, (share, LANES), 1)
-    key_block = jnp.where(column == 0, key_high, jnp.where(column == 1, key_low, 0))
+    coded = (column == key // LOW) | (column == HIGH + key % LOW)
+    key_block = coded.astype(jnp.bfloat16)
     own = jnp.concatenate([unit_low, key_block], axis=1)
 
     near = lax.ppermute(own, "tower", [(0, 1), (1, 0)])
     across = lax.ppermute(own, ("tower", "x"), [(0, 3), (3, 0), (1, 2), (2, 1)])
     other = jnp.concatenate([near, across], axis=0)
     copies = jnp.broadcast_to(other[None], (n_y,) + other.shape)
-    own_all = swap_gather(own, "z", other[:1, :LANES])
-    other_mine = mirrored(copies, "y")
+    held = swap_gather(own, "z")
+    other_mine = staggered(copies, "y")
     other_mine = other_mine.reshape(n_y * n_x * share, width + LANES)
     other_theirs = lax.ppermute(other_mine, "mp", [(0, 1), (1, 0)])
-
-    def sent_key(gathered):
-        pair = gathered[:, width : width + 2].astype(jnp.int32)
-        return pair[:, 0] * BASE + pair[:, 1]
-
-    z = lax.axis_index("z")
-    y = lax.axis_index("y")
-    x = lax.axis_index("x")
-
-    def pair_at(z_at, x_at, y_at):
-        return ((z_at * n_x + x_at) * n_y + y_at) * row_count
-
-    own_slot = lax.iota(jnp.int32, n_z * share)
-    own_z = jnp.where(core == 0, own_slot // share, n_z - 1 - own_slot // share)
-    own_place = pair_at(own_z, x, y) + core * share + own_slot % share
-    other_slot = lax.iota(jnp.int32, n_y * n_x * share)
-    other_x = x ^ (other_slot // share % n_x)
-    other_y = other_slot // (n_x * share)
-    other_reversed = n_y - 1 - other_y
-    own_key = jnp.where(tower == 0, sent_key(own_all), own_place)
+    own_all = in_order(held, "z", share, other_mine)
+
     temper = jnp.exp(log_scale[0])
     own_low = own_all[:, :width]
 
-    def score(others, other_core):
-        other_at = jnp.where(other_core == 0, other_y, other_reversed)
-        other_place = pair_at(z, other_x, other_at) + other_core * share + other_slot % share
-        other_key = jnp.where(tower == 0, other_place, sent_key(others))
+    def products(rows, columns):
+        return lax.dot_general(
+            rows, columns, (((1,), (1,)), ((), ())), preferred_element_type=jnp.float32
+        )
+
+    def score(others):
         other_low = others[:, :width]
-        logits = (
-            temper
-            * lax.dot_general(
-                own_low, other_low, (((1,), (1,)), ((), ())), preferred_element_type=jnp.float32
-            )
-            + bias[0]
-        )
-        paired = own_key[:, None] == other_key[None, :]
+        logits = temper * products(own_low, other_low) + bias[0]
+        paired = products(own_all[:, width:], others[:, width:]) > 1.5
         losses = jax.nn.softplus(jnp.where(paired, -logits, logits))
         weights = (jax.nn.sigmoid(logits) - paired.astype(jnp.float32)).astype(jnp.bfloat16)
         grad = jnp.dot(weights, other_low, preferred_element_type=jnp.float32)
         return grad, jnp.sum(losses, axis=1, keepdims=True)
 
-    grad_mine, loss_mine = score(other_mine, core)
-    grad_theirs, loss_theirs = score(other_theirs, 1 - core)
+    grad_mine, loss_mine = score(other_mine)
+    grad_theirs, loss_theirs = score(other_theirs)
     grad_part = grad_mine + grad_theirs
     loss_part = loss_mine + loss_theirs
 
@@ -250,7 +241,7 @@
     lane = lax.broadcasted_iota(jnp.int32, (n_z * share, LANES), 1)
     loss_block = jnp.where(lane == 0, loss_high, loss_rest).astype(jnp.float16)
     sums = jnp.concatenate([grad_part.astype(jnp.float16), loss_block], axis=1)
-    sums = mirrored(sums.reshape(n_z, share, width + LANES), "z")
+    sums = staggered(sums.reshape(n_z, share, width + LANES), "z")
     total = jnp.sum(sums.astype(jnp.float32), axis=0)
     vmem = pl.BlockSpec(memory_space=pltpu.VMEM)
     any_space = pl.BlockSpec(memory_space=pl.ANY)

time: 65.8 us -> 63.9 us (0.971)
  the two profiles are of different devices: /device:TPU:10 before, /device:TPU:1 now
where the time goes in v4:
time: 63.9 us; the launch traced here: 62.7 us
  starting transfers between devices  41 us (64%)
  blocking collectives  12.3 us (19%)
  Pallas kernels  2.89 us (5%)
  between operations  2.26 us (4%)
  matrix products  1.75 us (3%)
  waiting for transfers between devices  0.96 us (2%)
  local copies, waits for them, and re-layouts  0.79 us (1%)
  other arithmetic  0.71 us (1%)
    ppermute x4, starting transfers between devices, brought(): lax.ppermute(value, axis, [(index, index ^ across) for index in range(mem...  16.9 us
    all_to_all x1, blocking collectives, staggered(): lax.all_to_all(blocks, (axis, 'mp'), 0, 0, axis_index_groups=groups, tile...  12.3 us
    all_to_all x1, starting transfers between devices, staggered(): lax.all_to_all(blocks, (axis, 'mp'), 0, 0, axis_index_groups=groups, tile...  8.93 us
    ppermute x1, starting transfers between devices, shards(): embedding = kept + lax.ppermute(sent, 'mp', [(0, 1), (1, 0)])  8.79 us
    ppermute x1, starting transfers between devices, shards(): other_theirs = lax.ppermute(other_mine, 'mp', [(0, 1), (1, 0)])  2.56 us
    pallas_call x1, Pallas kernels, pooled_partial(): pl.pallas_call(kernel, out_shape=(half, half), in_specs=[pl.BlockSpec(mem...  2.05 us
    ppermute x1, starting transfers between devices, shards(): near = lax.ppermute(own, 'tower', [(0, 1), (1, 0)])  1.92 us
    ppermute x1, starting transfers between devices, shards(): across = lax.ppermute(own, ('tower', 'x'), [(0, 3), (3, 0), (1, 2), (2, 1)])  1.92 us
  transfers between devices with their start and end apart: 9, of which 2 were waited for; matrix products, arithmetic and copies ran while one was open for 3% of the time, Pallas kernels for 0%

profile of v4, /device:TPU:1, one launch (start us, length us, event | category | flops | bytes accessed | tf_op | source)
XLA Modules:
  0.0 62.7 jit_solution(197792876492997089)
XLA Ops:
  0.6 2.1 %conditional.1 = ((f32[8,1536]{1,0:T(8,128)S(1)}, f32[8,1536]{1,0:T(8,128)S(1)})) conditional(s32[]{:T(128)} %convert_element_type.48, (s32[1]{0:T(128)}, s32[16]{0:T(128)}, bf16[16,18432]{1,0:T(8,128)(2,1)}, bf16[576,1536]{1,0:T(8,128)(2,1)}) %tuple.27, (s32[1]{0:T(128)}, bf16[16,18432]{1,0:T(8,128)(2,1)}, bf16[768,1536]{1,0:T(8,128)(2,1)}) %tuple.28), branch_computations={%region_0.0_spmd, %region_1.0_spmd} | conditional | bytes 8 | solution.py:189
  0.7 2.1 %branch_1_fun.1 = (f32[8,1536]{1,0:T(8,128)S(1)}, f32[8,1536]{1,0:T(8,128)S(1)}) custom-call(s32[1]{0:T(128)} %get-tuple-element.18.core_ref, bf16[16,18432]{1,0:T(8,128)(2,1)} %get-tuple-element.19.slices_hbm, bf16[768,1536]{1,0:T(8,128)(2,1)} %get-tuple-element.32.weights_hbm), custom_call_target="tpu_custom_call" | custom-call | tf_op jit(solution)/shard_map/cond/branch_1_fun/pallas_call | solution.py:103
  2.7 8.8 %collective-permute-start = (f32[8,1536]{1,0:T(8,128)S(1)}, f32[8,1536]{1,0:T(8,128)S(1)}, u32[]{:S(2)}, u32[]{:S(2)}) collective-permute-start(f32[8,1536]{1,0:T(8,128)S(1)} %get-tuple-element.26), channel_id=1, source_target_pairs={{0,1},{1,0},{2,3},{3,2},{4,5},{5,4},{6,7},{7,6},{8,9},{9,8},{10,11... | collective-permute-start | bytes 147464 | tf_op jit(solution)/shard_map/ppermute | solution.py:194
  11.6 0.1 and_select_fusion.1
  11.7 0.1 fusion.70
  11.7 0.6 %collective-permute-done = f32[8,1536]{1,0:T(8,128)S(1)} collective-permute-done((f32[8,1536]{1,0:T(8,128)S(1)}, f32[8,1536]{1,0:T(8,128)S(1)}, u32[]{:S(2)}, u32[]{:S(2)}) %collective-permute-start) | collective-permute-done | bytes 49184 | tf_op jit(solution)/shard_map/ppermute | solution.py:194
  12.4 0.1 multiply_reduce_fusion
  12.5 0.1 multiply_convert_fusion
  12.6 1.9 %collective-permute-start.2 = (bf16[8,1664]{1,0:T(8,128)(2,1)S(1)}, bf16[8,1664]{1,0:T(8,128)(2,1)S(1)}, u32[]{:S(2)}, u32[]{:S(2)}) collective-permute-start(bf16[8,1664]{1,0:T(8,128)(2,1)S(1)} %pad_maximum_fusion.2), channel_id=1, source_target_pairs={{0,272},{272,0},{16,256},{256,16},{1,273},{273,1},{17,257},{257,17... | collective-permute-start | bytes 79880 | tf_op jit(solution)/shard_map/ppermute | solution.py:208
  14.5 1.9 %collective-permute-start.1 = (bf16[8,1664]{1,0:T(8,128)(2,1)S(1)}, bf16[8,1664]{1,0:T(8,128)(2,1)S(1)}, u32[]{:S(2)}, u32[]{:S(2)}) collective-permute-start(bf16[8,1664]{1,0:T(8,128)(2,1)S(1)} %pad_maximum_fusion.2), channel_id=1, source_target_pairs={{0,256},{256,0},{1,257},{257,1},{2,258},{258,2},{3,259},{259,3},{4... | collective-permute-start | bytes 79880 | tf_op jit(solution)/shard_map/ppermute | solution.py:207
  16.5 7.7 %collective-permute-start.3 = (bf16[8,1664]{1,0:T(8,128)(2,1)S(1)}, bf16[8,1664]{1,0:T(8,128)(2,1)S(1)}, u32[]{:S(2)}, u32[]{:S(2)}) collective-permute-start(bf16[8,1664]{1,0:T(8,128)(2,1)S(1)} %pad_maximum_fusion.2), channel_id=1, source_target_pairs={{0,128},{32,160},{64,192},{96,224},{128,0},{160,32},{192,64},{224,... | collective-permute-start | bytes 79880 | tf_op jit(solution)/shard_map/ppermute | solution.py:128
  24.1 0.0 collective-permute-done.2
  24.1 0.0 collective-permute-done.1
  24.2 0.8 %broadcast_in_dim.12 = bf16[8,16,1664]{2,1,0:T(8,128)(2,1)} broadcast(bf16[16,1664]{1,0:T(8,128)(2,1)S(1)} %pad_maximum_fusion), dimensions={1,2} | broadcast | bytes 479232 | tf_op jit(solution)/shard_map/broadcast_in_dim | solution.py:210
  25.0 8.9 %all-to-all-start = ((bf16[8,16,1664]{2,1,0:T(8,128)(2,1)}), bf16[8,16,1664]{2,1,0:T(8,128)(2,1)S(1)}, u32[]{:S(2)}, u32[]{:S(2)}) async-start(bf16[8,16,1664]{2,1,0:T(8,128)(2,1)} %broadcast_in_dim.12), calls=%async_computation | async-start | bytes 851968 | tf_op jit(solution)/shard_map/all_to_all | solution.py:120
  34.0 4.9 %collective-permute-start.6 = (bf16[16,1664]{1,0:T(8,128)(2,1)S(1)}, bf16[16,1664]{1,0:T(8,128)(2,1)S(1)}, u32[]{:S(2)}, u32[]{:S(2)}) collective-permute-start(bf16[16,1664]{1,0:T(8,128)(2,1)S(1)} %broadcast_add_fusion), channel_id=1, source_target_pairs={{0,96},{32,64},{64,32},{96,0},{128,224},{160,192},{192,160},{224,1... | collective-permute-start | bytes 159752 | tf_op jit(solution)/shard_map/ppermute | solution.py:128
  39.0 1.9 %collective-permute-start.5 = (bf16[16,1664]{1,0:T(8,128)(2,1)S(1)}, bf16[16,1664]{1,0:T(8,128)(2,1)S(1)}, u32[]{:S(2)}, u32[]{:S(2)}) collective-permute-start(bf16[16,1664]{1,0:T(8,128)(2,1)S(1)} %broadcast_add_fusion), channel_id=1, source_target_pairs={{0,64},{32,96},{64,0},{96,32},{128,192},{160,224},{192,128},{224,1... | collective-permute-start | bytes 159752 | tf_op jit(solution)/shard_map/ppermute | solution.py:128
  40.9 2.4 %collective-permute-start.4 = (bf16[16,1664]{1,0:T(8,128)(2,1)S(1)}, bf16[16,1664]{1,0:T(8,128)(2,1)S(1)}, u32[]{:S(2)}, u32[]{:S(2)}) collective-permute-start(bf16[16,1664]{1,0:T(8,128)(2,1)S(1)} %broadcast_add_fusion), channel_id=1, source_target_pairs={{0,32},{32,0},{64,96},{96,64},{128,160},{160,128},{192,224},{224,1... | collective-permute-start | bytes 159752 | tf_op jit(solution)/shard_map/ppermute | solution.py:128
  44.7 0.0 all-to-all-done
  44.7 2.6 %collective-permute-start.7 = (bf16[128,1664]{1,0:T(8,128)(2,1)S(1)}, bf16[128,1664]{1,0:T(8,128)(2,1)S(1)}, u32[]{:S(2)}, u32[]{:S(2)}) collective-permute-start(bf16[128,1664]{1,0:T(8,128)(2,1)S(1)} %bitcast.11), channel_id=1, source_target_pairs={{0,1},{1,0},{2,3},{3,2},{4,5},{5,4},{6,7},{7,6},{8,9},{9,8},{10,11... | collective-permute-start | bytes 1277960 | tf_op jit(solution)/shard_map/ppermute | solution.py:214
  47.3 0.3 convolution_convert_fusion
  47.6 0.3 fusion.1
  47.8 0.3 fusion.32
  48.1 0.2 fusion.5
  48.3 0.3 collective-permute-done.7
  48.6 0.3 fusion.2
  48.9 0.3 fusion.33
  49.2 0.1 select_convert_fusion
  49.3 0.2 fusion
  49.5 0.1 maximum_bitcast_fusion
  49.6 12.3 %all_to_all.10 = f16[8,8,1664]{2,1,0:T(8,128)(2,1)S(1)} all-to-all(f16[8,8,1664]{2,1,0:T(8,128)(2,1)S(1)} %maximum_bitcast_fusion), channel_id=1, replica_groups={{0,32,64,96,128,160,192,224},{129,161,193,225,1,33,65,97},{2,34,66,98,1..., dimensions={0} | all-to-all | bytes 425984 | tf_op jit(solution)/shard_map/all_to_all | solution.py:120
  61.9 0.8 %shard_map.89 = (f32[1,8,1536]{2,1,0:T(8,128)}, f32[1,8]{1,0:T(1,128)}) custom-call(f32[1]{0:T(128)S(6)} %copy.18.scale_ref, f32[8,1664]{1,0:T(8,128)S(1)} %convert_reduce_fusion.total_ref, f32[8,1536]{1,0:T(8,128)S(1)} %get-tuple-element.34.embedding_ref), custom_call_target="tpu_custom_call" | custom-call | tf_op jit(solution)/shard_map/pallas_call | solution.py:248
  (21 shorter events, 0.2 us)
Async XLA Ops:
  0.6 10.9 %copy-start = (s32[16]{0:T(128)S(1)}, s32[16]{0:T(128)}, u32[]{:S(2)}) copy-start(s32[16]{0:T(128)} %param.13) | copy-start | bytes 196
  2.7 9.7 %collective-permute-start = (f32[8,1536]{1,0:T(8,128)S(1)}, f32[8,1536]{1,0:T(8,128)S(1)}, u32[]{:S(2)}, u32[]{:S(2)}) collective-permute-start(f32[8,1536]{1,0:T(8,128)S(1)} %get-tuple-element.26), channel_id=1, source_target_pairs={{0,1},{1,0},{2,3},{3,2},{4,5},{5,4},{6,7},{7,6},{8,9},{9,8},{10,11... | collective-permute-start | bytes 147464 | tf_op jit(solution)/shard_map/ppermute | solution.py:194
  12.6 11.5 %collective-permute-start.2 = (bf16[8,1664]{1,0:T(8,128)(2,1)S(1)}, bf16[8,1664]{1,0:T(8,128)(2,1)S(1)}, u32[]{:S(2)}, u32[]{:S(2)}) collective-permute-start(bf16[8,1664]{1,0:T(8,128)(2,1)S(1)} %pad_maximum_fusion.2), channel_id=1, source_target_pairs={{0,272},{272,0},{16,256},{256,16},{1,273},{273,1},{17,257},{257,17... | collective-permute-start | bytes 79880 | tf_op jit(solution)/shard_map/ppermute | solution.py:208
  14.5 9.6 %collective-permute-start.1 = (bf16[8,1664]{1,0:T(8,128)(2,1)S(1)}, bf16[8,1664]{1,0:T(8,128)(2,1)S(1)}, u32[]{:S(2)}, u32[]{:S(2)}) collective-permute-start(bf16[8,1664]{1,0:T(8,128)(2,1)S(1)} %pad_maximum_fusion.2), channel_id=1, source_target_pairs={{0,256},{256,0},{1,257},{257,1},{2,258},{258,2},{3,259},{259,3},{4... | collective-permute-start | bytes 79880 | tf_op jit(solution)/shard_map/ppermute | solution.py:207
  16.5 17.4 %collective-permute-start.3 = (bf16[8,1664]{1,0:T(8,128)(2,1)S(1)}, bf16[8,1664]{1,0:T(8,128)(2,1)S(1)}, u32[]{:S(2)}, u32[]{:S(2)}) collective-permute-start(bf16[8,1664]{1,0:T(8,128)(2,1)S(1)} %pad_maximum_fusion.2), channel_id=1, source_target_pairs={{0,128},{32,160},{64,192},{96,224},{128,0},{160,32},{192,64},{224,... | collective-permute-start | bytes 79880 | tf_op jit(solution)/shard_map/ppermute | solution.py:128
  25.0 19.7 %all-to-all-start = ((bf16[8,16,1664]{2,1,0:T(8,128)(2,1)}), bf16[8,16,1664]{2,1,0:T(8,128)(2,1)S(1)}, u32[]{:S(2)}, u32[]{:S(2)}) async-start(bf16[8,16,1664]{2,1,0:T(8,128)(2,1)} %broadcast_in_dim.12), calls=%async_computation | async-start | bytes 851968 | tf_op jit(solution)/shard_map/all_to_all | solution.py:120
  34.0 13.2 %collective-permute-start.6 = (bf16[16,1664]{1,0:T(8,128)(2,1)S(1)}, bf16[16,1664]{1,0:T(8,128)(2,1)S(1)}, u32[]{:S(2)}, u32[]{:S(2)}) collective-permute-start(bf16[16,1664]{1,0:T(8,128)(2,1)S(1)} %broadcast_add_fusion), channel_id=1, source_target_pairs={{0,96},{32,64},{64,32},{96,0},{128,224},{160,192},{192,160},{224,1... | collective-permute-start | bytes 159752 | tf_op jit(solution)/shard_map/ppermute | solution.py:128
  39.0 8.3 %collective-permute-start.5 = (bf16[16,1664]{1,0:T(8,128)(2,1)S(1)}, bf16[16,1664]{1,0:T(8,128)(2,1)S(1)}, u32[]{:S(2)}, u32[]{:S(2)}) collective-permute-start(bf16[16,1664]{1,0:T(8,128)(2,1)S(1)} %broadcast_add_fusion), channel_id=1, source_target_pairs={{0,64},{32,96},{64,0},{96,32},{128,192},{160,224},{192,128},{224,1... | collective-permute-start | bytes 159752 | tf_op jit(solution)/shard_map/ppermute | solution.py:128
  40.9 6.4 %collective-permute-start.4 = (bf16[16,1664]{1,0:T(8,128)(2,1)S(1)}, bf16[16,1664]{1,0:T(8,128)(2,1)S(1)}, u32[]{:S(2)}, u32[]{:S(2)}) collective-permute-start(bf16[16,1664]{1,0:T(8,128)(2,1)S(1)} %broadcast_add_fusion), channel_id=1, source_target_pairs={{0,32},{32,0},{64,96},{96,64},{128,160},{160,128},{192,224},{224,1... | collective-permute-start | bytes 159752 | tf_op jit(solution)/shard_map/ppermute | solution.py:128
  44.7 3.9 %collective-permute-start.7 = (bf16[128,1664]{1,0:T(8,128)(2,1)S(1)}, bf16[128,1664]{1,0:T(8,128)(2,1)S(1)}, u32[]{:S(2)}, u32[]{:S(2)}) collective-permute-start(bf16[128,1664]{1,0:T(8,128)(2,1)S(1)} %bitcast.11), channel_id=1, source_target_pairs={{0,1},{1,0},{2,3},{3,2},{4,5},{5,4},{6,7},{7,6},{8,9},{9,8},{10,11... | collective-permute-start | bytes 1277960 | tf_op jit(solution)/shard_map/ppermute | solution.py:214

commit v5 on v4

--- a/solution.py
+++ b/solution.py
@@ -8,6 +8,7 @@
 
 EPS = 1e-06
 PIECE = 256
+QUARTERS = 4
 LANES = 128
 HIGH, LOW = 64, 32
 SUMS = 3
@@ -15,8 +16,12 @@
 
 def project(pooled, weights, copies, core_ref, keep_ref, send_ref):
     total = None
-    for copy, first, last in copies:
-        copy.wait()
+    depth = weights.shape[0]
+    for first in range(0, depth, PIECE):
+        last = min(first + PIECE, depth)
+        for copy, start in copies:
+            if first <= start < last:
+                copy.wait()
         piece = jnp.dot(
             pooled[:, first:last], weights[first:last, :], preferred_element_type=jnp.float32
         )
@@ -30,26 +35,33 @@
 
 def fetch(slices_hbm, weights_hbm, slices, weights, sems):
     depth = weights_hbm.shape[0]
-    first_copy = pltpu.make_async_copy(slices_hbm, slices, sems.at[0])
-    first_copy.start()
+    quarter = slices.shape[1] // QUARTERS
+    quarters = []
+    for place in range(QUARTERS):
+        columns = pl.ds(place * quarter, quarter)
+        quarters.append(
+            pltpu.make_async_copy(slices_hbm.at[:, columns], slices.at[:, columns], sems.at[place])
+        )
+        quarters[-1].start()
     copies = []
-    for place, first in enumerate(range(0, depth, PIECE)):
-        last = min(first + PIECE, depth)
+    for place, first in enumerate(range(0, depth, LANES)):
+        rows = pl.ds(first, min(LANES, depth - first))
         copy = pltpu.make_async_copy(
-            weights_hbm.at[first:last], weights.at[first:last], sems.at[1 + place]
+            weights_hbm.at[rows], weights.at[rows], sems.at[QUARTERS + place]
         )
         copy.start()
-        copies.append((copy, first, min(first + PIECE, weights.shape[0])))
-    return first_copy, copies
+        copies.append((copy, first))
+    return quarters, copies
 
 
 def image_kernel(core_ref, slices_hbm, weights_hbm, keep_ref, send_ref, slices, weights, sems):
-    first_copy, copies = fetch(slices_hbm, weights_hbm, slices, weights, sems)
+    quarters, copies = fetch(slices_hbm, weights_hbm, slices, weights, sems)
     width = weights_hbm.shape[0]
     patch_count = slices.shape[1] // width
-    first_copy.wait()
-    summed = slices[:, :width].astype(jnp.float32)
-    for patch in range(1, patch_count):
+    summed = jnp.zeros((slices.shape[0], width), jnp.float32)
+    for patch in range(patch_count):
+        if patch % (patch_count // QUARTERS) == 0:
+            quarters[patch // (patch_count // QUARTERS)].wait()
         summed += slices[:, patch * width : (patch + 1) * width].astype(jnp.float32)
     pooled = (summed / patch_count).astype(jnp.bfloat16)
     project(pooled, weights, copies, core_ref, keep_ref, send_ref)
@@ -60,7 +72,7 @@
 ):
     lengths_copy = pltpu.make_async_copy(lengths_hbm, lengths_ref, sems.at[sems.shape[0] - 1])
     lengths_copy.start()
-    first_copy, copies = fetch(slices_hbm, weights_hbm, slices, weights, sems)
+    quarters, copies = fetch(slices_hbm, weights_hbm, slices, weights, sems)
     width = weights_hbm.shape[0]
     row_count = slices.shape[0]
     slot_count = slices.shape[1] // width
@@ -75,9 +87,10 @@
         lengths = jnp.where(row == index, lengths_ref[index], lengths)
     second = (lax.broadcasted_iota(jnp.int32, shape, 1) >= width).astype(jnp.int32)
     left = lengths - second
-    first_copy.wait()
     summed = jnp.zeros(shape, jnp.float32)
     for slot in range(0, slot_count, 2):
+        if slot % (slot_count // QUARTERS) == 0:
+            quarters[slot // (slot_count // QUARTERS)].wait()
         piece = slices[:, slot * width : (slot + 2) * width].astype(jnp.float32)
         summed += jnp.where(slot < left, piece, 0.0)
     summed = summed + pltpu.roll(summed, width, 1)
@@ -89,14 +102,13 @@
     row_count = slices.shape[0]
     depth, width = weights.shape
     padded = -(-depth // LANES) * LANES
-    pieces = -(-depth // PIECE)
     any_space = pl.BlockSpec(memory_space=pl.ANY)
     half = jax.ShapeDtypeStruct((row_count // 2, width), jnp.float32)
     given = (slices, weights) if lengths is None else (lengths, slices, weights)
     scratch = [
         pltpu.VMEM(slices.shape, jnp.bfloat16),
         pltpu.VMEM((padded, width), jnp.bfloat16),
-        pltpu.SemaphoreType.DMA((2 + pieces,)),
+        pltpu.SemaphoreType.DMA((QUARTERS + padded // LANES + 1,)),
     ]
     if lengths is not None:
         scratch.append(pltpu.SMEM(lengths.shape, jnp.int32))

time: 63.9 us -> 64.1 us (level)
  no operation moved by 1% of the time
where the time goes in v5:
time: 64.1 us; the launch traced here: 62.9 us
  starting transfers between devices  41 us (64%)
  blocking collectives  12.3 us (19%)
  Pallas kernels  3.04 us (5%)
  between operations  2.26 us (4%)
  matrix products  1.75 us (3%)
  waiting for transfers between devices  0.97 us (2%)
  local copies, waits for them, and re-layouts  0.79 us (1%)
  other arithmetic  0.71 us (1%)
    ppermute x4, starting transfers between devices, brought(): lax.ppermute(value, axis, [(index, index ^ across) for index in range(mem...  16.9 us
    all_to_all x1, blocking collectives, staggered(): lax.all_to_all(blocks, (axis, 'mp'), 0, 0, axis_index_groups=groups, tile...  12.3 us
    all_to_all x1, starting transfers between devices, staggered(): lax.all_to_all(blocks, (axis, 'mp'), 0, 0, axis_index_groups=groups, tile...  8.93 us
    ppermute x1, starting transfers between devices, shards(): embedding = kept + lax.ppermute(sent, 'mp', [(0, 1), (1, 0)])  8.79 us
    ppermute x1, starting transfers between devices, shards(): other_theirs = lax.ppermute(other_mine, 'mp', [(0, 1), (1, 0)])  2.56 us
    pallas_call x1, Pallas kernels, pooled_partial(): pl.pallas_call(kernel, out_shape=(half, half), in_specs=[pl.BlockSpec(mem...  2.2 us
    ppermute x1, starting transfers between devices, shards(): near = lax.ppermute(own, 'tower', [(0, 1), (1, 0)])  1.92 us
    ppermute x1, starting transfers between devices, shards(): across = lax.ppermute(own, ('tower', 'x'), [(0, 3), (3, 0), (1, 2), (2, 1)])  1.92 us
  transfers between devices with their start and end apart: 9, of which 2 were waited for; matrix products, arithmetic and copies ran while one was open for 3% of the time, Pallas kernels for 0%

profile of v5, /device:TPU:1, one launch (start us, length us, event | category | flops | bytes accessed | tf_op | source)
XLA Modules:
  0.0 62.9 jit_solution(11534748091594441814)
XLA Ops:
  0.6 2.2 %conditional.1 = ((f32[8,1536]{1,0:T(8,128)S(1)}, f32[8,1536]{1,0:T(8,128)S(1)})) conditional(s32[]{:T(128)} %convert_element_type.48, (s32[1]{0:T(128)}, s32[16]{0:T(128)}, bf16[16,18432]{1,0:T(8,128)(2,1)}, bf16[576,1536]{1,0:T(8,128)(2,1)}) %tuple.27, (s32[1]{0:T(128)}, bf16[16,18432]{1,0:T(8,128)(2,1)}, bf16[768,1536]{1,0:T(8,128)(2,1)}) %tuple.28), branch_computations={%region_0.0_spmd, %region_1.0_spmd} | conditional | bytes 8 | solution.py:201
  0.7 2.2 %branch_1_fun.1 = (f32[8,1536]{1,0:T(8,128)S(1)}, f32[8,1536]{1,0:T(8,128)S(1)}) custom-call(s32[1]{0:T(128)} %get-tuple-element.18.core_ref, bf16[16,18432]{1,0:T(8,128)(2,1)} %get-tuple-element.19.slices_hbm, bf16[768,1536]{1,0:T(8,128)(2,1)} %get-tuple-element.32.weights_hbm), custom_call_target="tpu_custom_call" | custom-call | tf_op jit(solution)/shard_map/cond/branch_1_fun/pallas_call | solution.py:115
  2.9 8.8 %collective-permute-start = (f32[8,1536]{1,0:T(8,128)S(1)}, f32[8,1536]{1,0:T(8,128)S(1)}, u32[]{:S(2)}, u32[]{:S(2)}) collective-permute-start(f32[8,1536]{1,0:T(8,128)S(1)} %get-tuple-element.26), channel_id=1, source_target_pairs={{0,1},{1,0},{2,3},{3,2},{4,5},{5,4},{6,7},{7,6},{8,9},{9,8},{10,11... | collective-permute-start | bytes 147464 | tf_op jit(solution)/shard_map/ppermute | solution.py:206
  11.7 0.1 and_select_fusion.1
  11.8 0.1 fusion.70
  11.9 0.6 %collective-permute-done = f32[8,1536]{1,0:T(8,128)S(1)} collective-permute-done((f32[8,1536]{1,0:T(8,128)S(1)}, f32[8,1536]{1,0:T(8,128)S(1)}, u32[]{:S(2)}, u32[]{:S(2)}) %collective-permute-start) | collective-permute-done | bytes 49184 | tf_op jit(solution)/shard_map/ppermute | solution.py:206
  12.5 0.1 multiply_reduce_fusion
  12.7 0.1 multiply_convert_fusion
  12.8 1.9 %collective-permute-start.2 = (bf16[8,1664]{1,0:T(8,128)(2,1)S(1)}, bf16[8,1664]{1,0:T(8,128)(2,1)S(1)}, u32[]{:S(2)}, u32[]{:S(2)}) collective-permute-start(bf16[8,1664]{1,0:T(8,128)(2,1)S(1)} %pad_maximum_fusion.2), channel_id=1, source_target_pairs={{0,272},{272,0},{16,256},{256,16},{1,273},{273,1},{17,257},{257,17... | collective-permute-start | bytes 79880 | tf_op jit(solution)/shard_map/ppermute | solution.py:220
  14.7 1.9 %collective-permute-start.1 = (bf16[8,1664]{1,0:T(8,128)(2,1)S(1)}, bf16[8,1664]{1,0:T(8,128)(2,1)S(1)}, u32[]{:S(2)}, u32[]{:S(2)}) collective-permute-start(bf16[8,1664]{1,0:T(8,128)(2,1)S(1)} %pad_maximum_fusion.2), channel_id=1, source_target_pairs={{0,256},{256,0},{1,257},{257,1},{2,258},{258,2},{3,259},{259,3},{4... | collective-permute-start | bytes 79880 | tf_op jit(solution)/shard_map/ppermute | solution.py:219
  16.6 7.7 %collective-permute-start.3 = (bf16[8,1664]{1,0:T(8,128)(2,1)S(1)}, bf16[8,1664]{1,0:T(8,128)(2,1)S(1)}, u32[]{:S(2)}, u32[]{:S(2)}) collective-permute-start(bf16[8,1664]{1,0:T(8,128)(2,1)S(1)} %pad_maximum_fusion.2), channel_id=1, source_target_pairs={{0,128},{32,160},{64,192},{96,224},{128,0},{160,32},{192,64},{224,... | collective-permute-start | bytes 79880 | tf_op jit(solution)/shard_map/ppermute | solution.py:140
  24.3 0.0 collective-permute-done.1
  24.3 0.8 %broadcast_in_dim.12 = bf16[8,16,1664]{2,1,0:T(8,128)(2,1)} broadcast(bf16[16,1664]{1,0:T(8,128)(2,1)S(1)} %pad_maximum_fusion), dimensions={1,2} | broadcast | bytes 479232 | tf_op jit(solution)/shard_map/broadcast_in_dim | solution.py:222
  25.1 8.9 %all-to-all-start = ((bf16[8,16,1664]{2,1,0:T(8,128)(2,1)}), bf16[8,16,1664]{2,1,0:T(8,128)(2,1)S(1)}, u32[]{:S(2)}, u32[]{:S(2)}) async-start(bf16[8,16,1664]{2,1,0:T(8,128)(2,1)} %broadcast_in_dim.12), calls=%async_computation | async-start | bytes 851968 | tf_op jit(solution)/shard_map/all_to_all | solution.py:132
  34.2 4.9 %collective-permute-start.6 = (bf16[16,1664]{1,0:T(8,128)(2,1)S(1)}, bf16[16,1664]{1,0:T(8,128)(2,1)S(1)}, u32[]{:S(2)}, u32[]{:S(2)}) collective-permute-start(bf16[16,1664]{1,0:T(8,128)(2,1)S(1)} %broadcast_add_fusion), channel_id=1, source_target_pairs={{0,96},{32,64},{64,32},{96,0},{128,224},{160,192},{192,160},{224,1... | collective-permute-start | bytes 159752 | tf_op jit(solution)/shard_map/ppermute | solution.py:140
  39.1 1.9 %collective-permute-start.5 = (bf16[16,1664]{1,0:T(8,128)(2,1)S(1)}, bf16[16,1664]{1,0:T(8,128)(2,1)S(1)}, u32[]{:S(2)}, u32[]{:S(2)}) collective-permute-start(bf16[16,1664]{1,0:T(8,128)(2,1)S(1)} %broadcast_add_fusion), channel_id=1, source_target_pairs={{0,64},{32,96},{64,0},{96,32},{128,192},{160,224},{192,128},{224,1... | collective-permute-start | bytes 159752 | tf_op jit(solution)/shard_map/ppermute | solution.py:140
  41.0 2.4 %collective-permute-start.4 = (bf16[16,1664]{1,0:T(8,128)(2,1)S(1)}, bf16[16,1664]{1,0:T(8,128)(2,1)S(1)}, u32[]{:S(2)}, u32[]{:S(2)}) collective-permute-start(bf16[16,1664]{1,0:T(8,128)(2,1)S(1)} %broadcast_add_fusion), channel_id=1, source_target_pairs={{0,32},{32,0},{64,96},{96,64},{128,160},{160,128},{192,224},{224,1... | collective-permute-start | bytes 159752 | tf_op jit(solution)/shard_map/ppermute | solution.py:140
  44.8 0.0 all-to-all-done
  44.8 2.6 %collective-permute-start.7 = (bf16[128,1664]{1,0:T(8,128)(2,1)S(1)}, bf16[128,1664]{1,0:T(8,128)(2,1)S(1)}, u32[]{:S(2)}, u32[]{:S(2)}) collective-permute-start(bf16[128,1664]{1,0:T(8,128)(2,1)S(1)} %bitcast.11), channel_id=1, source_target_pairs={{0,1},{1,0},{2,3},{3,2},{4,5},{5,4},{6,7},{7,6},{8,9},{9,8},{10,11... | collective-permute-start | bytes 1277960 | tf_op jit(solution)/shard_map/ppermute | solution.py:226
  47.4 0.0 collective-permute-done.6
  47.4 0.3 convolution_convert_fusion
  47.7 0.3 fusion.1
  48.0 0.3 fusion.32
  48.3 0.2 fusion.5
  48.5 0.3 collective-permute-done.7
  48.8 0.3 fusion.2
  49.0 0.3 fusion.33
  49.3 0.1 select_convert_fusion
  49.4 0.2 fusion
  49.6 0.1 maximum_bitcast_fusion
  49.7 12.3 %all_to_all.10 = f16[8,8,1664]{2,1,0:T(8,128)(2,1)S(1)} all-to-all(f16[8,8,1664]{2,1,0:T(8,128)(2,1)S(1)} %maximum_bitcast_fusion), channel_id=1, replica_groups={{0,32,64,96,128,160,192,224},{129,161,193,225,1,33,65,97},{2,34,66,98,1..., dimensions={0} | all-to-all | bytes 425984 | tf_op jit(solution)/shard_map/all_to_all | solution.py:132
  62.1 0.8 %shard_map.89 = (f32[1,8,1536]{2,1,0:T(8,128)}, f32[1,8]{1,0:T(1,128)}) custom-call(f32[1]{0:T(128)S(6)} %copy.18.scale_ref, f32[8,1664]{1,0:T(8,128)S(1)} %convert_reduce_fusion.total_ref, f32[8,1536]{1,0:T(8,128)S(1)} %get-tuple-element.34.embedding_ref), custom_call_target="tpu_custom_call" | custom-call | tf_op jit(solution)/shard_map/pallas_call | solution.py:260
  (21 shorter events, 0.2 us)
Async XLA Ops:
  0.6 11.1 %copy-start = (s32[16]{0:T(128)S(1)}, s32[16]{0:T(128)}, u32[]{:S(2)}) copy-start(s32[16]{0:T(128)} %param.13) | copy-start | bytes 196
  2.9 9.7 %collective-permute-start = (f32[8,1536]{1,0:T(8,128)S(1)}, f32[8,1536]{1,0:T(8,128)S(1)}, u32[]{:S(2)}, u32[]{:S(2)}) collective-permute-start(f32[8,1536]{1,0:T(8,128)S(1)} %get-tuple-element.26), channel_id=1, source_target_pairs={{0,1},{1,0},{2,3},{3,2},{4,5},{5,4},{6,7},{7,6},{8,9},{9,8},{10,11... | collective-permute-start | bytes 147464 | tf_op jit(solution)/shard_map/ppermute | solution.py:206
  12.8 11.5 %collective-permute-start.2 = (bf16[8,1664]{1,0:T(8,128)(2,1)S(1)}, bf16[8,1664]{1,0:T(8,128)(2,1)S(1)}, u32[]{:S(2)}, u32[]{:S(2)}) collective-permute-start(bf16[8,1664]{1,0:T(8,128)(2,1)S(1)} %pad_maximum_fusion.2), channel_id=1, source_target_pairs={{0,272},{272,0},{16,256},{256,16},{1,273},{273,1},{17,257},{257,17... | collective-permute-start | bytes 79880 | tf_op jit(solution)/shard_map/ppermute | solution.py:220
  14.7 9.6 %collective-permute-start.1 = (bf16[8,1664]{1,0:T(8,128)(2,1)S(1)}, bf16[8,1664]{1,0:T(8,128)(2,1)S(1)}, u32[]{:S(2)}, u32[]{:S(2)}) collective-permute-start(bf16[8,1664]{1,0:T(8,128)(2,1)S(1)} %pad_maximum_fusion.2), channel_id=1, source_target_pairs={{0,256},{256,0},{1,257},{257,1},{2,258},{258,2},{3,259},{259,3},{4... | collective-permute-start | bytes 79880 | tf_op jit(solution)/shard_map/ppermute | solution.py:219
  16.6 17.4 %collective-permute-start.3 = (bf16[8,1664]{1,0:T(8,128)(2,1)S(1)}, bf16[8,1664]{1,0:T(8,128)(2,1)S(1)}, u32[]{:S(2)}, u32[]{:S(2)}) collective-permute-start(bf16[8,1664]{1,0:T(8,128)(2,1)S(1)} %pad_maximum_fusion.2), channel_id=1, source_target_pairs={{0,128},{32,160},{64,192},{96,224},{128,0},{160,32},{192,64},{224,... | collective-permute-start | bytes 79880 | tf_op jit(solution)/shard_map/ppermute | solution.py:140
  25.1 19.7 %all-to-all-start = ((bf16[8,16,1664]{2,1,0:T(8,128)(2,1)}), bf16[8,16,1664]{2,1,0:T(8,128)(2,1)S(1)}, u32[]{:S(2)}, u32[]{:S(2)}) async-start(bf16[8,16,1664]{2,1,0:T(8,128)(2,1)} %broadcast_in_dim.12), calls=%async_computation | async-start | bytes 851968 | tf_op jit(solution)/shard_map/all_to_all | solution.py:132
  34.2 13.2 %collective-permute-start.6 = (bf16[16,1664]{1,0:T(8,128)(2,1)S(1)}, bf16[16,1664]{1,0:T(8,128)(2,1)S(1)}, u32[]{:S(2)}, u32[]{:S(2)}) collective-permute-start(bf16[16,1664]{1,0:T(8,128)(2,1)S(1)} %broadcast_add_fusion), channel_id=1, source_target_pairs={{0,96},{32,64},{64,32},{96,0},{128,224},{160,192},{192,160},{224,1... | collective-permute-start | bytes 159752 | tf_op jit(solution)/shard_map/ppermute | solution.py:140
  39.1 8.3 %collective-permute-start.5 = (bf16[16,1664]{1,0:T(8,128)(2,1)S(1)}, bf16[16,1664]{1,0:T(8,128)(2,1)S(1)}, u32[]{:S(2)}, u32[]{:S(2)}) collective-permute-start(bf16[16,1664]{1,0:T(8,128)(2,1)S(1)} %broadcast_add_fusion), channel_id=1, source_target_pairs={{0,64},{32,96},{64,0},{96,32},{128,192},{160,224},{192,128},{224,1... | collective-permute-start | bytes 159752 | tf_op jit(solution)/shard_map/ppermute | solution.py:140
  41.0 6.4 %collective-permute-start.4 = (bf16[16,1664]{1,0:T(8,128)(2,1)S(1)}, bf16[16,1664]{1,0:T(8,128)(2,1)S(1)}, u32[]{:S(2)}, u32[]{:S(2)}) collective-permute-start(bf16[16,1664]{1,0:T(8,128)(2,1)S(1)} %broadcast_add_fusion), channel_id=1, source_target_pairs={{0,32},{32,0},{64,96},{96,64},{128,160},{160,128},{192,224},{224,1... | collective-permute-start | bytes 159752 | tf_op jit(solution)/shard_map/ppermute | solution.py:140
  44.8 3.9 %collective-permute-start.7 = (bf16[128,1664]{1,0:T(8,128)(2,1)S(1)}, bf16[128,1664]{1,0:T(8,128)(2,1)S(1)}, u32[]{:S(2)}, u32[]{:S(2)}) collective-permute-start(bf16[128,1664]{1,0:T(8,128)(2,1)S(1)} %bitcast.11), channel_id=1, source_target_pairs={{0,1},{1,0},{2,3},{3,2},{4,5},{5,4},{6,7},{7,6},{8,9},{9,8},{10,11... | collective-permute-start | bytes 1277960 | tf_op jit(solution)/shard_map/ppermute | solution.py:226

commit v6 on v4

--- a/solution.py
+++ b/solution.py
@@ -11,6 +11,7 @@
 LANES = 128
 HIGH, LOW = 64, 32
 SUMS = 3
+FIRST_Z = (4, 6)
 
 
 def project(pooled, weights, copies, core_ref, keep_ref, send_ref):
@@ -110,11 +111,11 @@
     )(core_index, *given)
 
 
-def staggered(blocks, axis):
+def staggered(blocks, axis, firsts):
     members = lax.axis_size(axis)
     cores = lax.axis_size("mp")
     groups = [
-        [(at ^ (core * (members // 2))) * cores + core for at in range(members)]
+        [(at + firsts[core]) % members * cores + core for at in range(members)]
         for core in range(cores)
     ]
     return lax.all_to_all(blocks, (axis, "mp"), 0, 0, axis_index_groups=groups, tiled=True)
@@ -136,13 +137,14 @@
     return jnp.concatenate([pair] + [brought(pair, across) for across in range(1, half)], axis=0)
 
 
-def in_order(held, axis, size, last):
+def in_order(held, axis, size, firsts, last):
     members = lax.axis_size(axis)
     place = lax.broadcasted_iota(jnp.int32, (members * size, members * size), 0)
     slot = lax.broadcasted_iota(jnp.int32, (members * size, members * size), 1)
     number = slot // size
     came_from = lax.axis_index(axis) ^ (number // 2 + (number % 2) * (members // 2))
-    member = (place // size) ^ (lax.axis_index("mp") * (members // 2))
+    first = jnp.where(lax.axis_index("mp") == 0, firsts[0], firsts[1])
+    member = (place // size + first) % members
     moves = (member == came_from) & (place % size == slot % size)
     moves = moves.astype(held.dtype) + last[: members * size, : members * size] * 0
     ordered = jnp.dot(moves, held, preferred_element_type=jnp.float32)
@@ -209,10 +211,10 @@
     other = jnp.concatenate([near, across], axis=0)
     copies = jnp.broadcast_to(other[None], (n_y,) + other.shape)
     held = swap_gather(own, "z")
-    other_mine = staggered(copies, "y")
+    other_mine = staggered(copies, "y", (0, n_y // 2))
     other_mine = other_mine.reshape(n_y * n_x * share, width + LANES)
     other_theirs = lax.ppermute(other_mine, "mp", [(0, 1), (1, 0)])
-    own_all = in_order(held, "z", share, other_mine)
+    own_all = in_order(held, "z", share, FIRST_Z, other_mine)
 
     temper = jnp.exp(log_scale[0])
     own_low = own_all[:, :width]
@@ -241,7 +243,7 @@
     lane = lax.broadcasted_iota(jnp.int32, (n_z * share, LANES), 1)
     loss_block = jnp.where(lane == 0, loss_high, loss_rest).astype(jnp.float16)
     sums = jnp.concatenate([grad_part.astype(jnp.float16), loss_block], axis=1)
-    sums = staggered(sums.reshape(n_z, share, width + LANES), "z")
+    sums = staggered(sums.reshape(n_z, share, width + LANES), "z", FIRST_Z)
     total = jnp.sum(sums.astype(jnp.float32), axis=0)
     vmem = pl.BlockSpec(memory_space=pltpu.VMEM)
     any_space = pl.BlockSpec(memory_space=pl.ANY)

time: 63.9 us -> 63.7 us (level)
  no operation moved by 1% of the time
where the time goes in v6:
time: 63.7 us; the launch traced here: 63.2 us
  starting transfers between devices  41 us (64%)
  blocking collectives  12.7 us (20%)
  Pallas kernels  2.89 us (5%)
  between operations  2.26 us (4%)
  matrix products  1.77 us (3%)
  waiting for transfers between devices  0.95 us (1%)
  local copies, waits for them, and re-layouts  0.79 us (1%)
  other arithmetic  0.71 us (1%)
    ppermute x4, starting transfers between devices, brought(): lax.ppermute(value, axis, [(index, index ^ across) for index in range(mem...  16.9 us
    all_to_all x1, blocking collectives, staggered(): lax.all_to_all(blocks, (axis, 'mp'), 0, 0, axis_index_groups=groups, tile...  12.7 us
    all_to_all x1, starting transfers between devices, staggered(): lax.all_to_all(blocks, (axis, 'mp'), 0, 0, axis_index_groups=groups, tile...  8.93 us
    ppermute x1, starting transfers between devices, shards(): embedding = kept + lax.ppermute(sent, 'mp', [(0, 1), (1, 0)])  8.79 us
    ppermute x1, starting transfers between devices, shards(): other_theirs = lax.ppermute(other_mine, 'mp', [(0, 1), (1, 0)])  2.56 us
    pallas_call x1, Pallas kernels, pooled_partial(): pl.pallas_call(kernel, out_shape=(half, half), in_specs=[pl.BlockSpec(mem...  2.05 us
    ppermute x1, starting transfers between devices, shards(): near = lax.ppermute(own, 'tower', [(0, 1), (1, 0)])  1.92 us
    ppermute x1, starting transfers between devices, shards(): across = lax.ppermute(own, ('tower', 'x'), [(0, 3), (3, 0), (1, 2), (2, 1)])  1.92 us
  transfers between devices with their start and end apart: 9, of which 2 were waited for; matrix products, arithmetic and copies ran while one was open for 3% of the time, Pallas kernels for 0%

profile of v6, /device:TPU:1, one launch (start us, length us, event | category | flops | bytes accessed | tf_op | source)
XLA Modules:
  0.0 63.2 jit_solution(18227904588001071416)
XLA Ops:
  0.6 2.1 %conditional.1 = ((f32[8,1536]{1,0:T(8,128)S(1)}, f32[8,1536]{1,0:T(8,128)S(1)})) conditional(s32[]{:T(128)} %convert_element_type.48, (s32[1]{0:T(128)}, s32[16]{0:T(128)}, bf16[16,18432]{1,0:T(8,128)(2,1)}, bf16[576,1536]{1,0:T(8,128)(2,1)}) %tuple.27, (s32[1]{0:T(128)}, bf16[16,18432]{1,0:T(8,128)(2,1)}, bf16[768,1536]{1,0:T(8,128)(2,1)}) %tuple.28), branch_computations={%region_0.0_spmd, %region_1.0_spmd} | conditional | bytes 8 | solution.py:191
  0.7 2.1 %branch_1_fun.1 = (f32[8,1536]{1,0:T(8,128)S(1)}, f32[8,1536]{1,0:T(8,128)S(1)}) custom-call(s32[1]{0:T(128)} %get-tuple-element.18.core_ref, bf16[16,18432]{1,0:T(8,128)(2,1)} %get-tuple-element.19.slices_hbm, bf16[768,1536]{1,0:T(8,128)(2,1)} %get-tuple-element.32.weights_hbm), custom_call_target="tpu_custom_call" | custom-call | tf_op jit(solution)/shard_map/cond/branch_1_fun/pallas_call | solution.py:104
  2.7 8.8 %collective-permute-start = (f32[8,1536]{1,0:T(8,128)S(1)}, f32[8,1536]{1,0:T(8,128)S(1)}, u32[]{:S(2)}, u32[]{:S(2)}) collective-permute-start(f32[8,1536]{1,0:T(8,128)S(1)} %get-tuple-element.26), channel_id=1, source_target_pairs={{0,1},{1,0},{2,3},{3,2},{4,5},{5,4},{6,7},{7,6},{8,9},{9,8},{10,11... | collective-permute-start | bytes 147464 | tf_op jit(solution)/shard_map/ppermute | solution.py:196
  11.6 0.1 and_select_fusion.1
  11.7 0.1 fusion.73
  11.7 0.6 %collective-permute-done = f32[8,1536]{1,0:T(8,128)S(1)} collective-permute-done((f32[8,1536]{1,0:T(8,128)S(1)}, f32[8,1536]{1,0:T(8,128)S(1)}, u32[]{:S(2)}, u32[]{:S(2)}) %collective-permute-start) | collective-permute-done | bytes 49184 | tf_op jit(solution)/shard_map/ppermute | solution.py:196
  12.4 0.1 multiply_reduce_fusion
  12.5 0.1 multiply_convert_fusion
  12.6 1.9 %collective-permute-start.2 = (bf16[8,1664]{1,0:T(8,128)(2,1)S(1)}, bf16[8,1664]{1,0:T(8,128)(2,1)S(1)}, u32[]{:S(2)}, u32[]{:S(2)}) collective-permute-start(bf16[8,1664]{1,0:T(8,128)(2,1)S(1)} %pad_maximum_fusion.2), channel_id=1, source_target_pairs={{0,272},{272,0},{16,256},{256,16},{1,273},{273,1},{17,257},{257,17... | collective-permute-start | bytes 79880 | tf_op jit(solution)/shard_map/ppermute | solution.py:210
  14.5 1.9 %collective-permute-start.1 = (bf16[8,1664]{1,0:T(8,128)(2,1)S(1)}, bf16[8,1664]{1,0:T(8,128)(2,1)S(1)}, u32[]{:S(2)}, u32[]{:S(2)}) collective-permute-start(bf16[8,1664]{1,0:T(8,128)(2,1)S(1)} %pad_maximum_fusion.2), channel_id=1, source_target_pairs={{0,256},{256,0},{1,257},{257,1},{2,258},{258,2},{3,259},{259,3},{4... | collective-permute-start | bytes 79880 | tf_op jit(solution)/shard_map/ppermute | solution.py:209
  16.5 7.7 %collective-permute-start.3 = (bf16[8,1664]{1,0:T(8,128)(2,1)S(1)}, bf16[8,1664]{1,0:T(8,128)(2,1)S(1)}, u32[]{:S(2)}, u32[]{:S(2)}) collective-permute-start(bf16[8,1664]{1,0:T(8,128)(2,1)S(1)} %pad_maximum_fusion.2), channel_id=1, source_target_pairs={{0,128},{32,160},{64,192},{96,224},{128,0},{160,32},{192,64},{224,... | collective-permute-start | bytes 79880 | tf_op jit(solution)/shard_map/ppermute | solution.py:129
  24.1 0.0 collective-permute-done.2
  24.1 0.0 collective-permute-done.1
  24.2 0.8 %broadcast_in_dim.12 = bf16[8,16,1664]{2,1,0:T(8,128)(2,1)} broadcast(bf16[16,1664]{1,0:T(8,128)(2,1)S(1)} %pad_maximum_fusion), dimensions={1,2} | broadcast | bytes 479232 | tf_op jit(solution)/shard_map/broadcast_in_dim | solution.py:212
  25.0 8.9 %all-to-all-start = ((bf16[8,16,1664]{2,1,0:T(8,128)(2,1)}), bf16[8,16,1664]{2,1,0:T(8,128)(2,1)S(1)}, u32[]{:S(2)}, u32[]{:S(2)}) async-start(bf16[8,16,1664]{2,1,0:T(8,128)(2,1)} %broadcast_in_dim.12), calls=%async_computation | async-start | bytes 851968 | tf_op jit(solution)/shard_map/all_to_all | solution.py:121
  34.0 4.9 %collective-permute-start.6 = (bf16[16,1664]{1,0:T(8,128)(2,1)S(1)}, bf16[16,1664]{1,0:T(8,128)(2,1)S(1)}, u32[]{:S(2)}, u32[]{:S(2)}) collective-permute-start(bf16[16,1664]{1,0:T(8,128)(2,1)S(1)} %broadcast_add_fusion), channel_id=1, source_target_pairs={{0,96},{32,64},{64,32},{96,0},{128,224},{160,192},{192,160},{224,1... | collective-permute-start | bytes 159752 | tf_op jit(solution)/shard_map/ppermute | solution.py:129
  39.0 1.9 %collective-permute-start.5 = (bf16[16,1664]{1,0:T(8,128)(2,1)S(1)}, bf16[16,1664]{1,0:T(8,128)(2,1)S(1)}, u32[]{:S(2)}, u32[]{:S(2)}) collective-permute-start(bf16[16,1664]{1,0:T(8,128)(2,1)S(1)} %broadcast_add_fusion), channel_id=1, source_target_pairs={{0,64},{32,96},{64,0},{96,32},{128,192},{160,224},{192,128},{224,1... | collective-permute-start | bytes 159752 | tf_op jit(solution)/shard_map/ppermute | solution.py:129
  40.9 2.4 %collective-permute-start.4 = (bf16[16,1664]{1,0:T(8,128)(2,1)S(1)}, bf16[16,1664]{1,0:T(8,128)(2,1)S(1)}, u32[]{:S(2)}, u32[]{:S(2)}) collective-permute-start(bf16[16,1664]{1,0:T(8,128)(2,1)S(1)} %broadcast_add_fusion), channel_id=1, source_target_pairs={{0,32},{32,0},{64,96},{96,64},{128,160},{160,128},{192,224},{224,1... | collective-permute-start | bytes 159752 | tf_op jit(solution)/shard_map/ppermute | solution.py:129
  44.7 0.0 all-to-all-done
  44.7 2.6 %collective-permute-start.7 = (bf16[128,1664]{1,0:T(8,128)(2,1)S(1)}, bf16[128,1664]{1,0:T(8,128)(2,1)S(1)}, u32[]{:S(2)}, u32[]{:S(2)}) collective-permute-start(bf16[128,1664]{1,0:T(8,128)(2,1)S(1)} %bitcast.11), channel_id=1, source_target_pairs={{0,1},{1,0},{2,3},{3,2},{4,5},{5,4},{6,7},{7,6},{8,9},{9,8},{10,11... | collective-permute-start | bytes 1277960 | tf_op jit(solution)/shard_map/ppermute | solution.py:216
  47.3 0.3 convolution_convert_fusion
  47.6 0.3 fusion.1
  47.8 0.3 fusion.33
  48.1 0.2 fusion.5
  48.3 0.3 collective-permute-done.7
  48.6 0.3 fusion.2
  48.9 0.3 fusion.34
  49.2 0.1 select_convert_fusion
  49.3 0.2 fusion
  49.5 0.1 maximum_bitcast_fusion
  49.6 12.7 %all_to_all.10 = f16[8,8,1664]{2,1,0:T(8,128)(2,1)S(1)} all-to-all(f16[8,8,1664]{2,1,0:T(8,128)(2,1)S(1)} %maximum_bitcast_fusion), channel_id=1, replica_groups={{128,160,192,224,0,32,64,96},{193,225,1,33,65,97,129,161},{130,162,194,..., dimensions={0} | all-to-all | bytes 425984 | tf_op jit(solution)/shard_map/all_to_all | solution.py:121
  62.3 0.8 %shard_map.89 = (f32[1,8,1536]{2,1,0:T(8,128)}, f32[1,8]{1,0:T(1,128)}) custom-call(f32[1]{0:T(128)S(6)} %copy.18.scale_ref, f32[8,1664]{1,0:T(8,128)S(1)} %convert_reduce_fusion.total_ref, f32[8,1536]{1,0:T(8,128)S(1)} %get-tuple-element.34.embedding_ref), custom_call_target="tpu_custom_call" | custom-call | tf_op jit(solution)/shard_map/pallas_call | solution.py:250
  (21 shorter events, 0.2 us)
Async XLA Ops:
  0.6 10.9 %copy-start = (s32[16]{0:T(128)S(1)}, s32[16]{0:T(128)}, u32[]{:S(2)}) copy-start(s32[16]{0:T(128)} %param.13) | copy-start | bytes 196
  2.7 9.7 %collective-permute-start = (f32[8,1536]{1,0:T(8,128)S(1)}, f32[8,1536]{1,0:T(8,128)S(1)}, u32[]{:S(2)}, u32[]{:S(2)}) collective-permute-start(f32[8,1536]{1,0:T(8,128)S(1)} %get-tuple-element.26), channel_id=1, source_target_pairs={{0,1},{1,0},{2,3},{3,2},{4,5},{5,4},{6,7},{7,6},{8,9},{9,8},{10,11... | collective-permute-start | bytes 147464 | tf_op jit(solution)/shard_map/ppermute | solution.py:196
  12.6 11.5 %collective-permute-start.2 = (bf16[8,1664]{1,0:T(8,128)(2,1)S(1)}, bf16[8,1664]{1,0:T(8,128)(2,1)S(1)}, u32[]{:S(2)}, u32[]{:S(2)}) collective-permute-start(bf16[8,1664]{1,0:T(8,128)(2,1)S(1)} %pad_maximum_fusion.2), channel_id=1, source_target_pairs={{0,272},{272,0},{16,256},{256,16},{1,273},{273,1},{17,257},{257,17... | collective-permute-start | bytes 79880 | tf_op jit(solution)/shard_map/ppermute | solution.py:210
  14.5 9.6 %collective-permute-start.1 = (bf16[8,1664]{1,0:T(8,128)(2,1)S(1)}, bf16[8,1664]{1,0:T(8,128)(2,1)S(1)}, u32[]{:S(2)}, u32[]{:S(2)}) collective-permute-start(bf16[8,1664]{1,0:T(8,128)(2,1)S(1)} %pad_maximum_fusion.2), channel_id=1, source_target_pairs={{0,256},{256,0},{1,257},{257,1},{2,258},{258,2},{3,259},{259,3},{4... | collective-permute-start | bytes 79880 | tf_op jit(solution)/shard_map/ppermute | solution.py:209
  16.5 17.4 %collective-permute-start.3 = (bf16[8,1664]{1,0:T(8,128)(2,1)S(1)}, bf16[8,1664]{1,0:T(8,128)(2,1)S(1)}, u32[]{:S(2)}, u32[]{:S(2)}) collective-permute-start(bf16[8,1664]{1,0:T(8,128)(2,1)S(1)} %pad_maximum_fusion.2), channel_id=1, source_target_pairs={{0,128},{32,160},{64,192},{96,224},{128,0},{160,32},{192,64},{224,... | collective-permute-start | bytes 79880 | tf_op jit(solution)/shard_map/ppermute | solution.py:129
  25.0 19.7 %all-to-all-start = ((bf16[8,16,1664]{2,1,0:T(8,128)(2,1)}), bf16[8,16,1664]{2,1,0:T(8,128)(2,1)S(1)}, u32[]{:S(2)}, u32[]{:S(2)}) async-start(bf16[8,16,1664]{2,1,0:T(8,128)(2,1)} %broadcast_in_dim.12), calls=%async_computation | async-start | bytes 851968 | tf_op jit(solution)/shard_map/all_to_all | solution.py:121
  34.0 13.2 %collective-permute-start.6 = (bf16[16,1664]{1,0:T(8,128)(2,1)S(1)}, bf16[16,1664]{1,0:T(8,128)(2,1)S(1)}, u32[]{:S(2)}, u32[]{:S(2)}) collective-permute-start(bf16[16,1664]{1,0:T(8,128)(2,1)S(1)} %broadcast_add_fusion), channel_id=1, source_target_pairs={{0,96},{32,64},{64,32},{96,0},{128,224},{160,192},{192,160},{224,1... | collective-permute-start | bytes 159752 | tf_op jit(solution)/shard_map/ppermute | solution.py:129
  39.0 8.3 %collective-permute-start.5 = (bf16[16,1664]{1,0:T(8,128)(2,1)S(1)}, bf16[16,1664]{1,0:T(8,128)(2,1)S(1)}, u32[]{:S(2)}, u32[]{:S(2)}) collective-permute-start(bf16[16,1664]{1,0:T(8,128)(2,1)S(1)} %broadcast_add_fusion), channel_id=1, source_target_pairs={{0,64},{32,96},{64,0},{96,32},{128,192},{160,224},{192,128},{224,1... | collective-permute-start | bytes 159752 | tf_op jit(solution)/shard_map/ppermute | solution.py:129
  40.9 6.4 %collective-permute-start.4 = (bf16[16,1664]{1,0:T(8,128)(2,1)S(1)}, bf16[16,1664]{1,0:T(8,128)(2,1)S(1)}, u32[]{:S(2)}, u32[]{:S(2)}) collective-permute-start(bf16[16,1664]{1,0:T(8,128)(2,1)S(1)} %broadcast_add_fusion), channel_id=1, source_target_pairs={{0,32},{32,0},{64,96},{96,64},{128,160},{160,128},{192,224},{224,1... | collective-permute-start | bytes 159752 | tf_op jit(solution)/shard_map/ppermute | solution.py:129
  44.7 3.9 %collective-permute-start.7 = (bf16[128,1664]{1,0:T(8,128)(2,1)S(1)}, bf16[128,1664]{1,0:T(8,128)(2,1)S(1)}, u32[]{:S(2)}, u32[]{:S(2)}) collective-permute-start(bf16[128,1664]{1,0:T(8,128)(2,1)S(1)} %bitcast.11), channel_id=1, source_target_pairs={{0,1},{1,0},{2,3},{3,2},{4,5},{5,4},{6,7},{7,6},{8,9},{9,8},{10,11... | collective-permute-start | bytes 1277960 | tf_op jit(solution)/shard_map/ppermute | solution.py:216

commit v7 on v6

--- a/solution.py
+++ b/solution.py
@@ -11,6 +11,7 @@
 LANES = 128
 HIGH, LOW = 64, 32
 SUMS = 3
+FIRST_Y = (7, 4)
 FIRST_Z = (4, 6)
 
 
@@ -208,15 +209,15 @@
 
     near = lax.ppermute(own, "tower", [(0, 1), (1, 0)])
     across = lax.ppermute(own, ("tower", "x"), [(0, 3), (3, 0), (1, 2), (2, 1)])
-    other = jnp.concatenate([near, across], axis=0)
+    temper = jnp.exp(log_scale[0])
+    other = jnp.concatenate([near, across], axis=0) + (temper * 0).astype(near.dtype)
     copies = jnp.broadcast_to(other[None], (n_y,) + other.shape)
     held = swap_gather(own, "z")
-    other_mine = staggered(copies, "y", (0, n_y // 2))
+    other_mine = staggered(copies, "y", FIRST_Y)
     other_mine = other_mine.reshape(n_y * n_x * share, width + LANES)
     other_theirs = lax.ppermute(other_mine, "mp", [(0, 1), (1, 0)])
     own_all = in_order(held, "z", share, FIRST_Z, other_mine)
 
-    temper = jnp.exp(log_scale[0])
     own_low = own_all[:, :width]
 
     def products(rows, columns):

time: 63.7 us -> 64 us (level)
  transfers between devices with their start and end apart: 9 -> 9, of which waited for: 2 -> 3; matrix products, arithmetic and copies ran while one was open for 3% -> 3% of each run, Pallas kernels for 0% -> 0%
where the time goes in v7:
time: 64 us; the launch traced here: 63.5 us
  starting transfers between devices  41.2 us (64%)
  blocking collectives  12.9 us (20%)
  Pallas kernels  2.89 us (5%)
  between operations  2.26 us (4%)
  matrix products  1.76 us (3%)
  waiting for transfers between devices  0.96 us (2%)
  local copies, waits for them, and re-layouts  0.79 us (1%)
  other arithmetic  0.71 us (1%)
    ppermute x4, starting transfers between devices, brought(): lax.ppermute(value, axis, [(index, index ^ across) for index in range(mem...  16.9 us
    all_to_all x1, blocking collectives, staggered(): lax.all_to_all(blocks, (axis, 'mp'), 0, 0, axis_index_groups=groups, tile...  12.9 us
    all_to_all x1, starting transfers between devices, staggered(): lax.all_to_all(blocks, (axis, 'mp'), 0, 0, axis_index_groups=groups, tile...  8.93 us
    ppermute x1, starting transfers between devices, shards(): embedding = kept + lax.ppermute(sent, 'mp', [(0, 1), (1, 0)])  8.79 us
    ppermute x1, starting transfers between devices, shards(): other_theirs = lax.ppermute(other_mine, 'mp', [(0, 1), (1, 0)])  2.67 us
    pallas_call x1, Pallas kernels, pooled_partial(): pl.pallas_call(kernel, out_shape=(half, half), in_specs=[pl.BlockSpec(mem...  2.05 us
    ppermute x1, starting transfers between devices, shards(): near = lax.ppermute(own, 'tower', [(0, 1), (1, 0)])  1.92 us
    ppermute x1, starting transfers between devices, shards(): across = lax.ppermute(own, ('tower', 'x'), [(0, 3), (3, 0), (1, 2), (2, 1)])  1.92 us
  transfers between devices with their start and end apart: 9, of which 3 were waited for; matrix products, arithmetic and copies ran while one was open for 3% of the time, Pallas kernels for 0%

profile of v7, /device:TPU:1, one launch (start us, length us, event | category | flops | bytes accessed | tf_op | source)
XLA Modules:
  0.0 63.5 jit_solution(15349254697067359483)
XLA Ops:
  0.6 2.1 %conditional.1 = ((f32[8,1536]{1,0:T(8,128)S(1)}, f32[8,1536]{1,0:T(8,128)S(1)})) conditional(s32[]{:T(128)} %convert_element_type.51, (s32[1]{0:T(128)}, s32[16]{0:T(128)}, bf16[16,18432]{1,0:T(8,128)(2,1)}, bf16[576,1536]{1,0:T(8,128)(2,1)}) %tuple.27, (s32[1]{0:T(128)}, bf16[16,18432]{1,0:T(8,128)(2,1)}, bf16[768,1536]{1,0:T(8,128)(2,1)}) %tuple.28), branch_computations={%region_0.0_spmd, %region_1.0_spmd} | conditional | bytes 8 | solution.py:192
  0.7 2.1 %branch_1_fun.1 = (f32[8,1536]{1,0:T(8,128)S(1)}, f32[8,1536]{1,0:T(8,128)S(1)}) custom-call(s32[1]{0:T(128)} %get-tuple-element.18.core_ref, bf16[16,18432]{1,0:T(8,128)(2,1)} %get-tuple-element.19.slices_hbm, bf16[768,1536]{1,0:T(8,128)(2,1)} %get-tuple-element.32.weights_hbm), custom_call_target="tpu_custom_call" | custom-call | tf_op jit(solution)/shard_map/cond/branch_1_fun/pallas_call | solution.py:105
  2.7 8.8 %collective-permute-start = (f32[8,1536]{1,0:T(8,128)S(1)}, f32[8,1536]{1,0:T(8,128)S(1)}, u32[]{:S(2)}, u32[]{:S(2)}) collective-permute-start(f32[8,1536]{1,0:T(8,128)S(1)} %get-tuple-element.26), channel_id=1, source_target_pairs={{0,1},{1,0},{2,3},{3,2},{4,5},{5,4},{6,7},{7,6},{8,9},{9,8},{10,11... | collective-permute-start | bytes 147464 | tf_op jit(solution)/shard_map/ppermute | solution.py:197
  11.6 0.1 and_select_fusion.1
  11.7 0.1 fusion.73
  11.7 0.6 %collective-permute-done = f32[8,1536]{1,0:T(8,128)S(1)} collective-permute-done((f32[8,1536]{1,0:T(8,128)S(1)}, f32[8,1536]{1,0:T(8,128)S(1)}, u32[]{:S(2)}, u32[]{:S(2)}) %collective-permute-start) | collective-permute-done | bytes 49184 | tf_op jit(solution)/shard_map/ppermute | solution.py:197
  12.4 0.1 multiply_reduce_fusion
  12.5 0.1 multiply_convert_fusion
  12.6 1.9 %collective-permute-start.2 = (bf16[8,1664]{1,0:T(8,128)(2,1)S(1)}, bf16[8,1664]{1,0:T(8,128)(2,1)S(1)}, u32[]{:S(2)}, u32[]{:S(2)}) collective-permute-start(bf16[8,1664]{1,0:T(8,128)(2,1)S(1)} %pad_maximum_fusion.1), channel_id=1, source_target_pairs={{0,272},{272,0},{16,256},{256,16},{1,273},{273,1},{17,257},{257,17... | collective-permute-start | bytes 79880 | tf_op jit(solution)/shard_map/ppermute | solution.py:211
  14.5 1.9 %collective-permute-start.1 = (bf16[8,1664]{1,0:T(8,128)(2,1)S(1)}, bf16[8,1664]{1,0:T(8,128)(2,1)S(1)}, u32[]{:S(2)}, u32[]{:S(2)}) collective-permute-start(bf16[8,1664]{1,0:T(8,128)(2,1)S(1)} %pad_maximum_fusion.1), channel_id=1, source_target_pairs={{0,256},{256,0},{1,257},{257,1},{2,258},{258,2},{3,259},{259,3},{4... | collective-permute-start | bytes 79880 | tf_op jit(solution)/shard_map/ppermute | solution.py:210
  17.2 7.7 %collective-permute-start.3 = (bf16[8,1664]{1,0:T(8,128)(2,1)S(1)}, bf16[8,1664]{1,0:T(8,128)(2,1)S(1)}, u32[]{:S(2)}, u32[]{:S(2)}) collective-permute-start(bf16[8,1664]{1,0:T(8,128)(2,1)S(1)} %pad_maximum_fusion.1), channel_id=1, source_target_pairs={{0,128},{32,160},{64,192},{96,224},{128,0},{160,32},{192,64},{224,... | collective-permute-start | bytes 79880 | tf_op jit(solution)/shard_map/ppermute | solution.py:130
  24.8 0.0 collective-permute-done.2
  24.9 0.8 %broadcast_in_dim.12 = bf16[8,16,1664]{2,1,0:T(8,128)(2,1)} broadcast(bf16[16,1664]{1,0:T(8,128)(2,1)S(1)} %maximum_add_fusion), dimensions={1,2} | broadcast | bytes 479232 | tf_op jit(solution)/shard_map/broadcast_in_dim | solution.py:214
  25.7 8.9 %all-to-all-start = ((bf16[8,16,1664]{2,1,0:T(8,128)(2,1)}), bf16[8,16,1664]{2,1,0:T(8,128)(2,1)S(1)}, u32[]{:S(2)}, u32[]{:S(2)}) async-start(bf16[8,16,1664]{2,1,0:T(8,128)(2,1)} %broadcast_in_dim.12), calls=%async_computation | async-start | bytes 851968 | tf_op jit(solution)/shard_map/all_to_all | solution.py:122
  34.7 4.9 %collective-permute-start.6 = (bf16[16,1664]{1,0:T(8,128)(2,1)S(1)}, bf16[16,1664]{1,0:T(8,128)(2,1)S(1)}, u32[]{:S(2)}, u32[]{:S(2)}) collective-permute-start(bf16[16,1664]{1,0:T(8,128)(2,1)S(1)} %broadcast_add_fusion), channel_id=1, source_target_pairs={{0,96},{32,64},{64,32},{96,0},{128,224},{160,192},{192,160},{224,1... | collective-permute-start | bytes 159752 | tf_op jit(solution)/shard_map/ppermute | solution.py:130
  39.7 1.9 %collective-permute-start.5 = (bf16[16,1664]{1,0:T(8,128)(2,1)S(1)}, bf16[16,1664]{1,0:T(8,128)(2,1)S(1)}, u32[]{:S(2)}, u32[]{:S(2)}) collective-permute-start(bf16[16,1664]{1,0:T(8,128)(2,1)S(1)} %broadcast_add_fusion), channel_id=1, source_target_pairs={{0,64},{32,96},{64,0},{96,32},{128,192},{160,224},{192,128},{224,1... | collective-permute-start | bytes 159752 | tf_op jit(solution)/shard_map/ppermute | solution.py:130
  41.6 2.4 %collective-permute-start.4 = (bf16[16,1664]{1,0:T(8,128)(2,1)S(1)}, bf16[16,1664]{1,0:T(8,128)(2,1)S(1)}, u32[]{:S(2)}, u32[]{:S(2)}) collective-permute-start(bf16[16,1664]{1,0:T(8,128)(2,1)S(1)} %broadcast_add_fusion), channel_id=1, source_target_pairs={{0,32},{32,0},{64,96},{96,64},{128,160},{160,128},{192,224},{224,1... | collective-permute-start | bytes 159752 | tf_op jit(solution)/shard_map/ppermute | solution.py:130
  44.7 2.7 %collective-permute-start.7 = (bf16[128,1664]{1,0:T(8,128)(2,1)S(1)}, bf16[128,1664]{1,0:T(8,128)(2,1)S(1)}, u32[]{:S(2)}, u32[]{:S(2)}) collective-permute-start(bf16[128,1664]{1,0:T(8,128)(2,1)S(1)} %bitcast.11), channel_id=1, source_target_pairs={{0,1},{1,0},{2,3},{3,2},{4,5},{5,4},{6,7},{7,6},{8,9},{9,8},{10,11... | collective-permute-start | bytes 1277960 | tf_op jit(solution)/shard_map/ppermute | solution.py:218
  47.4 0.0 collective-permute-done.6
  47.4 0.1 collective-permute-done.4
  47.5 0.3 convolution_convert_fusion
  47.8 0.3 fusion.1
  48.1 0.3 fusion.33
  48.4 0.2 fusion.5
  48.6 0.2 collective-permute-done.7
  48.8 0.3 fusion.2
  49.0 0.3 fusion.34
  49.3 0.1 select_convert_fusion
  49.4 0.2 fusion
  49.6 0.1 maximum_bitcast_fusion
  49.7 12.9 %all_to_all.10 = f16[8,8,1664]{2,1,0:T(8,128)(2,1)S(1)} all-to-all(f16[8,8,1664]{2,1,0:T(8,128)(2,1)S(1)} %maximum_bitcast_fusion), channel_id=1, replica_groups={{128,160,192,224,0,32,64,96},{193,225,1,33,65,97,129,161},{130,162,194,..., dimensions={0} | all-to-all | bytes 425984 | tf_op jit(solution)/shard_map/all_to_all | solution.py:122
  62.6 0.8 %shard_map.89 = (f32[1,8,1536]{2,1,0:T(8,128)}, f32[1,8]{1,0:T(1,128)}) custom-call(f32[1]{0:T(128)S(6)} %copy.18.scale_ref, f32[8,1664]{1,0:T(8,128)S(1)} %convert_reduce_fusion.total_ref, f32[8,1536]{1,0:T(8,128)S(1)} %get-tuple-element.34.embedding_ref), custom_call_target="tpu_custom_call" | custom-call | tf_op jit(solution)/shard_map/pallas_call | solution.py:251
  (21 shorter events, 0.2 us)
Async XLA Ops:
  0.6 10.9 %copy-start = (s32[16]{0:T(128)S(1)}, s32[16]{0:T(128)}, u32[]{:S(2)}) copy-start(s32[16]{0:T(128)} %param.13) | copy-start | bytes 196
  2.7 9.7 %collective-permute-start = (f32[8,1536]{1,0:T(8,128)S(1)}, f32[8,1536]{1,0:T(8,128)S(1)}, u32[]{:S(2)}, u32[]{:S(2)}) collective-permute-start(f32[8,1536]{1,0:T(8,128)S(1)} %get-tuple-element.26), channel_id=1, source_target_pairs={{0,1},{1,0},{2,3},{3,2},{4,5},{5,4},{6,7},{7,6},{8,9},{9,8},{10,11... | collective-permute-start | bytes 147464 | tf_op jit(solution)/shard_map/ppermute | solution.py:197
  12.6 12.2 %collective-permute-start.2 = (bf16[8,1664]{1,0:T(8,128)(2,1)S(1)}, bf16[8,1664]{1,0:T(8,128)(2,1)S(1)}, u32[]{:S(2)}, u32[]{:S(2)}) collective-permute-start(bf16[8,1664]{1,0:T(8,128)(2,1)S(1)} %pad_maximum_fusion.1), channel_id=1, source_target_pairs={{0,272},{272,0},{16,256},{256,16},{1,273},{273,1},{17,257},{257,17... | collective-permute-start | bytes 79880 | tf_op jit(solution)/shard_map/ppermute | solution.py:211
  14.5 10.3 %collective-permute-start.1 = (bf16[8,1664]{1,0:T(8,128)(2,1)S(1)}, bf16[8,1664]{1,0:T(8,128)(2,1)S(1)}, u32[]{:S(2)}, u32[]{:S(2)}) collective-permute-start(bf16[8,1664]{1,0:T(8,128)(2,1)S(1)} %pad_maximum_fusion.1), channel_id=1, source_target_pairs={{0,256},{256,0},{1,257},{257,1},{2,258},{258,2},{3,259},{259,3},{4... | collective-permute-start | bytes 79880 | tf_op jit(solution)/shard_map/ppermute | solution.py:210
  17.2 17.4 %collective-permute-start.3 = (bf16[8,1664]{1,0:T(8,128)(2,1)S(1)}, bf16[8,1664]{1,0:T(8,128)(2,1)S(1)}, u32[]{:S(2)}, u32[]{:S(2)}) collective-permute-start(bf16[8,1664]{1,0:T(8,128)(2,1)S(1)} %pad_maximum_fusion.1), channel_id=1, source_target_pairs={{0,128},{32,160},{64,192},{96,224},{128,0},{160,32},{192,64},{224,... | collective-permute-start | bytes 79880 | tf_op jit(solution)/shard_map/ppermute | solution.py:130
  25.7 19.0 %all-to-all-start = ((bf16[8,16,1664]{2,1,0:T(8,128)(2,1)}), bf16[8,16,1664]{2,1,0:T(8,128)(2,1)S(1)}, u32[]{:S(2)}, u32[]{:S(2)}) async-start(bf16[8,16,1664]{2,1,0:T(8,128)(2,1)} %broadcast_in_dim.12), calls=%async_computation | async-start | bytes 851968 | tf_op jit(solution)/shard_map/all_to_all | solution.py:122
  34.7 12.7 %collective-permute-start.6 = (bf16[16,1664]{1,0:T(8,128)(2,1)S(1)}, bf16[16,1664]{1,0:T(8,128)(2,1)S(1)}, u32[]{:S(2)}, u32[]{:S(2)}) collective-permute-start(bf16[16,1664]{1,0:T(8,128)(2,1)S(1)} %broadcast_add_fusion), channel_id=1, source_target_pairs={{0,96},{32,64},{64,32},{96,0},{128,224},{160,192},{192,160},{224,1... | collective-permute-start | bytes 159752 | tf_op jit(solution)/shard_map/ppermute | solution.py:130
  39.7 7.7 %collective-permute-start.5 = (bf16[16,1664]{1,0:T(8,128)(2,1)S(1)}, bf16[16,1664]{1,0:T(8,128)(2,1)S(1)}, u32[]{:S(2)}, u32[]{:S(2)}) collective-permute-start(bf16[16,1664]{1,0:T(8,128)(2,1)S(1)} %broadcast_add_fusion), channel_id=1, source_target_pairs={{0,64},{32,96},{64,0},{96,32},{128,192},{160,224},{192,128},{224,1... | collective-permute-start | bytes 159752 | tf_op jit(solution)/shard_map/ppermute | solution.py:130
  41.6 5.9 %collective-permute-start.4 = (bf16[16,1664]{1,0:T(8,128)(2,1)S(1)}, bf16[16,1664]{1,0:T(8,128)(2,1)S(1)}, u32[]{:S(2)}, u32[]{:S(2)}) collective-permute-start(bf16[16,1664]{1,0:T(8,128)(2,1)S(1)} %broadcast_add_fusion), channel_id=1, source_target_pairs={{0,32},{32,0},{64,96},{96,64},{128,160},{160,128},{192,224},{224,1... | collective-permute-start | bytes 159752 | tf_op jit(solution)/shard_map/ppermute | solution.py:130
  44.7 4.1 %collective-permute-start.7 = (bf16[128,1664]{1,0:T(8,128)(2,1)S(1)}, bf16[128,1664]{1,0:T(8,128)(2,1)S(1)}, u32[]{:S(2)}, u32[]{:S(2)}) collective-permute-start(bf16[128,1664]{1,0:T(8,128)(2,1)S(1)} %bitcast.11), channel_id=1, source_target_pairs={{0,1},{1,0},{2,3},{3,2},{4,5},{5,4},{6,7},{7,6},{8,9},{9,8},{10,11... | collective-permute-start | bytes 1277960 | tf_op jit(solution)/shard_map/ppermute | solution.py:218

commit v8 on v7

--- a/solution.py
+++ b/solution.py
@@ -122,20 +122,26 @@
     return lax.all_to_all(blocks, (axis, "mp"), 0, 0, axis_index_groups=groups, tiled=True)
 
 
+def ring_partners(index, members):
+    return (index ^ 1, ((index + 1) ^ 1) + members - 1 & members - 1, index ^ 2)
+
+
 def swap_gather(block, axis):
     members = lax.axis_size(axis)
     half = members // 2
 
-    def brought(value, across):
-        return lax.ppermute(value, axis, [(index, index ^ across) for index in range(members)])
-
-    pair = jnp.concatenate([block, brought(block, half)], axis=0)
+    def brought(value, partners):
+        return lax.ppermute(value, axis, list(enumerate(partners)))
+
+    pair = jnp.concatenate([block, brought(block, [at ^ half for at in range(members)])], axis=0)
     wide = pair.astype(jnp.float32)
     passed = jnp.sum(wide, axis=0, keepdims=True)
     for _ in range(SUMS - 1):
         passed = jnp.sum(wide * passed, axis=0, keepdims=True)
     pair = pair + (passed * 0).astype(pair.dtype)
-    return jnp.concatenate([pair] + [brought(pair, across) for across in range(1, half)], axis=0)
+    table = [ring_partners(at, members) for at in range(members)]
+    near = [brought(pair, [row[step] for row in table]) for step in range(half - 1)]
+    return jnp.concatenate([pair] + near, axis=0)
 
 
 def in_order(held, axis, size, firsts, last):
@@ -143,7 +149,11 @@
     place = lax.broadcasted_iota(jnp.int32, (members * size, members * size), 0)
     slot = lax.broadcasted_iota(jnp.int32, (members * size, members * size), 1)
     number = slot // size
-    came_from = lax.axis_index(axis) ^ (number // 2 + (number % 2) * (members // 2))
+    me = lax.axis_index(axis)
+    came_from = me
+    for step, partner in enumerate(ring_partners(me, members)):
+        came_from = jnp.where(number // 2 == step + 1, partner, came_from)
+    came_from = came_from ^ ((number % 2) * (members // 2))
     first = jnp.where(lax.axis_index("mp") == 0, firsts[0], firsts[1])
     member = (place // size + first) % members
     moves = (member == came_from) & (place % size == slot % size)

time: 64 us -> 63.4 us (level)
  transfers between devices with their start and end apart: 9 -> 9, of which waited for: 3 -> 2; matrix products, arithmetic and copies ran while one was open for 3% -> 3% of each run, Pallas kernels for 0% -> 0%
where the time goes in v8:
time: 63.4 us; the launch traced here: 62.6 us
  starting transfers between devices  40.6 us (64%)
  blocking collectives  12.6 us (20%)
  Pallas kernels  2.89 us (5%)
  between operations  2.28 us (4%)
  matrix products  1.78 us (3%)
  waiting for transfers between devices  0.94 us (1%)
  local copies, waits for them, and re-layouts  0.79 us (1%)
  other arithmetic  0.71 us (1%)
    ppermute x4, starting transfers between devices, brought(): return lax.ppermute(value, axis, list(enumerate(partners)))  16.7 us
    all_to_all x1, blocking collectives, staggered(): lax.all_to_all(blocks, (axis, 'mp'), 0, 0, axis_index_groups=groups, tile...  12.6 us
    all_to_all x1, starting transfers between devices, staggered(): lax.all_to_all(blocks, (axis, 'mp'), 0, 0, axis_index_groups=groups, tile...  8.93 us
    ppermute x1, starting transfers between devices, shards(): embedding = kept + lax.ppermute(sent, 'mp', [(0, 1), (1, 0)])  8.79 us
    ppermute x1, starting transfers between devices, shards(): other_theirs = lax.ppermute(other_mine, 'mp', [(0, 1), (1, 0)])  2.39 us
    pallas_call x1, Pallas kernels, pooled_partial(): pl.pallas_call(kernel, out_shape=(half, half), in_specs=[pl.BlockSpec(mem...  2.05 us
    ppermute x1, starting transfers between devices, shards(): near = lax.ppermute(own, 'tower', [(0, 1), (1, 0)])  1.92 us
    ppermute x1, starting transfers between devices, shards(): across = lax.ppermute(own, ('tower', 'x'), [(0, 3), (3, 0), (1, 2), (2, 1)])  1.92 us
  transfers between devices with their start and end apart: 9, of which 2 were waited for; matrix products, arithmetic and copies ran while one was open for 3% of the time, Pallas kernels for 0%

profile of v8, /device:TPU:1, one launch (start us, length us, event | category | flops | bytes accessed | tf_op | source)
XLA Modules:
  0.0 62.6 jit_solution(10212820372441315799)
XLA Ops:
  0.6 2.1 %conditional.1 = ((f32[8,1536]{1,0:T(8,128)S(1)}, f32[8,1536]{1,0:T(8,128)S(1)})) conditional(s32[]{:T(128)} %convert_element_type.51, (s32[1]{0:T(128)}, s32[16]{0:T(128)}, bf16[16,18432]{1,0:T(8,128)(2,1)}, bf16[576,1536]{1,0:T(8,128)(2,1)}) %tuple.27, (s32[1]{0:T(128)}, bf16[16,18432]{1,0:T(8,128)(2,1)}, bf16[768,1536]{1,0:T(8,128)(2,1)}) %tuple.28), branch_computations={%region_0.0_spmd, %region_1.0_spmd} | conditional | bytes 8 | solution.py:202
  0.7 2.1 %branch_1_fun.1 = (f32[8,1536]{1,0:T(8,128)S(1)}, f32[8,1536]{1,0:T(8,128)S(1)}) custom-call(s32[1]{0:T(128)} %get-tuple-element.18.core_ref, bf16[16,18432]{1,0:T(8,128)(2,1)} %get-tuple-element.19.slices_hbm, bf16[768,1536]{1,0:T(8,128)(2,1)} %get-tuple-element.32.weights_hbm), custom_call_target="tpu_custom_call" | custom-call | tf_op jit(solution)/shard_map/cond/branch_1_fun/pallas_call | solution.py:105
  2.7 8.8 %collective-permute-start = (f32[8,1536]{1,0:T(8,128)S(1)}, f32[8,1536]{1,0:T(8,128)S(1)}, u32[]{:S(2)}, u32[]{:S(2)}) collective-permute-start(f32[8,1536]{1,0:T(8,128)S(1)} %get-tuple-element.26), channel_id=1, source_target_pairs={{0,1},{1,0},{2,3},{3,2},{4,5},{5,4},{6,7},{7,6},{8,9},{9,8},{10,11... | collective-permute-start | bytes 147464 | tf_op jit(solution)/shard_map/ppermute | solution.py:207
  11.6 0.1 and_select_fusion.1
  11.7 0.1 fusion.76
  11.7 0.6 %collective-permute-done = f32[8,1536]{1,0:T(8,128)S(1)} collective-permute-done((f32[8,1536]{1,0:T(8,128)S(1)}, f32[8,1536]{1,0:T(8,128)S(1)}, u32[]{:S(2)}, u32[]{:S(2)}) %collective-permute-start) | collective-permute-done | bytes 49184 | tf_op jit(solution)/shard_map/ppermute | solution.py:207
  12.4 0.1 multiply_reduce_fusion
  12.5 0.1 multiply_convert_fusion
  12.6 1.9 %collective-permute-start.2 = (bf16[8,1664]{1,0:T(8,128)(2,1)S(1)}, bf16[8,1664]{1,0:T(8,128)(2,1)S(1)}, u32[]{:S(2)}, u32[]{:S(2)}) collective-permute-start(bf16[8,1664]{1,0:T(8,128)(2,1)S(1)} %pad_maximum_fusion.1), channel_id=1, source_target_pairs={{0,272},{272,0},{16,256},{256,16},{1,273},{273,1},{17,257},{257,17... | collective-permute-start | bytes 79880 | tf_op jit(solution)/shard_map/ppermute | solution.py:221
  14.5 1.9 %collective-permute-start.1 = (bf16[8,1664]{1,0:T(8,128)(2,1)S(1)}, bf16[8,1664]{1,0:T(8,128)(2,1)S(1)}, u32[]{:S(2)}, u32[]{:S(2)}) collective-permute-start(bf16[8,1664]{1,0:T(8,128)(2,1)S(1)} %pad_maximum_fusion.1), channel_id=1, source_target_pairs={{0,256},{256,0},{1,257},{257,1},{2,258},{258,2},{3,259},{259,3},{4... | collective-permute-start | bytes 79880 | tf_op jit(solution)/shard_map/ppermute | solution.py:220
  17.2 7.7 %collective-permute-start.3 = (bf16[8,1664]{1,0:T(8,128)(2,1)S(1)}, bf16[8,1664]{1,0:T(8,128)(2,1)S(1)}, u32[]{:S(2)}, u32[]{:S(2)}) collective-permute-start(bf16[8,1664]{1,0:T(8,128)(2,1)S(1)} %pad_maximum_fusion.1), channel_id=1, source_target_pairs={{0,128},{32,160},{64,192},{96,224},{128,0},{160,32},{192,64},{224,... | collective-permute-start | bytes 79880 | tf_op jit(solution)/shard_map/ppermute | solution.py:134
  24.8 0.0 collective-permute-done.2
  24.8 0.0 collective-permute-done.1
  24.9 0.8 %broadcast_in_dim.48 = bf16[8,16,1664]{2,1,0:T(8,128)(2,1)} broadcast(bf16[16,1664]{1,0:T(8,128)(2,1)S(1)} %maximum_add_fusion), dimensions={1,2} | broadcast | bytes 479232 | tf_op jit(solution)/shard_map/broadcast_in_dim | solution.py:224
  25.7 8.9 %all-to-all-start = ((bf16[8,16,1664]{2,1,0:T(8,128)(2,1)}), bf16[8,16,1664]{2,1,0:T(8,128)(2,1)S(1)}, u32[]{:S(2)}, u32[]{:S(2)}) async-start(bf16[8,16,1664]{2,1,0:T(8,128)(2,1)} %broadcast_in_dim.48), calls=%async_computation | async-start | bytes 851968 | tf_op jit(solution)/shard_map/all_to_all | solution.py:122
  34.6 0.0 collective-permute-done.3
  34.7 4.0 %collective-permute-start.6 = (bf16[16,1664]{1,0:T(8,128)(2,1)S(1)}, bf16[16,1664]{1,0:T(8,128)(2,1)S(1)}, u32[]{:S(2)}, u32[]{:S(2)}) collective-permute-start(bf16[16,1664]{1,0:T(8,128)(2,1)S(1)} %broadcast_add_fusion), channel_id=1, source_target_pairs={{0,64},{32,96},{64,0},{96,32},{128,192},{160,224},{192,128},{224,1... | collective-permute-start | bytes 159752 | tf_op jit(solution)/shard_map/ppermute | solution.py:134
  38.7 1.9 %collective-permute-start.5 = (bf16[16,1664]{1,0:T(8,128)(2,1)S(1)}, bf16[16,1664]{1,0:T(8,128)(2,1)S(1)}, u32[]{:S(2)}, u32[]{:S(2)}) collective-permute-start(bf16[16,1664]{1,0:T(8,128)(2,1)S(1)} %broadcast_add_fusion), channel_id=1, source_target_pairs={{0,224},{32,64},{64,32},{96,128},{128,96},{160,192},{192,160},{224... | collective-permute-start | bytes 159752 | tf_op jit(solution)/shard_map/ppermute | solution.py:134
  40.7 3.1 %collective-permute-start.4 = (bf16[16,1664]{1,0:T(8,128)(2,1)S(1)}, bf16[16,1664]{1,0:T(8,128)(2,1)S(1)}, u32[]{:S(2)}, u32[]{:S(2)}) collective-permute-start(bf16[16,1664]{1,0:T(8,128)(2,1)S(1)} %broadcast_add_fusion), channel_id=1, source_target_pairs={{0,32},{32,0},{64,96},{96,64},{128,160},{160,128},{192,224},{224,1... | collective-permute-start | bytes 159752 | tf_op jit(solution)/shard_map/ppermute | solution.py:134
  44.5 2.4 %collective-permute-start.7 = (bf16[128,1664]{1,0:T(8,128)(2,1)S(1)}, bf16[128,1664]{1,0:T(8,128)(2,1)S(1)}, u32[]{:S(2)}, u32[]{:S(2)}) collective-permute-start(bf16[128,1664]{1,0:T(8,128)(2,1)S(1)} %bitcast.11), channel_id=1, source_target_pairs={{0,1},{1,0},{2,3},{3,2},{4,5},{5,4},{6,7},{7,6},{8,9},{9,8},{10,11... | collective-permute-start | bytes 1277960 | tf_op jit(solution)/shard_map/ppermute | solution.py:228
  46.9 0.3 convolution_convert_fusion
  47.2 0.3 fusion.1
  47.5 0.3 fusion.32
  47.8 0.2 fusion.5
  48.0 0.3 collective-permute-done.7
  48.2 0.3 fusion.2
  48.5 0.3 fusion.33
  48.8 0.1 select_convert_fusion
  48.9 0.2 fusion
  49.1 0.1 maximum_bitcast_fusion
  49.2 12.6 %all_to_all.10 = f16[8,8,1664]{2,1,0:T(8,128)(2,1)S(1)} all-to-all(f16[8,8,1664]{2,1,0:T(8,128)(2,1)S(1)} %maximum_bitcast_fusion), channel_id=1, replica_groups={{128,160,192,224,0,32,64,96},{193,225,1,33,65,97,129,161},{130,162,194,..., dimensions={0} | all-to-all | bytes 425984 | tf_op jit(solution)/shard_map/all_to_all | solution.py:122
  61.8 0.8 %shard_map.89 = (f32[1,8,1536]{2,1,0:T(8,128)}, f32[1,8]{1,0:T(1,128)}) custom-call(f32[1]{0:T(128)S(6)} %copy.18.scale_ref, f32[8,1664]{1,0:T(8,128)S(1)} %convert_reduce_fusion.total_ref, f32[8,1536]{1,0:T(8,128)S(1)} %get-tuple-element.34.embedding_ref), custom_call_target="tpu_custom_call" | custom-call | tf_op jit(solution)/shard_map/pallas_call | solution.py:261
  (21 shorter events, 0.2 us)
Async XLA Ops:
  0.6 10.9 %copy-start = (s32[16]{0:T(128)S(1)}, s32[16]{0:T(128)}, u32[]{:S(2)}) copy-start(s32[16]{0:T(128)} %param.13) | copy-start | bytes 196
  2.7 9.7 %collective-permute-start = (f32[8,1536]{1,0:T(8,128)S(1)}, f32[8,1536]{1,0:T(8,128)S(1)}, u32[]{:S(2)}, u32[]{:S(2)}) collective-permute-start(f32[8,1536]{1,0:T(8,128)S(1)} %get-tuple-element.26), channel_id=1, source_target_pairs={{0,1},{1,0},{2,3},{3,2},{4,5},{5,4},{6,7},{7,6},{8,9},{9,8},{10,11... | collective-permute-start | bytes 147464 | tf_op jit(solution)/shard_map/ppermute | solution.py:207
  12.6 12.2 %collective-permute-start.2 = (bf16[8,1664]{1,0:T(8,128)(2,1)S(1)}, bf16[8,1664]{1,0:T(8,128)(2,1)S(1)}, u32[]{:S(2)}, u32[]{:S(2)}) collective-permute-start(bf16[8,1664]{1,0:T(8,128)(2,1)S(1)} %pad_maximum_fusion.1), channel_id=1, source_target_pairs={{0,272},{272,0},{16,256},{256,16},{1,273},{273,1},{17,257},{257,17... | collective-permute-start | bytes 79880 | tf_op jit(solution)/shard_map/ppermute | solution.py:221
  14.5 10.3 %collective-permute-start.1 = (bf16[8,1664]{1,0:T(8,128)(2,1)S(1)}, bf16[8,1664]{1,0:T(8,128)(2,1)S(1)}, u32[]{:S(2)}, u32[]{:S(2)}) collective-permute-start(bf16[8,1664]{1,0:T(8,128)(2,1)S(1)} %pad_maximum_fusion.1), channel_id=1, source_target_pairs={{0,256},{256,0},{1,257},{257,1},{2,258},{258,2},{3,259},{259,3},{4... | collective-permute-start | bytes 79880 | tf_op jit(solution)/shard_map/ppermute | solution.py:220
  17.2 17.4 %collective-permute-start.3 = (bf16[8,1664]{1,0:T(8,128)(2,1)S(1)}, bf16[8,1664]{1,0:T(8,128)(2,1)S(1)}, u32[]{:S(2)}, u32[]{:S(2)}) collective-permute-start(bf16[8,1664]{1,0:T(8,128)(2,1)S(1)} %pad_maximum_fusion.1), channel_id=1, source_target_pairs={{0,128},{32,160},{64,192},{96,224},{128,0},{160,32},{192,64},{224,... | collective-permute-start | bytes 79880 | tf_op jit(solution)/shard_map/ppermute | solution.py:134
  25.7 18.8 %all-to-all-start = ((bf16[8,16,1664]{2,1,0:T(8,128)(2,1)}), bf16[8,16,1664]{2,1,0:T(8,128)(2,1)S(1)}, u32[]{:S(2)}, u32[]{:S(2)}) async-start(bf16[8,16,1664]{2,1,0:T(8,128)(2,1)} %broadcast_in_dim.48), calls=%async_computation | async-start | bytes 851968 | tf_op jit(solution)/shard_map/all_to_all | solution.py:122
  34.7 12.1 %collective-permute-start.6 = (bf16[16,1664]{1,0:T(8,128)(2,1)S(1)}, bf16[16,1664]{1,0:T(8,128)(2,1)S(1)}, u32[]{:S(2)}, u32[]{:S(2)}) collective-permute-start(bf16[16,1664]{1,0:T(8,128)(2,1)S(1)} %broadcast_add_fusion), channel_id=1, source_target_pairs={{0,64},{32,96},{64,0},{96,32},{128,192},{160,224},{192,128},{224,1... | collective-permute-start | bytes 159752 | tf_op jit(solution)/shard_map/ppermute | solution.py:134
  38.7 8.1 %collective-permute-start.5 = (bf16[16,1664]{1,0:T(8,128)(2,1)S(1)}, bf16[16,1664]{1,0:T(8,128)(2,1)S(1)}, u32[]{:S(2)}, u32[]{:S(2)}) collective-permute-start(bf16[16,1664]{1,0:T(8,128)(2,1)S(1)} %broadcast_add_fusion), channel_id=1, source_target_pairs={{0,224},{32,64},{64,32},{96,128},{128,96},{160,192},{192,160},{224... | collective-permute-start | bytes 159752 | tf_op jit(solution)/shard_map/ppermute | solution.py:134
  40.7 6.2 %collective-permute-start.4 = (bf16[16,1664]{1,0:T(8,128)(2,1)S(1)}, bf16[16,1664]{1,0:T(8,128)(2,1)S(1)}, u32[]{:S(2)}, u32[]{:S(2)}) collective-permute-start(bf16[16,1664]{1,0:T(8,128)(2,1)S(1)} %broadcast_add_fusion), channel_id=1, source_target_pairs={{0,32},{32,0},{64,96},{96,64},{128,160},{160,128},{192,224},{224,1... | collective-permute-start | bytes 159752 | tf_op jit(solution)/shard_map/ppermute | solution.py:134
  44.5 3.8 %collective-permute-start.7 = (bf16[128,1664]{1,0:T(8,128)(2,1)S(1)}, bf16[128,1664]{1,0:T(8,128)(2,1)S(1)}, u32[]{:S(2)}, u32[]{:S(2)}) collective-permute-start(bf16[128,1664]{1,0:T(8,128)(2,1)S(1)} %bitcast.11), channel_id=1, source_target_pairs={{0,1},{1,0},{2,3},{3,2},{4,5},{5,4},{6,7},{7,6},{8,9},{9,8},{10,11... | collective-permute-start | bytes 1277960 | tf_op jit(solution)/shard_map/ppermute | solution.py:228

commit v9 on v7

--- a/solution.py
+++ b/solution.py
@@ -209,8 +209,8 @@
 
     near = lax.ppermute(own, "tower", [(0, 1), (1, 0)])
     across = lax.ppermute(own, ("tower", "x"), [(0, 3), (3, 0), (1, 2), (2, 1)])
-    temper = jnp.exp(log_scale[0])
-    other = jnp.concatenate([near, across], axis=0) + (temper * 0).astype(near.dtype)
+    temper, offset = jnp.exp(log_scale[0]), bias[0]
+    other = jnp.concatenate([near, across], axis=0) + ((temper + offset) * 0).astype(near.dtype)
     copies = jnp.broadcast_to(other[None], (n_y,) + other.shape)
     held = swap_gather(own, "z")
     other_mine = staggered(copies, "y", FIRST_Y)
@@ -227,7 +227,7 @@
 
     def score(others):
         other_low = others[:, :width]
-        logits = temper * products(own_low, other_low) + bias[0]
+        logits = temper * products(own_low, other_low) + offset
         paired = products(own_all[:, width:], others[:, width:]) > 1.5
         losses = jax.nn.softplus(jnp.where(paired, -logits, logits))
         weights = (jax.nn.sigmoid(logits) - paired.astype(jnp.float32)).astype(jnp.bfloat16)

time: 64 us -> 64.2 us (level)
    ppermute x4, waiting for transfers between devices: 0.14 us -> 0.79 us  [brought(): lax.ppermute(value, axis, [(index, index ^ across) for index in range(mem...]
  transfers between devices with their start and end apart: 9 -> 9, of which waited for: 3 -> 2; matrix products, arithmetic and copies ran while one was open for 3% -> 3% of each run, Pallas kernels for 0% -> 0%
where the time goes in v9:
time: 64.2 us; the launch traced here: 63.7 us
  starting transfers between devices  41.2 us (64%)
  blocking collectives  12.6 us (20%)
  Pallas kernels  2.89 us (5%)
  between operations  2.27 us (4%)
  matrix products  1.77 us (3%)
  waiting for transfers between devices  1.45 us (2%)
  local copies, waits for them, and re-layouts  0.79 us (1%)
  other arithmetic  0.71 us (1%)
    ppermute x4, starting transfers between devices, brought(): lax.ppermute(value, axis, [(index, index ^ across) for index in range(mem...  16.9 us
    all_to_all x1, blocking collectives, staggered(): lax.all_to_all(blocks, (axis, 'mp'), 0, 0, axis_index_groups=groups, tile...  12.6 us
    all_to_all x1, starting transfers between devices, staggered(): lax.all_to_all(blocks, (axis, 'mp'), 0, 0, axis_index_groups=groups, tile...  8.93 us
    ppermute x1, starting transfers between devices, shards(): embedding = kept + lax.ppermute(sent, 'mp', [(0, 1), (1, 0)])  8.79 us
    ppermute x1, starting transfers between devices, shards(): other_theirs = lax.ppermute(other_mine, 'mp', [(0, 1), (1, 0)])  2.67 us
    pallas_call x1, Pallas kernels, pooled_partial(): pl.pallas_call(kernel, out_shape=(half, half), in_specs=[pl.BlockSpec(mem...  2.05 us
    ppermute x1, starting transfers between devices, shards(): near = lax.ppermute(own, 'tower', [(0, 1), (1, 0)])  1.92 us
    ppermute x1, starting transfers between devices, shards(): across = lax.ppermute(own, ('tower', 'x'), [(0, 3), (3, 0), (1, 2), (2, 1)])  1.92 us
  transfers between devices with their start and end apart: 9, of which 2 were waited for; matrix products, arithmetic and copies ran while one was open for 3% of the time, Pallas kernels for 0%

profile of v9, /device:TPU:1, one launch (start us, length us, event | category | flops | bytes accessed | tf_op | source)
XLA Modules:
  0.0 63.7 jit_solution(13304342369242053233)
XLA Ops:
  0.6 2.1 %conditional.1 = ((f32[8,1536]{1,0:T(8,128)S(1)}, f32[8,1536]{1,0:T(8,128)S(1)})) conditional(s32[]{:T(128)} %convert_element_type.51, (s32[1]{0:T(128)}, s32[16]{0:T(128)}, bf16[16,18432]{1,0:T(8,128)(2,1)}, bf16[576,1536]{1,0:T(8,128)(2,1)}) %tuple.27, (s32[1]{0:T(128)}, bf16[16,18432]{1,0:T(8,128)(2,1)}, bf16[768,1536]{1,0:T(8,128)(2,1)}) %tuple.28), branch_computations={%region_0.0_spmd, %region_1.0_spmd} | conditional | bytes 8 | solution.py:192
  0.7 2.1 %branch_1_fun.1 = (f32[8,1536]{1,0:T(8,128)S(1)}, f32[8,1536]{1,0:T(8,128)S(1)}) custom-call(s32[1]{0:T(128)} %get-tuple-element.18.core_ref, bf16[16,18432]{1,0:T(8,128)(2,1)} %get-tuple-element.19.slices_hbm, bf16[768,1536]{1,0:T(8,128)(2,1)} %get-tuple-element.32.weights_hbm), custom_call_target="tpu_custom_call" | custom-call | tf_op jit(solution)/shard_map/cond/branch_1_fun/pallas_call | solution.py:105
  2.7 8.8 %collective-permute-start = (f32[8,1536]{1,0:T(8,128)S(1)}, f32[8,1536]{1,0:T(8,128)S(1)}, u32[]{:S(2)}, u32[]{:S(2)}) collective-permute-start(f32[8,1536]{1,0:T(8,128)S(1)} %get-tuple-element.26), channel_id=1, source_target_pairs={{0,1},{1,0},{2,3},{3,2},{4,5},{5,4},{6,7},{7,6},{8,9},{9,8},{10,11... | collective-permute-start | bytes 147464 | tf_op jit(solution)/shard_map/ppermute | solution.py:197
  11.6 0.1 and_select_fusion.1
  11.7 0.1 fusion.73
  11.7 0.6 %collective-permute-done = f32[8,1536]{1,0:T(8,128)S(1)} collective-permute-done((f32[8,1536]{1,0:T(8,128)S(1)}, f32[8,1536]{1,0:T(8,128)S(1)}, u32[]{:S(2)}, u32[]{:S(2)}) %collective-permute-start) | collective-permute-done | bytes 49184 | tf_op jit(solution)/shard_map/ppermute | solution.py:197
  12.4 0.1 multiply_reduce_fusion
  12.5 0.1 multiply_convert_fusion
  12.6 1.9 %collective-permute-start.2 = (bf16[8,1664]{1,0:T(8,128)(2,1)S(1)}, bf16[8,1664]{1,0:T(8,128)(2,1)S(1)}, u32[]{:S(2)}, u32[]{:S(2)}) collective-permute-start(bf16[8,1664]{1,0:T(8,128)(2,1)S(1)} %pad_maximum_fusion.1), channel_id=1, source_target_pairs={{0,272},{272,0},{16,256},{256,16},{1,273},{273,1},{17,257},{257,17... | collective-permute-start | bytes 79880 | tf_op jit(solution)/shard_map/ppermute | solution.py:211
  14.5 1.9 %collective-permute-start.1 = (bf16[8,1664]{1,0:T(8,128)(2,1)S(1)}, bf16[8,1664]{1,0:T(8,128)(2,1)S(1)}, u32[]{:S(2)}, u32[]{:S(2)}) collective-permute-start(bf16[8,1664]{1,0:T(8,128)(2,1)S(1)} %pad_maximum_fusion.1), channel_id=1, source_target_pairs={{0,256},{256,0},{1,257},{257,1},{2,258},{258,2},{3,259},{259,3},{4... | collective-permute-start | bytes 79880 | tf_op jit(solution)/shard_map/ppermute | solution.py:210
  17.8 7.7 %collective-permute-start.3 = (bf16[8,1664]{1,0:T(8,128)(2,1)S(1)}, bf16[8,1664]{1,0:T(8,128)(2,1)S(1)}, u32[]{:S(2)}, u32[]{:S(2)}) collective-permute-start(bf16[8,1664]{1,0:T(8,128)(2,1)S(1)} %pad_maximum_fusion.1), channel_id=1, source_target_pairs={{0,128},{32,160},{64,192},{96,224},{128,0},{160,32},{192,64},{224,... | collective-permute-start | bytes 79880 | tf_op jit(solution)/shard_map/ppermute | solution.py:130
  25.5 0.0 collective-permute-done.1
  25.5 0.8 %broadcast_in_dim.12 = bf16[8,16,1664]{2,1,0:T(8,128)(2,1)} broadcast(bf16[16,1664]{1,0:T(8,128)(2,1)S(1)} %maximum_add_fusion), dimensions={1,2} | broadcast | bytes 479232 | tf_op jit(solution)/shard_map/broadcast_in_dim | solution.py:214
  26.3 8.9 %all-to-all-start = ((bf16[8,16,1664]{2,1,0:T(8,128)(2,1)}), bf16[8,16,1664]{2,1,0:T(8,128)(2,1)S(1)}, u32[]{:S(2)}, u32[]{:S(2)}) async-start(bf16[8,16,1664]{2,1,0:T(8,128)(2,1)} %broadcast_in_dim.12), calls=%async_computation | async-start | bytes 851968 | tf_op jit(solution)/shard_map/all_to_all | solution.py:122
  35.2 0.0 collective-permute-done.3
  35.4 4.9 %collective-permute-start.6 = (bf16[16,1664]{1,0:T(8,128)(2,1)S(1)}, bf16[16,1664]{1,0:T(8,128)(2,1)S(1)}, u32[]{:S(2)}, u32[]{:S(2)}) collective-permute-start(bf16[16,1664]{1,0:T(8,128)(2,1)S(1)} %broadcast_add_fusion), channel_id=1, source_target_pairs={{0,96},{32,64},{64,32},{96,0},{128,224},{160,192},{192,160},{224,1... | collective-permute-start | bytes 159752 | tf_op jit(solution)/shard_map/ppermute | solution.py:130
  40.3 1.9 %collective-permute-start.5 = (bf16[16,1664]{1,0:T(8,128)(2,1)S(1)}, bf16[16,1664]{1,0:T(8,128)(2,1)S(1)}, u32[]{:S(2)}, u32[]{:S(2)}) collective-permute-start(bf16[16,1664]{1,0:T(8,128)(2,1)S(1)} %broadcast_add_fusion), channel_id=1, source_target_pairs={{0,64},{32,96},{64,0},{96,32},{128,192},{160,224},{192,128},{224,1... | collective-permute-start | bytes 159752 | tf_op jit(solution)/shard_map/ppermute | solution.py:130
  42.2 2.4 %collective-permute-start.4 = (bf16[16,1664]{1,0:T(8,128)(2,1)S(1)}, bf16[16,1664]{1,0:T(8,128)(2,1)S(1)}, u32[]{:S(2)}, u32[]{:S(2)}) collective-permute-start(bf16[16,1664]{1,0:T(8,128)(2,1)S(1)} %broadcast_add_fusion), channel_id=1, source_target_pairs={{0,32},{32,0},{64,96},{96,64},{128,160},{160,128},{192,224},{224,1... | collective-permute-start | bytes 159752 | tf_op jit(solution)/shard_map/ppermute | solution.py:130
  44.7 2.7 %collective-permute-start.7 = (bf16[128,1664]{1,0:T(8,128)(2,1)S(1)}, bf16[128,1664]{1,0:T(8,128)(2,1)S(1)}, u32[]{:S(2)}, u32[]{:S(2)}) collective-permute-start(bf16[128,1664]{1,0:T(8,128)(2,1)S(1)} %bitcast.12), channel_id=1, source_target_pairs={{0,1},{1,0},{2,3},{3,2},{4,5},{5,4},{6,7},{7,6},{8,9},{9,8},{10,11... | collective-permute-start | bytes 1277960 | tf_op jit(solution)/shard_map/ppermute | solution.py:218
  47.4 0.0 collective-permute-done.6
  47.4 0.8 %collective-permute-done.4 = bf16[16,1664]{1,0:T(8,128)(2,1)S(1)} collective-permute-done((bf16[16,1664]{1,0:T(8,128)(2,1)S(1)}, bf16[16,1664]{1,0:T(8,128)(2,1)S(1)}, u32[]{:S(2)}, u32[]{:S(2)}) %collective-permute-start.4) | collective-permute-done | bytes 53280 | tf_op jit(solution)/shard_map/ppermute | solution.py:130
  48.2 0.3 convolution_convert_fusion
  48.5 0.3 fusion.1
  48.7 0.3 fusion.33
  49.0 0.2 fusion.5
  49.2 0.3 fusion.2
  49.5 0.3 fusion.34
  49.8 0.1 select_convert_fusion
  49.9 0.2 fusion
  50.1 0.1 maximum_bitcast_fusion
  50.2 12.6 %all_to_all.10 = f16[8,8,1664]{2,1,0:T(8,128)(2,1)S(1)} all-to-all(f16[8,8,1664]{2,1,0:T(8,128)(2,1)S(1)} %maximum_bitcast_fusion), channel_id=1, replica_groups={{128,160,192,224,0,32,64,96},{193,225,1,33,65,97,129,161},{130,162,194,..., dimensions={0} | all-to-all | bytes 425984 | tf_op jit(solution)/shard_map/all_to_all | solution.py:122
  62.8 0.8 %shard_map.89 = (f32[1,8,1536]{2,1,0:T(8,128)}, f32[1,8]{1,0:T(1,128)}) custom-call(f32[1]{0:T(128)S(6)} %copy.18.scale_ref, f32[8,1664]{1,0:T(8,128)S(1)} %convert_reduce_fusion.total_ref, f32[8,1536]{1,0:T(8,128)S(1)} %get-tuple-element.34.embedding_ref), custom_call_target="tpu_custom_call" | custom-call | tf_op jit(solution)/shard_map/pallas_call | solution.py:251
  (21 shorter events, 0.2 us)
Async XLA Ops:
  0.6 10.9 %copy-start = (s32[16]{0:T(128)S(1)}, s32[16]{0:T(128)}, u32[]{:S(2)}) copy-start(s32[16]{0:T(128)} %param.13) | copy-start | bytes 196
  2.7 9.7 %collective-permute-start = (f32[8,1536]{1,0:T(8,128)S(1)}, f32[8,1536]{1,0:T(8,128)S(1)}, u32[]{:S(2)}, u32[]{:S(2)}) collective-permute-start(f32[8,1536]{1,0:T(8,128)S(1)} %get-tuple-element.26), channel_id=1, source_target_pairs={{0,1},{1,0},{2,3},{3,2},{4,5},{5,4},{6,7},{7,6},{8,9},{9,8},{10,11... | collective-permute-start | bytes 147464 | tf_op jit(solution)/shard_map/ppermute | solution.py:197
  12.6 12.9 %collective-permute-start.2 = (bf16[8,1664]{1,0:T(8,128)(2,1)S(1)}, bf16[8,1664]{1,0:T(8,128)(2,1)S(1)}, u32[]{:S(2)}, u32[]{:S(2)}) collective-permute-start(bf16[8,1664]{1,0:T(8,128)(2,1)S(1)} %pad_maximum_fusion.1), channel_id=1, source_target_pairs={{0,272},{272,0},{16,256},{256,16},{1,273},{273,1},{17,257},{257,17... | collective-permute-start | bytes 79880 | tf_op jit(solution)/shard_map/ppermute | solution.py:211
  14.5 11.0 %collective-permute-start.1 = (bf16[8,1664]{1,0:T(8,128)(2,1)S(1)}, bf16[8,1664]{1,0:T(8,128)(2,1)S(1)}, u32[]{:S(2)}, u32[]{:S(2)}) collective-permute-start(bf16[8,1664]{1,0:T(8,128)(2,1)S(1)} %pad_maximum_fusion.1), channel_id=1, source_target_pairs={{0,256},{256,0},{1,257},{257,1},{2,258},{258,2},{3,259},{259,3},{4... | collective-permute-start | bytes 79880 | tf_op jit(solution)/shard_map/ppermute | solution.py:210
  17.8 17.4 %collective-permute-start.3 = (bf16[8,1664]{1,0:T(8,128)(2,1)S(1)}, bf16[8,1664]{1,0:T(8,128)(2,1)S(1)}, u32[]{:S(2)}, u32[]{:S(2)}) collective-permute-start(bf16[8,1664]{1,0:T(8,128)(2,1)S(1)} %pad_maximum_fusion.1), channel_id=1, source_target_pairs={{0,128},{32,160},{64,192},{96,224},{128,0},{160,32},{192,64},{224,... | collective-permute-start | bytes 79880 | tf_op jit(solution)/shard_map/ppermute | solution.py:130
  26.3 18.4 %all-to-all-start = ((bf16[8,16,1664]{2,1,0:T(8,128)(2,1)}), bf16[8,16,1664]{2,1,0:T(8,128)(2,1)S(1)}, u32[]{:S(2)}, u32[]{:S(2)}) async-start(bf16[8,16,1664]{2,1,0:T(8,128)(2,1)} %broadcast_in_dim.12), calls=%async_computation | async-start | bytes 851968 | tf_op jit(solution)/shard_map/all_to_all | solution.py:122
  35.4 12.0 %collective-permute-start.6 = (bf16[16,1664]{1,0:T(8,128)(2,1)S(1)}, bf16[16,1664]{1,0:T(8,128)(2,1)S(1)}, u32[]{:S(2)}, u32[]{:S(2)}) collective-permute-start(bf16[16,1664]{1,0:T(8,128)(2,1)S(1)} %broadcast_add_fusion), channel_id=1, source_target_pairs={{0,96},{32,64},{64,32},{96,0},{128,224},{160,192},{192,160},{224,1... | collective-permute-start | bytes 159752 | tf_op jit(solution)/shard_map/ppermute | solution.py:130
  40.3 7.1 %collective-permute-start.5 = (bf16[16,1664]{1,0:T(8,128)(2,1)S(1)}, bf16[16,1664]{1,0:T(8,128)(2,1)S(1)}, u32[]{:S(2)}, u32[]{:S(2)}) collective-permute-start(bf16[16,1664]{1,0:T(8,128)(2,1)S(1)} %broadcast_add_fusion), channel_id=1, source_target_pairs={{0,64},{32,96},{64,0},{96,32},{128,192},{160,224},{192,128},{224,1... | collective-permute-start | bytes 159752 | tf_op jit(solution)/shard_map/ppermute | solution.py:130
  42.2 5.9 %collective-permute-start.4 = (bf16[16,1664]{1,0:T(8,128)(2,1)S(1)}, bf16[16,1664]{1,0:T(8,128)(2,1)S(1)}, u32[]{:S(2)}, u32[]{:S(2)}) collective-permute-start(bf16[16,1664]{1,0:T(8,128)(2,1)S(1)} %broadcast_add_fusion), channel_id=1, source_target_pairs={{0,32},{32,0},{64,96},{96,64},{128,160},{160,128},{192,224},{224,1... | collective-permute-start | bytes 159752 | tf_op jit(solution)/shard_map/ppermute | solution.py:130
  44.7 4.5 %collective-permute-start.7 = (bf16[128,1664]{1,0:T(8,128)(2,1)S(1)}, bf16[128,1664]{1,0:T(8,128)(2,1)S(1)}, u32[]{:S(2)}, u32[]{:S(2)}) collective-permute-start(bf16[128,1664]{1,0:T(8,128)(2,1)S(1)} %bitcast.12), channel_id=1, source_target_pairs={{0,1},{1,0},{2,3},{3,2},{4,5},{5,4},{6,7},{7,6},{8,9},{9,8},{10,11... | collective-permute-start | bytes 1277960 | tf_op jit(solution)/shard_map/ppermute | solution.py:218

commit v10 on v7

--- a/solution.py
+++ b/solution.py
@@ -12,7 +12,7 @@
 HIGH, LOW = 64, 32
 SUMS = 3
 FIRST_Y = (7, 4)
-FIRST_Z = (4, 6)
+FIRST_Z = (4, 7)
 
 
 def project(pooled, weights, copies, core_ref, keep_ref, send_ref):

time: 64 us -> 64 us (level)
  no operation moved by 1% of the time
where the time goes in v10:
time: 64 us; the launch traced here: 63.5 us
  starting transfers between devices  41.2 us (64%)
  blocking collectives  12.9 us (20%)
  Pallas kernels  2.89 us (5%)
  between operations  2.26 us (4%)
  matrix products  1.76 us (3%)
  waiting for transfers between devices  0.96 us (2%)
  local copies, waits for them, and re-layouts  0.79 us (1%)
  other arithmetic  0.71 us (1%)
    ppermute x4, starting transfers between devices, brought(): lax.ppermute(value, axis, [(index, index ^ across) for index in range(mem...  16.9 us
    all_to_all x1, blocking collectives, staggered(): lax.all_to_all(blocks, (axis, 'mp'), 0, 0, axis_index_groups=groups, tile...  12.9 us
    all_to_all x1, starting transfers between devices, staggered(): lax.all_to_all(blocks, (axis, 'mp'), 0, 0, axis_index_groups=groups, tile...  8.93 us
    ppermute x1, starting transfers between devices, shards(): embedding = kept + lax.ppermute(sent, 'mp', [(0, 1), (1, 0)])  8.79 us
    ppermute x1, starting transfers between devices, shards(): other_theirs = lax.ppermute(other_mine, 'mp', [(0, 1), (1, 0)])  2.67 us
    pallas_call x1, Pallas kernels, pooled_partial(): pl.pallas_call(kernel, out_shape=(half, half), in_specs=[pl.BlockSpec(mem...  2.05 us
    ppermute x1, starting transfers between devices, shards(): near = lax.ppermute(own, 'tower', [(0, 1), (1, 0)])  1.92 us
    ppermute x1, starting transfers between devices, shards(): across = lax.ppermute(own, ('tower', 'x'), [(0, 3), (3, 0), (1, 2), (2, 1)])  1.92 us
  transfers between devices with their start and end apart: 9, of which 3 were waited for; matrix products, arithmetic and copies ran while one was open for 3% of the time, Pallas kernels for 0%

profile of v10, /device:TPU:1, one launch (start us, length us, event | category | flops | bytes accessed | tf_op | source)
XLA Modules:
  0.0 63.5 jit_solution(10850687192680472478)
XLA Ops:
  0.6 2.1 %conditional.1 = ((f32[8,1536]{1,0:T(8,128)S(1)}, f32[8,1536]{1,0:T(8,128)S(1)})) conditional(s32[]{:T(128)} %convert_element_type.51, (s32[1]{0:T(128)}, s32[16]{0:T(128)}, bf16[16,18432]{1,0:T(8,128)(2,1)}, bf16[576,1536]{1,0:T(8,128)(2,1)}) %tuple.27, (s32[1]{0:T(128)}, bf16[16,18432]{1,0:T(8,128)(2,1)}, bf16[768,1536]{1,0:T(8,128)(2,1)}) %tuple.28), branch_computations={%region_0.0_spmd, %region_1.0_spmd} | conditional | bytes 8 | solution.py:192
  0.7 2.1 %branch_1_fun.1 = (f32[8,1536]{1,0:T(8,128)S(1)}, f32[8,1536]{1,0:T(8,128)S(1)}) custom-call(s32[1]{0:T(128)} %get-tuple-element.18.core_ref, bf16[16,18432]{1,0:T(8,128)(2,1)} %get-tuple-element.19.slices_hbm, bf16[768,1536]{1,0:T(8,128)(2,1)} %get-tuple-element.32.weights_hbm), custom_call_target="tpu_custom_call" | custom-call | tf_op jit(solution)/shard_map/cond/branch_1_fun/pallas_call | solution.py:105
  2.7 8.8 %collective-permute-start = (f32[8,1536]{1,0:T(8,128)S(1)}, f32[8,1536]{1,0:T(8,128)S(1)}, u32[]{:S(2)}, u32[]{:S(2)}) collective-permute-start(f32[8,1536]{1,0:T(8,128)S(1)} %get-tuple-element.26), channel_id=1, source_target_pairs={{0,1},{1,0},{2,3},{3,2},{4,5},{5,4},{6,7},{7,6},{8,9},{9,8},{10,11... | collective-permute-start | bytes 147464 | tf_op jit(solution)/shard_map/ppermute | solution.py:197
  11.6 0.1 and_select_fusion.1
  11.7 0.1 fusion.73
  11.7 0.6 %collective-permute-done = f32[8,1536]{1,0:T(8,128)S(1)} collective-permute-done((f32[8,1536]{1,0:T(8,128)S(1)}, f32[8,1536]{1,0:T(8,128)S(1)}, u32[]{:S(2)}, u32[]{:S(2)}) %collective-permute-start) | collective-permute-done | bytes 49184 | tf_op jit(solution)/shard_map/ppermute | solution.py:197
  12.4 0.1 multiply_reduce_fusion
  12.5 0.1 multiply_convert_fusion
  12.6 1.9 %collective-permute-start.2 = (bf16[8,1664]{1,0:T(8,128)(2,1)S(1)}, bf16[8,1664]{1,0:T(8,128)(2,1)S(1)}, u32[]{:S(2)}, u32[]{:S(2)}) collective-permute-start(bf16[8,1664]{1,0:T(8,128)(2,1)S(1)} %pad_maximum_fusion.1), channel_id=1, source_target_pairs={{0,272},{272,0},{16,256},{256,16},{1,273},{273,1},{17,257},{257,17... | collective-permute-start | bytes 79880 | tf_op jit(solution)/shard_map/ppermute | solution.py:211
  14.5 1.9 %collective-permute-start.1 = (bf16[8,1664]{1,0:T(8,128)(2,1)S(1)}, bf16[8,1664]{1,0:T(8,128)(2,1)S(1)}, u32[]{:S(2)}, u32[]{:S(2)}) collective-permute-start(bf16[8,1664]{1,0:T(8,128)(2,1)S(1)} %pad_maximum_fusion.1), channel_id=1, source_target_pairs={{0,256},{256,0},{1,257},{257,1},{2,258},{258,2},{3,259},{259,3},{4... | collective-permute-start | bytes 79880 | tf_op jit(solution)/shard_map/ppermute | solution.py:210
  17.2 7.7 %collective-permute-start.3 = (bf16[8,1664]{1,0:T(8,128)(2,1)S(1)}, bf16[8,1664]{1,0:T(8,128)(2,1)S(1)}, u32[]{:S(2)}, u32[]{:S(2)}) collective-permute-start(bf16[8,1664]{1,0:T(8,128)(2,1)S(1)} %pad_maximum_fusion.1), channel_id=1, source_target_pairs={{0,128},{32,160},{64,192},{96,224},{128,0},{160,32},{192,64},{224,... | collective-permute-start | bytes 79880 | tf_op jit(solution)/shard_map/ppermute | solution.py:130
  24.8 0.0 collective-permute-done.2
  24.8 0.0 collective-permute-done.1
  24.9 0.8 %broadcast_in_dim.12 = bf16[8,16,1664]{2,1,0:T(8,128)(2,1)} broadcast(bf16[16,1664]{1,0:T(8,128)(2,1)S(1)} %maximum_add_fusion), dimensions={1,2} | broadcast | bytes 479232 | tf_op jit(solution)/shard_map/broadcast_in_dim | solution.py:214
  25.7 8.9 %all-to-all-start = ((bf16[8,16,1664]{2,1,0:T(8,128)(2,1)}), bf16[8,16,1664]{2,1,0:T(8,128)(2,1)S(1)}, u32[]{:S(2)}, u32[]{:S(2)}) async-start(bf16[8,16,1664]{2,1,0:T(8,128)(2,1)} %broadcast_in_dim.12), calls=%async_computation | async-start | bytes 851968 | tf_op jit(solution)/shard_map/all_to_all | solution.py:122
  34.7 4.9 %collective-permute-start.6 = (bf16[16,1664]{1,0:T(8,128)(2,1)S(1)}, bf16[16,1664]{1,0:T(8,128)(2,1)S(1)}, u32[]{:S(2)}, u32[]{:S(2)}) collective-permute-start(bf16[16,1664]{1,0:T(8,128)(2,1)S(1)} %broadcast_add_fusion), channel_id=1, source_target_pairs={{0,96},{32,64},{64,32},{96,0},{128,224},{160,192},{192,160},{224,1... | collective-permute-start | bytes 159752 | tf_op jit(solution)/shard_map/ppermute | solution.py:130
  39.7 1.9 %collective-permute-start.5 = (bf16[16,1664]{1,0:T(8,128)(2,1)S(1)}, bf16[16,1664]{1,0:T(8,128)(2,1)S(1)}, u32[]{:S(2)}, u32[]{:S(2)}) collective-permute-start(bf16[16,1664]{1,0:T(8,128)(2,1)S(1)} %broadcast_add_fusion), channel_id=1, source_target_pairs={{0,64},{32,96},{64,0},{96,32},{128,192},{160,224},{192,128},{224,1... | collective-permute-start | bytes 159752 | tf_op jit(solution)/shard_map/ppermute | solution.py:130
  41.6 2.4 %collective-permute-start.4 = (bf16[16,1664]{1,0:T(8,128)(2,1)S(1)}, bf16[16,1664]{1,0:T(8,128)(2,1)S(1)}, u32[]{:S(2)}, u32[]{:S(2)}) collective-permute-start(bf16[16,1664]{1,0:T(8,128)(2,1)S(1)} %broadcast_add_fusion), channel_id=1, source_target_pairs={{0,32},{32,0},{64,96},{96,64},{128,160},{160,128},{192,224},{224,1... | collective-permute-start | bytes 159752 | tf_op jit(solution)/shard_map/ppermute | solution.py:130
  44.7 2.7 %collective-permute-start.7 = (bf16[128,1664]{1,0:T(8,128)(2,1)S(1)}, bf16[128,1664]{1,0:T(8,128)(2,1)S(1)}, u32[]{:S(2)}, u32[]{:S(2)}) collective-permute-start(bf16[128,1664]{1,0:T(8,128)(2,1)S(1)} %bitcast.11), channel_id=1, source_target_pairs={{0,1},{1,0},{2,3},{3,2},{4,5},{5,4},{6,7},{7,6},{8,9},{9,8},{10,11... | collective-permute-start | bytes 1277960 | tf_op jit(solution)/shard_map/ppermute | solution.py:218
  47.4 0.1 collective-permute-done.4
  47.5 0.3 convolution_convert_fusion
  47.8 0.3 fusion.1
  48.1 0.3 fusion.33
  48.4 0.2 fusion.5
  48.6 0.2 collective-permute-done.7
  48.8 0.3 fusion.2
  49.0 0.3 fusion.34
  49.3 0.1 select_convert_fusion
  49.4 0.2 fusion
  49.6 0.1 maximum_bitcast_fusion
  49.7 12.9 %all_to_all.10 = f16[8,8,1664]{2,1,0:T(8,128)(2,1)S(1)} all-to-all(f16[8,8,1664]{2,1,0:T(8,128)(2,1)S(1)} %maximum_bitcast_fusion), channel_id=1, replica_groups={{128,160,192,224,0,32,64,96},{225,1,33,65,97,129,161,193},{130,162,194,..., dimensions={0} | all-to-all | bytes 425984 | tf_op jit(solution)/shard_map/all_to_all | solution.py:122
  62.7 0.8 %shard_map.89 = (f32[1,8,1536]{2,1,0:T(8,128)}, f32[1,8]{1,0:T(1,128)}) custom-call(f32[1]{0:T(128)S(6)} %copy.18.scale_ref, f32[8,1664]{1,0:T(8,128)S(1)} %convert_reduce_fusion.total_ref, f32[8,1536]{1,0:T(8,128)S(1)} %get-tuple-element.34.embedding_ref), custom_call_target="tpu_custom_call" | custom-call | tf_op jit(solution)/shard_map/pallas_call | solution.py:251
  (21 shorter events, 0.2 us)
Async XLA Ops:
  0.6 10.9 %copy-start = (s32[16]{0:T(128)S(1)}, s32[16]{0:T(128)}, u32[]{:S(2)}) copy-start(s32[16]{0:T(128)} %param.13) | copy-start | bytes 196
  2.7 9.7 %collective-permute-start = (f32[8,1536]{1,0:T(8,128)S(1)}, f32[8,1536]{1,0:T(8,128)S(1)}, u32[]{:S(2)}, u32[]{:S(2)}) collective-permute-start(f32[8,1536]{1,0:T(8,128)S(1)} %get-tuple-element.26), channel_id=1, source_target_pairs={{0,1},{1,0},{2,3},{3,2},{4,5},{5,4},{6,7},{7,6},{8,9},{9,8},{10,11... | collective-permute-start | bytes 147464 | tf_op jit(solution)/shard_map/ppermute | solution.py:197
  12.6 12.2 %collective-permute-start.2 = (bf16[8,1664]{1,0:T(8,128)(2,1)S(1)}, bf16[8,1664]{1,0:T(8,128)(2,1)S(1)}, u32[]{:S(2)}, u32[]{:S(2)}) collective-permute-start(bf16[8,1664]{1,0:T(8,128)(2,1)S(1)} %pad_maximum_fusion.1), channel_id=1, source_target_pairs={{0,272},{272,0},{16,256},{256,16},{1,273},{273,1},{17,257},{257,17... | collective-permute-start | bytes 79880 | tf_op jit(solution)/shard_map/ppermute | solution.py:211
  14.5 10.3 %collective-permute-start.1 = (bf16[8,1664]{1,0:T(8,128)(2,1)S(1)}, bf16[8,1664]{1,0:T(8,128)(2,1)S(1)}, u32[]{:S(2)}, u32[]{:S(2)}) collective-permute-start(bf16[8,1664]{1,0:T(8,128)(2,1)S(1)} %pad_maximum_fusion.1), channel_id=1, source_target_pairs={{0,256},{256,0},{1,257},{257,1},{2,258},{258,2},{3,259},{259,3},{4... | collective-permute-start | bytes 79880 | tf_op jit(solution)/shard_map/ppermute | solution.py:210
  17.2 17.4 %collective-permute-start.3 = (bf16[8,1664]{1,0:T(8,128)(2,1)S(1)}, bf16[8,1664]{1,0:T(8,128)(2,1)S(1)}, u32[]{:S(2)}, u32[]{:S(2)}) collective-permute-start(bf16[8,1664]{1,0:T(8,128)(2,1)S(1)} %pad_maximum_fusion.1), channel_id=1, source_target_pairs={{0,128},{32,160},{64,192},{96,224},{128,0},{160,32},{192,64},{224,... | collective-permute-start | bytes 79880 | tf_op jit(solution)/shard_map/ppermute | solution.py:130
  25.7 19.0 %all-to-all-start = ((bf16[8,16,1664]{2,1,0:T(8,128)(2,1)}), bf16[8,16,1664]{2,1,0:T(8,128)(2,1)S(1)}, u32[]{:S(2)}, u32[]{:S(2)}) async-start(bf16[8,16,1664]{2,1,0:T(8,128)(2,1)} %broadcast_in_dim.12), calls=%async_computation | async-start | bytes 851968 | tf_op jit(solution)/shard_map/all_to_all | solution.py:122
  34.7 12.7 %collective-permute-start.6 = (bf16[16,1664]{1,0:T(8,128)(2,1)S(1)}, bf16[16,1664]{1,0:T(8,128)(2,1)S(1)}, u32[]{:S(2)}, u32[]{:S(2)}) collective-permute-start(bf16[16,1664]{1,0:T(8,128)(2,1)S(1)} %broadcast_add_fusion), channel_id=1, source_target_pairs={{0,96},{32,64},{64,32},{96,0},{128,224},{160,192},{192,160},{224,1... | collective-permute-start | bytes 159752 | tf_op jit(solution)/shard_map/ppermute | solution.py:130
  39.7 7.7 %collective-permute-start.5 = (bf16[16,1664]{1,0:T(8,128)(2,1)S(1)}, bf16[16,1664]{1,0:T(8,128)(2,1)S(1)}, u32[]{:S(2)}, u32[]{:S(2)}) collective-permute-start(bf16[16,1664]{1,0:T(8,128)(2,1)S(1)} %broadcast_add_fusion), channel_id=1, source_target_pairs={{0,64},{32,96},{64,0},{96,32},{128,192},{160,224},{192,128},{224,1... | collective-permute-start | bytes 159752 | tf_op jit(solution)/shard_map/ppermute | solution.py:130
  41.6 5.9 %collective-permute-start.4 = (bf16[16,1664]{1,0:T(8,128)(2,1)S(1)}, bf16[16,1664]{1,0:T(8,128)(2,1)S(1)}, u32[]{:S(2)}, u32[]{:S(2)}) collective-permute-start(bf16[16,1664]{1,0:T(8,128)(2,1)S(1)} %broadcast_add_fusion), channel_id=1, source_target_pairs={{0,32},{32,0},{64,96},{96,64},{128,160},{160,128},{192,224},{224,1... | collective-permute-start | bytes 159752 | tf_op jit(solution)/shard_map/ppermute | solution.py:130
  44.7 4.1 %collective-permute-start.7 = (bf16[128,1664]{1,0:T(8,128)(2,1)S(1)}, bf16[128,1664]{1,0:T(8,128)(2,1)S(1)}, u32[]{:S(2)}, u32[]{:S(2)}) collective-permute-start(bf16[128,1664]{1,0:T(8,128)(2,1)S(1)} %bitcast.11), channel_id=1, source_target_pairs={{0,1},{1,0},{2,3},{3,2},{4,5},{5,4},{6,7},{7,6},{8,9},{9,8},{10,11... | collective-permute-start | bytes 1277960 | tf_op jit(solution)/shard_map/ppermute | solution.py:218
